TPU v7x, 32 devices: a whole 2x2x4 slice. The times are simulated.
32 devices in a mesh: groups: 2 (over y), wide: 4 (over z), narrow: 4 (over x, core).
Axes of the slice: x: 2, y: 2, z: 4, core: 2. Of those that a mesh axis runs over, the one named last changes fastest.
Arguments:
- layer_input_hidden: bfloat16 [8192, 5120], P(('groups', 'wide'), 'narrow'), parts along dimension 0, may hold values from -6 to 6
- token_adapter_index: int32 [8192, 1], P(('groups', 'wide')), parts along dimension 0, may hold values from 0 to 15; in each aligned block of 1024 rows (0 to 1023, 1024 to 2047, ...) at most 128 rows name the same one
- frozen_value_weight: bfloat16 [5120, 1024], P('narrow'), may hold values from -0.078125 to 0.078125
- adapter_down_weight: bfloat16 [32, 5120, 64], P(('groups', 'wide'), 'narrow'), parts along dimension 0, may hold values from -0.078125 to 0.078125
- adapter_up_weight: bfloat16 [32, 64, 1024], P(('groups', 'wide'), None, 'narrow'), parts along dimension 0, may hold values from -0.1875 to 0.1875
- output_cotangent_rows: bfloat16 [8192, 1024], P(('groups', 'wide'), 'narrow'), parts along dimension 0, may hold values from -6 to 6
Outputs:
- projected: bfloat16 [8192, 1024], P(('groups', 'wide'), 'narrow'), parts along dimension 0
- input_grad: bfloat16 [8192, 5120], P(('groups', 'wide'), 'narrow'), parts along dimension 0
- grad_down: float32 [32, 5120, 64], P(('groups', 'wide'), 'narrow'), parts along dimension 0
- up_weight_gradient: float32 [32, 64, 1024], P(('groups', 'wide'), None, 'narrow'), parts along dimension 0
There are 2 independent parts, one for each index of `groups`. A program takes and returns all parts, laid end to end along the dimension named above; an argument that names none is the same for every part. Nothing has to cross between parts.
Inputs may be any that keep to these rules, and one draw needn't show every extreme that they name: `token_adapter_index`: within each packed row of 1024 tokens no adapter serves more than 128 tokens, and some adapter serves exactly 128 tokens of some row; every adapter serves some token.
All inputs are finite; a program needn't handle non-finite values.
Results may differ from a plain program's by a relative error of at most 0.0037.
Values may be sent and summed in bfloat16 or wider, within the bound.
No kernel may reach another device: no remote copies, remote signals or barrier semaphores. Data moves between devices by JAX's collectives and lax.ppermute only.
A program may use at most 128 MiB of HBM per device.

v0:
```python
import jax
import jax.numpy as jnp
from jax import lax
from jax.sharding import PartitionSpec as P

ADAPTER_SCALE = 2.0


def slot_layout(token_adapter_index, adapters, capacity):
    labels = token_adapter_index[:, 0]
    onehot = (labels[:, None] == jnp.arange(adapters, dtype=jnp.int32)[None, :]).astype(jnp.int32)
    earlier = jnp.cumsum(onehot, axis=0) - onehot
    rank_ids = jnp.sum(earlier * onehot, axis=1)
    return labels * capacity + rank_ids


def pack_rows(source, slot_ids, total_slot_count):
    blank_rows = jnp.zeros((total_slot_count, source.shape[1]), source.dtype)
    return blank_rows.at[slot_ids].set(source)


def rank_terms(features, cotangent_token_rows, down_part, up_part):
    rank_size = down_part.shape[2]
    down_term = jnp.einsum(
        "pecd,edr->pecr", features, down_part, preferred_element_type=jnp.float32
    )
    backward_input_term = ADAPTER_SCALE * jnp.einsum(
        "pecv,erv->pecr", cotangent_token_rows, up_part, preferred_element_type=jnp.float32
    )
    summed = lax.psum(jnp.concatenate((down_term, backward_input_term), axis=3), "narrow")
    rank_space_state = summed[..., :rank_size].astype(jnp.bfloat16)
    backward_rank_rows = summed[..., rank_size:].astype(jnp.bfloat16)
    adapter_output_delta = (
        ADAPTER_SCALE
        * jnp.einsum(
            "pecr,erv->pecv", rank_space_state, up_part, preferred_element_type=jnp.float32
        )
    ).astype(jnp.bfloat16)
    input_term = jnp.einsum(
        "pecr,edr->pecd", backward_rank_rows, down_part, preferred_element_type=jnp.float32
    ).astype(jnp.bfloat16)
    return (rank_space_state, backward_rank_rows, adapter_output_delta, input_term)


def owner_grads(features, cotangent_token_rows, rank_space_state, backward_rank_rows):
    grad_down = jnp.einsum(
        "pecd,pecr->edr", features, backward_rank_rows, preferred_element_type=jnp.float32
    )
    up_weight_gradient = ADAPTER_SCALE * jnp.einsum(
        "pecr,pecv->erv", rank_space_state, cotangent_token_rows, preferred_element_type=jnp.float32
    )
    return (grad_down, up_weight_gradient)


def body(
    layer_input_hidden,
    token_adapter_index,
    frozen_value_weight,
    adapter_down_weight,
    adapter_up_weight,
    output_cotangent_rows,
):
    tokens = layer_input_hidden.shape[0]
    width_part = layer_input_hidden.shape[1]
    value_part = output_cotangent_rows.shape[1]
    owners = lax.axis_size("wide")
    per_adapter_owner = adapter_down_weight.shape[0]
    adapters = per_adapter_owner * owners
    capacity = 2 * tokens // adapters
    total_slot_count = adapters * capacity
    slot_ids = slot_layout(token_adapter_index, adapters, capacity)
    features = pack_rows(layer_input_hidden, slot_ids, total_slot_count)
    cotangent_token_rows = pack_rows(output_cotangent_rows, slot_ids, total_slot_count)
    partial_out = jnp.dot(
        layer_input_hidden, frozen_value_weight, preferred_element_type=jnp.float32
    )
    base_out = lax.psum_scatter(partial_out, "narrow", scatter_dimension=1, tiled=True)
    base_back = lax.dot_general(
        lax.all_gather(output_cotangent_rows, "narrow", axis=1, tiled=True),
        frozen_value_weight,
        (((1,), (1,)), ((), ())),
        preferred_element_type=jnp.float32,
    )
    down_all, up_all = (
        lax.all_gather(adapter_down_weight, "wide", axis=0, tiled=True),
        lax.all_gather(adapter_up_weight, "wide", axis=0, tiled=True),
    )
    slot_feats = features.reshape(1, adapters, capacity, width_part)
    slot_cots = cotangent_token_rows.reshape(1, adapters, capacity, value_part)
    rank_space_state, backward_rank_rows, adapter_output_delta, input_term = rank_terms(
        slot_feats, slot_cots, down_all, up_all
    )
    grad_terms_down, grad_terms_up = owner_grads(
        slot_feats, slot_cots, rank_space_state, backward_rank_rows
    )
    grad_down, up_weight_gradient = (
        lax.psum_scatter(grad_terms_down, "wide", scatter_dimension=0, tiled=True),
        lax.psum_scatter(grad_terms_up, "wide", scatter_dimension=0, tiled=True),
    )
    adapter_output_delta = adapter_output_delta.reshape(total_slot_count, value_part)
    input_term = input_term.reshape(total_slot_count, width_part)
    projected = (base_out + adapter_output_delta[slot_ids].astype(jnp.float32)).astype(jnp.bfloat16)
    input_grad = (base_back + input_term[slot_ids].astype(jnp.float32)).astype(jnp.bfloat16)
    return (projected, input_grad, grad_down, up_weight_gradient)


def solution(mesh):
    in_specs = (
        P(("groups", "wide"), "narrow"),
        P(("groups", "wide"), None),
        P("narrow", None),
        P(("groups", "wide"), "narrow", None),
        P(("groups", "wide"), None, "narrow"),
        P(("groups", "wide"), "narrow"),
    )
    out_specs = (
        P(("groups", "wide"), "narrow"),
        P(("groups", "wide"), "narrow"),
        P(("groups", "wide"), "narrow", None),
        P(("groups", "wide"), None, "narrow"),
    )
    return jax.shard_map(body, mesh=mesh, in_specs=in_specs, out_specs=out_specs, check_vma=False)
```

profile of v0, /device:TPU:0, one launch (start us, length us, event | category | flops | bytes accessed | tf_op | source)
XLA Modules:
  0.0 286.9 jit_solution(2667679732436598914)
XLA Ops:
  7.2 0.0 copy-start
  7.2 0.0 all-gather.3.cloned.1.call-start
  7.2 0.7 all-gather.3.cloned.1.call-update
  7.9 0.0 all-gather.5.cloned.1.call-start
  8.0 0.7 all-gather.5.cloned.1.call-update
  8.7 0.0 reduce-scatter.4.cloned.1.call-start
  8.7 0.2 copy-done
  8.9 6.1 %fusion.10 = f32[1024,1024]{1,0:T(8,128)} fusion(bf16[1024,1280]{1,0:T(8,128)(2,1)} %param.6, bf16[1280,1024]{1,0:T(8,128)(2,1)S(1)} %copy-done), kind=kOutput, calls=%fused_computation.30 | convolution fusion | flops 2684354560 | bytes 9437184 | tf_op jit(solution)/shard_map/dot_general | solution.py:74
  15.1 0.0 copy-start.3
  15.1 0.0 reduce-scatter.4.cloned.1.call-update
  15.1 0.0 reduce-scatter.8.cloned.1.call-start
  15.1 0.6 copy-done.3
  15.8 4.5 %reduce-window.6 = s32[16,8,128]{2,1,0:T(8,128)S(1)} reduce-window(s32[16,8,128]{2,1,0:T(8,128)S(1)} %fusion.9, s32[]{:T(128)} %constant.7.clone.1), window={size=1x1x128 pad=0_0x0_0x127_0}, to_apply=%region_1.2 | reduce-window | flops 2080768 | bytes 131076 | tf_op jit(solution)/shard_map/reduce-window
  20.3 0.1 slice.22
  20.3 0.1 copy.14
  20.5 0.1 copy.15
  20.6 0.1 broadcast_add_fusion
  20.7 0.0 copy-start.2
  20.7 9.4 %scatter_custom_fusion = bf16[2048,1280]{1,0:T(8,128)(2,1)} fusion(s32[1024]{0:T(1024)S(1)} %bitcast.81, bf16[1024,1280]{1,0:T(8,128)(2,1)} %param.6, bf16[]{:T(256)} %constant.5.clone.1), kind=kCustom, calls=%fused_computation.6 | custom fusion | bytes 5243392 | tf_op jit(solution)/shard_map/scatter | solution.py:19
  30.1 6.4 %scatter_custom_fusion.1 = bf16[2048,256]{1,0:T(8,128)(2,1)} fusion(s32[1024]{0:T(1024)S(1)} %bitcast.82, bf16[1024,256]{1,0:T(8,128)(2,1)} %param.11, bf16[]{:T(256)} %constant.5.clone.1), kind=kCustom, calls=%fused_computation.15 | custom fusion | bytes 1049088 | tf_op jit(solution)/shard_map/scatter | solution.py:19
  36.5 0.0 copy-done.2
  36.5 24.3 %all_gather.10 = bf16[16,64,256]{2,1,0:T(8,128)(2,1)S(1)} all-gather(bf16[4,64,256]{2,1,0:T(8,128)(2,1)S(1)} %copy-done.2), channel_id=1, replica_groups=mesh['groups'=2,'wide'=4,'narrow'=4] {'wide'}, dimensions={0}, use_global_device_ids=true | all-gather | bytes 655360 | tf_op jit(solution)/shard_map/all_gather | solution.py:86
  60.8 0.0 copy-start.1
  60.8 0.8 copy-done.1
  61.6 1.7 fusion.2
  63.4 12.1 %all-gather.3.cloned.1.call-done = bf16[16,1280,64]{1,2,0:T(8,128)(2,1)} async-done(((bf16[4,1280,64]{1,2,0:T(8,128)(2,1)}), bf16[16,1280,64]{1,2,0:T(8,128)(2,1)}) %all-gather.3.cloned.1.call-update) | async-done | bytes 2621456 | tf_op jit(solution)/shard_map/all_gather | solution.py:85
  75.5 5.2 %convolution_bitcast_fusion = f32[1,16,128,64]{2,3,1,0:T(8,128)S(1)} fusion(bf16[16,128,1280]{2,1,0:T(8,128)(2,1)} %bitcast.71, bf16[16,1280,64]{1,2,0:T(8,128)(2,1)} %all-gather.3.cloned.1.call-done), kind=kOutput, calls=%fused_computation.12 | convolution fusion | flops 335544320 | bytes 8388608 | tf_op jit(solution)/shard_map/pecd,edr->pecr/dot_general | solution.py:24
  80.7 1.1 pad_maximum_fusion
  81.7 34.6 %all-reduce.1 = bf16[1,16,128,128]{2,3,1,0:T(8,128)(2,1)S(1)} all-reduce(f32[1,16,128,128]{2,3,1,0:T(8,128)} %pad_maximum_fusion), channel_id=1, replica_groups=mesh['groups'=2,'wide'=4,'narrow'=4] {'narrow'}, use_global_device_ids=true, to_apply=%region_6.7 | all-reduce | flops 262144 | bytes 1572864 | tf_op jit(solution)/shard_map/psum | solution.py:30
  116.3 2.5 convolution_multiply_fusion
  118.8 0.0 reduce-scatter.8.cloned.1.call-update
  118.8 0.2 reduce-scatter.6.cloned.1.call-start
  119.1 6.1 %fusion.5 = f32[16,1280,64]{1,2,0:T(8,128)} fusion(bf16[16,128,1280]{2,1,0:T(8,128)(2,1)} %bitcast.72, bf16[1,16,128,128]{2,3,1,0:T(8,128)(2,1)S(1)} %all-reduce.1), kind=kOutput, calls=%fused_computation.19 | convolution fusion | flops 335544320 | bytes 10747904 | tf_op jit(solution)/shard_map/pecd,pecr->edr/dot_general | solution.py:46
  125.2 0.0 reduce-scatter.6.cloned.1.call-update
  125.2 5.7 %convolution_convert_fusion = bf16[16,128,1280]{2,1,0:T(8,128)(2,1)} fusion(bf16[16,1280,64]{1,2,0:T(8,128)(2,1)} %all-gather.3.cloned.1.call-done, bf16[1,16,128,128]{2,3,1,0:T(8,128)(2,1)S(1)} %all-reduce.1), kind=kOutput, calls=%fused_computation.4 | convolution fusion | flops 338165760 | bytes 8126464 | tf_op jit(solution)/shard_map/pecr,edr->pecd/dot_general | solution.py:39
  130.9 9.7 %gather_fusion.1 = bf16[1024,1280]{1,0:T(8,128)(2,1)} fusion(bf16[2048,1280]{1,0:T(8,128)(2,1)} %bitcast.70, s32[1024]{0:T(1024)S(1)} %broadcast_clamp_fusion), kind=kCustom, calls=%fused_computation.1 | custom fusion | bytes 5246976 | tf_op jit(solution)/shard_map/gather | solution.py:103
  140.6 2.5 multiply_convert_fusion
  143.1 4.9 %gather_fusion = bf16[1024,256]{1,0:T(8,128)(2,1)S(1)} fusion(bf16[2048,256]{1,0:T(8,128)(2,1)} %bitcast.73, s32[1024]{0:T(1024)S(1)} %broadcast_clamp_fusion), kind=kCustom, calls=%fused_computation | custom fusion | bytes 1052672 | tf_op jit(solution)/shard_map/gather | solution.py:102
  148.0 0.0 all-gather.5.cloned.1.call-done
  148.0 6.9 %add_convert_fusion = bf16[1024,1280]{1,0:T(8,128)(2,1)} fusion(bf16[1024,1280]{1,0:T(8,128)(2,1)} %gather_fusion.1, bf16[1024,1024]{1,0:T(8,128)(2,1)} %all-gather.5.cloned.1.call-done, bf16[1280,1024]{1,0:T(8,128)(2,1)S(1)} %copy-done), kind=kOutput, calls=%fused_computation.5 | convolution fusion | flops 2688286720 | bytes 9961472 | tf_op jit(solution)/shard_map/dot_general | solution.py:78
  154.9 0.3 reduce-scatter.4.cloned.1.call-done
  155.2 2.1 add_convert_fusion.1
  157.3 27.9 %reduce-scatter.8.cloned.1.call-done = f32[4,64,256]{2,1,0:T(8,128)} async-done(((f32[16,64,256]{2,1,0:T(8,128)}), f32[4,64,256]{2,1,0:T(8,128)}) %reduce-scatter.8.cloned.1.call-update) | async-done | bytes 262160 | tf_op jit(solution)/shard_map/reduce_scatter | solution.py:98
  185.2 95.2 %reduce-scatter.6.cloned.1.call-done = f32[4,1280,64]{1,2,0:T(8,128)} async-done(((f32[16,1280,64]{1,2,0:T(8,128)}), f32[4,1280,64]{1,2,0:T(8,128)}) %reduce-scatter.6.cloned.1.call-update) | async-done | bytes 1310736 | tf_op jit(solution)/shard_map/reduce_scatter | solution.py:97
  (6 shorter events, 0.1 us)
Async XLA Ops:
  7.2 1.7 copy-start
  7.2 68.3 %all-gather.3.cloned.1.call-start = ((), (), s32[]{:S(2)}) async-start(), calls=%async_computation.4 | async-start | bytes 3276800 | tf_op jit(solution)/shard_map/all_gather | solution.py:85
  7.9 140.1 %all-gather.5.cloned.1.call-start = ((), (), s32[]{:S(2)}) async-start(), calls=%async_computation.5 | async-start | bytes 2621440 | tf_op jit(solution)/shard_map/all_gather | solution.py:79
  8.7 146.5 %reduce-scatter.4.cloned.1.call-start = ((), (), s32[]{:S(2)}) async-start(), calls=%async_computation.3 | async-start | bytes 5242880 | tf_op jit(solution)/shard_map/reduce_scatter | solution.py:77
  15.1 0.7 copy-start.3
  15.1 170.1 %reduce-scatter.8.cloned.1.call-start = ((), (), s32[]{:S(2)}) async-start(), calls=%async_computation.7 | async-start | bytes 1310720 | tf_op jit(solution)/shard_map/reduce_scatter | solution.py:98
  20.7 15.8 %copy-start.2 = (bf16[4,64,256]{2,1,0:T(8,128)(2,1)S(1)}, bf16[4,64,256]{2,1,0:T(8,128)(2,1)}, u32[]{:S(2)}) copy-start(bf16[4,64,256]{2,1,0:T(8,128)(2,1)} %param.10) | copy-start | bytes 393220
  60.8 0.8 copy-start.1
  118.8 161.5 %reduce-scatter.6.cloned.1.call-start = ((), (), s32[]{:S(2)}) async-start(), calls=%async_computation.6 | async-start | bytes 6553600 | tf_op jit(solution)/shard_map/reduce_scatter | solution.py:97
Sparse Core Ops, SparseCore 0:
  9.6 65.8 all-gather.2
  77.0 29.9 all-gather.4
  109.6 45.5 reduce-scatter.3
  158.0 27.1 reduce-scatter.7
  187.9 92.4 reduce-scatter.5
where the time goes:
time: 288 us; the launch traced here: 287 us
  waiting for transfers between devices  137 us (48%)
  blocking collectives  58.9 us (20%)
  matrix products  36.7 us (13%)
  local copies, waits for them, and re-layouts  32.3 us (11%)
  between operations  13.9 us (5%)
  other arithmetic  7.87 us (3%)
    reduce_scatter x1, waiting for transfers between devices, body(): lax.psum_scatter(grad_terms_down, 'wide', scatter_dimension=0, tiled=True)  95.2 us
    psum x1, blocking collectives, rank_terms(): lax.psum(jnp.concatenate((down_term, backward_input_term), axis=3), 'narr...  34.6 us
    reduce_scatter x1, waiting for transfers between devices, body(): lax.psum_scatter(grad_terms_up, 'wide', scatter_dimension=0, tiled=True)  27.9 us
    all_gather x1, blocking collectives, body(): lax.all_gather(adapter_up_weight, 'wide', axis=0, tiled=True)  24.3 us
    scatter x2, local copies, waits for them, and re-layouts, pack_rows(): return blank_rows.at[slot_ids].set(source)  15.8 us
    all_gather x1, waiting for transfers between devices, body(): lax.all_gather(adapter_down_weight, 'wide', axis=0, tiled=True)  12.1 us
    gather x1, local copies, waits for them, and re-layouts, body(): input_term[slot_ids].astype(jnp.float32)  9.74 us
    dot_general x1, matrix products, body(): lax.dot_general(lax.all_gather(output_cotangent_rows, 'narrow', axis=1, t...  6.86 us
  transfers between devices with their start and end apart: 5, of which 4 were waited for; matrix products, arithmetic and copies ran while one was open for 26% of the time, Pallas kernels for 0%

commit v1 on v0

v1 whole, which is shorter than its diff:
```python
import jax
import jax.numpy as jnp
from jax import lax
from jax.sharding import PartitionSpec as P

ADAPTER_SCALE = 2.0
F32 = jnp.float32
BF16 = jnp.bfloat16


def mask_of(labels, block, per_owner):
    names = block * per_owner + jnp.arange(per_owner, dtype=jnp.int32)
    return labels[None, :] == names[:, None]


def pick(products, labels, block, per_owner):
    rank, tokens = products.shape[0] // per_owner, products.shape[1]
    mask = mask_of(labels, block, per_owner)
    return jnp.sum(
        jnp.where(mask[:, None, :], products.reshape(per_owner, rank, tokens), 0.0), axis=0
    )


def spread(values, labels, block, per_owner):
    rank, tokens = values.shape
    mask = mask_of(labels, block, per_owner)
    wide = jnp.where(mask[:, None, :], values[None], jnp.zeros((), values.dtype))
    return wide.reshape(per_owner * rank, tokens)


def matmul(left, right):
    return jnp.dot(left, right, preferred_element_type=F32)


def matmul_nt(left, right):
    return lax.dot_general(left, right, (((1,), (1,)), ((), ())), preferred_element_type=F32)


def matmul_tn(left, right):
    return lax.dot_general(left, right, (((0,), (0,)), ((), ())), preferred_element_type=F32)


def gather_cyclic(block):
    owners = lax.axis_size("wide")
    return [block] + [
        lax.ppermute(block, "wide", [((k + m) % owners, k) for k in range(owners)])
        for m in range(1, owners)
    ]


def gather_line(block):
    owners, me = lax.axis_size("wide"), lax.axis_index("wide")
    from_left = from_right = block
    pieces = [(block, me)]
    for k in range(1, owners):
        from_left = lax.ppermute(
            from_left, "wide", [(d, d + 1) for d in range(k - 1, owners - 1)]
        )
        from_right = lax.ppermute(
            from_right, "wide", [(d, d - 1) for d in range(1, owners - k + 1)]
        )
        if 2 * k < owners:
            pieces += [(from_left, me - k), (from_right, me + k)]
        else:
            right_valid = me + k < owners
            pieces.append(
                (
                    jnp.where(right_valid, from_right, from_left),
                    jnp.where(right_valid, me + k, me - k),
                )
            )
    return pieces


def scatter_line(terms):
    owners = lax.axis_size("wide")
    to_right = to_left = 0.0
    for step in range(1, owners):
        to_right = lax.ppermute(
            (terms[owners - step] + to_right).astype(BF16),
            "wide",
            [(d, d + 1) for d in range(step) if d + 1 < owners],
        ).astype(F32)
        to_left = lax.ppermute(
            (terms[step] + to_left).astype(BF16),
            "wide",
            [(d, d - 1) for d in range(owners - step, owners) if d > 0],
        ).astype(F32)
    return terms[0] + to_right + to_left


def sum_narrow(values):
    size = lax.axis_size("narrow")
    step = 1
    while step < size:
        values = values + lax.ppermute(values, "narrow", [(d, d ^ step) for d in range(size)])
        step *= 2
    return values


def body(x, token_adapter_index, weight, down, up, cot):
    owners, me = lax.axis_size("wide"), lax.axis_index("wide")
    per_owner, width_part, rank = down.shape
    value_part = up.shape[2]
    rows = per_owner * rank
    labels = token_adapter_index[:, 0]
    down_own = jnp.swapaxes(down, 1, 2).reshape(rows, width_part)
    up_own = up.reshape(rows, value_part)
    blocks = [(me + m) % owners for m in range(owners)]

    up_all = gather_cyclic(up_own)
    down_all = gather_line(down_own)

    back = sum(
        pick(matmul_nt(u, cot), labels, b, per_owner) for u, b in zip(up_all, blocks)
    )
    back = (ADAPTER_SCALE * sum_narrow(back)).astype(BF16)
    down_terms = [matmul(spread(back, labels, b, per_owner), x) for b in blocks]
    grad_down = scatter_line(down_terms)

    partial_out = matmul(x, weight)
    base_out = lax.psum_scatter(partial_out, "narrow", scatter_dimension=1, tiled=True)
    cot_all = lax.all_gather(cot, "narrow", axis=1, tiled=True)
    base_back = matmul_nt(cot_all, weight)

    low = sum(pick(matmul_nt(d, x), labels, b, per_owner) for d, b in down_all)
    low = sum_narrow(low).astype(BF16)
    low_wide = [spread(low, labels, b, per_owner) for b in blocks]
    up_terms = [ADAPTER_SCALE * matmul(wide, cot) for wide in low_wide]
    grad_up = scatter_line(up_terms)

    update = ADAPTER_SCALE * matmul_tn(
        jnp.concatenate(low_wide, axis=0), jnp.concatenate(up_all, axis=0)
    )
    projected = (base_out + update.astype(BF16).astype(F32)).astype(BF16)
    input_term = matmul_tn(
        jnp.concatenate([spread(back, labels, b, per_owner) for _, b in down_all], axis=0),
        jnp.concatenate([d for d, _ in down_all], axis=0),
    )
    input_grad = (base_back + input_term.astype(BF16).astype(F32)).astype(BF16)

    return (
        projected,
        input_grad,
        jnp.swapaxes(grad_down.reshape(per_owner, rank, width_part), 1, 2),
        grad_up.reshape(per_owner, rank, value_part),
    )


def solution(mesh):
    in_specs = (
        P(("groups", "wide"), "narrow"),
        P(("groups", "wide"), None),
        P("narrow", None),
        P(("groups", "wide"), "narrow", None),
        P(("groups", "wide"), None, "narrow"),
        P(("groups", "wide"), "narrow"),
    )
    out_specs = (
        P(("groups", "wide"), "narrow"),
        P(("groups", "wide"), "narrow"),
        P(("groups", "wide"), "narrow", None),
        P(("groups", "wide"), None, "narrow"),
    )
    return jax.shard_map(body, mesh=mesh, in_specs=in_specs, out_specs=out_specs, check_vma=False)
```

time: 288 us -> 209 us (0.73)
  blocking collectives: 58.9 us -> 0 us
  starting transfers between devices: 0.38 us -> 51.1 us
  waiting for transfers between devices: 137 us -> 87.5 us
  local copies, waits for them, and re-layouts: 32.3 us -> 4.63 us
  other arithmetic: 7.87 us -> 12 us
    reduce_scatter x2 -> x0, waiting for transfers between devices: 123 us -> none  [the longest x1 95.2 us: body(): lax.psum_scatter(grad_terms_down, 'wide', scatter_dimension=0, tiled=True)]
    ppermute x0 -> x25, waiting for transfers between devices: none -> 87.4 us  [the longest x6 24.7 us: scatter_line(): lax.ppermute((terms[step] + to_left).astype(BF16), 'wide', [(d, d - 1) fo...]
    ppermute x0 -> x25, starting transfers between devices: none -> 51 us  [the longest x6 24.5 us: scatter_line(): lax.ppermute((terms[owners - step] + to_right).astype(BF16), 'wide', [(d,...]
    psum x1 -> x0, blocking collectives: 34.6 us -> none  [rank_terms(): lax.psum(jnp.concatenate((down_term, backward_input_term), axis=3), 'narr...]
    all_gather x1 -> x0, blocking collectives: 24.3 us -> none  [body(): lax.all_gather(adapter_up_weight, 'wide', axis=0, tiled=True)]
    scatter x2 -> x0, local copies, waits for them, and re-layouts: 15.8 us -> none  [pack_rows(): return blank_rows.at[slot_ids].set(source)]
    gather x2 -> x0, local copies, waits for them, and re-layouts: 14.6 us -> none  [the longest x1 9.74 us: body(): input_term[slot_ids].astype(jnp.float32)]
    all_gather x2 -> x1, waiting for transfers between devices: 12.1 us -> 0.02 us  [body(): cot_all = lax.all_gather(cot, 'narrow', axis=1, tiled=True)]
  transfers between devices with their start and end apart: 5 -> 27, of which waited for: 4 -> 8; matrix products, arithmetic and copies ran while one was open for 26% -> 24% of each run, Pallas kernels for 0% -> 0%
where the time goes in v1:
time: 209 us; the launch traced here: 208 us
  waiting for transfers between devices  87.5 us (42%)
  starting transfers between devices  51.1 us (24%)
  matrix products  38.2 us (18%)
  between operations  14.9 us (7%)
  other arithmetic  12 us (6%)
  local copies, waits for them, and re-layouts  4.63 us (2%)
    ppermute x6, waiting for transfers between devices, scatter_line(): lax.ppermute((terms[step] + to_left).astype(BF16), 'wide', [(d, d - 1) fo...  24.7 us
    ppermute x6, starting transfers between devices, scatter_line(): lax.ppermute((terms[owners - step] + to_right).astype(BF16), 'wide', [(d,...  24.5 us
    ppermute x6, waiting for transfers between devices, scatter_line(): lax.ppermute((terms[owners - step] + to_right).astype(BF16), 'wide', [(d,...  24.4 us
    ppermute x4, waiting for transfers between devices, sum_narrow(): lax.ppermute(values, 'narrow', [(d, d ^ step) for d in range(size)])  21.3 us
    ppermute x3, waiting for transfers between devices, gather_line(): lax.ppermute(from_right, 'wide', [(d, d - 1) for d in range(1, owners - k...  17 us
    dot_general x10, matrix products, matmul_nt(): lax.dot_general(left, right, (((1,), (1,)), ((), ())), preferred_element_...  16.7 us
    dot_general x9, matrix products, matmul(): return jnp.dot(left, right, preferred_element_type=F32)  12.7 us
    dot_general x2, matrix products, matmul_tn(): lax.dot_general(left, right, (((0,), (0,)), ((), ())), preferred_element_...  8.77 us
  transfers between devices with their start and end apart: 27, of which 8 were waited for; matrix products, arithmetic and copies ran while one was open for 24% of the time, Pallas kernels for 0%

profile of v1, /device:TPU:0, one launch (start us, length us, event | category | flops | bytes accessed | tf_op | source)
XLA Modules:
  0.0 208.3 jit_solution(10511949325144482885)
XLA Ops:
  7.2 4.1 %collective-permute-start.9 = (bf16[256,256]{1,0:T(8,128)(2,1)}, bf16[256,256]{1,0:T(8,128)(2,1)S(1)}, u32[]{:S(2)}, u32[]{:S(2)}) collective-permute-start(bf16[256,256]{1,0:T(8,128)(2,1)} %bitcast.106), channel_id=1, source_target_pairs={{8,0},{12,4},{0,8},{4,12},{9,1},{13,5},{1,9},{5,13},{10,2},{14,6},... | collective-permute-start | bytes 393224 | tf_op jit(solution)/shard_map/ppermute | solution.py:46
  11.3 1.6 collective-permute-start.10
  12.9 2.2 %collective-permute-start.8 = (bf16[256,256]{1,0:T(8,128)(2,1)}, bf16[256,256]{1,0:T(8,128)(2,1)S(1)}, u32[]{:S(2)}, u32[]{:S(2)}) collective-permute-start(bf16[256,256]{1,0:T(8,128)(2,1)} %bitcast.108), channel_id=1, source_target_pairs={{4,0},{8,4},{12,8},{0,12},{5,1},{9,5},{13,9},{1,13},{6,2},{10,6},{... | collective-permute-start | bytes 393224 | tf_op jit(solution)/shard_map/ppermute | solution.py:46
  15.2 1.3 collective-permute-start.1
  16.5 5.4 %collective-permute-start = (bf16[256,1280]{1,0:T(8,128)(2,1)}, bf16[256,1280]{1,0:T(8,128)(2,1)}, u32[]{:S(2)}, u32[]{:S(2)}) collective-permute-start(bf16[256,1280]{1,0:T(8,128)(2,1)} %bitcast.102), channel_id=1, source_target_pairs={{0,4},{4,8},{8,12},{1,5},{5,9},{9,13},{2,6},{6,10},{10,14},{3,7},{... | collective-permute-start | bytes 1966088 | tf_op jit(solution)/shard_map/ppermute | solution.py:56
  23.6 1.4 broadcast_compare_fusion.8
  25.0 1.5 fusion.28
  26.5 1.5 fusion.53
  29.3 1.0 copy-done.29
  30.3 4.4 %fusion.48 = f32[1024,1024]{1,0:T(8,128)} fusion(bf16[1024,1280]{1,0:T(8,128)(2,1)S(1)} %copy-done, bf16[1280,1024]{1,0:T(8,128)(2,1)S(1)} %copy-done.29), kind=kOutput, calls=%fused_computation.103 | convolution fusion | flops 2684354560 | bytes 9437184 | tf_op jit(solution)/shard_map/dot_general | solution.py:32
  34.8 1.0 add.258
  35.8 1.5 collective-permute-start.12
  37.4 2.0 fusion.29
  39.4 1.3 collective-permute-start.2
  40.7 6.2 %collective-permute-done.12 = f32[64,1024]{1,0:T(8,128)S(1)} collective-permute-done((f32[64,1024]{1,0:T(8,128)S(1)}, f32[64,1024]{1,0:T(8,128)S(1)}, u32[]{:S(2)}, u32[]{:S(2)}) %collective-permute-start.12) | collective-permute-done | bytes 262176 | tf_op jit(solution)/shard_map/ppermute | solution.py:96
  47.7 1.1 constant_dynamic-update-slice_fusion.6
  48.8 2.0 fusion.49
  50.8 2.0 fusion.50
  52.7 4.6 %collective-permute-done.2 = bf16[256,1280]{1,0:T(8,128)(2,1)S(1)} collective-permute-done((bf16[256,1280]{1,0:T(8,128)(2,1)}, bf16[256,1280]{1,0:T(8,128)(2,1)S(1)}, u32[]{:S(2)}, u32[]{:S(2)}) %collective-permute-start.2) | collective-permute-done | bytes 655392 | tf_op jit(solution)/shard_map/ppermute | solution.py:59
  57.4 1.3 collective-permute-start.4
  59.7 1.2 constant_dynamic-update-slice_fusion.5
  60.9 0.9 fusion.42
  61.8 12.4 %collective-permute-done.4 = bf16[256,1280]{1,0:T(8,128)(2,1)S(1)} collective-permute-done((bf16[256,1280]{1,0:T(8,128)(2,1)S(1)}, bf16[256,1280]{1,0:T(8,128)(2,1)S(1)}, u32[]{:S(2)}, u32[]{:S(2)}) %collective-permute-start.4) | collective-permute-done | bytes 655392 | tf_op jit(solution)/shard_map/ppermute | solution.py:59
  75.8 1.4 collective-permute-done.6
  78.0 13.7 %collective-permute-done.7 = f32[64,1024]{1,0:T(8,128)S(1)} collective-permute-done((f32[64,1024]{1,0:T(8,128)S(1)}, f32[64,1024]{1,0:T(8,128)S(1)}, u32[]{:S(2)}, u32[]{:S(2)}) %collective-permute-start.7) | collective-permute-done | bytes 262176 | tf_op jit(solution)/shard_map/ppermute | solution.py:96
  92.9 1.5 collective-permute-start.19
  94.3 1.9 fusion.46
  96.2 1.3 collective-permute-start.13
  97.9 1.9 fusion.55
  99.8 11.4 %collective-permute-done.13 = bf16[256,1280]{1,0:T(8,128)(2,1)S(1)} collective-permute-done((bf16[256,1280]{1,0:T(8,128)(2,1)S(1)}, bf16[256,1280]{1,0:T(8,128)(2,1)S(1)}, u32[]{:S(2)}, u32[]{:S(2)}) %collective-permute-start.13) | collective-permute-done | bytes 655392 | tf_op jit(solution)/shard_map/ppermute | solution.py:79
  112.0 4.6 %collective-permute-start.14 = (bf16[256,1280]{1,0:T(8,128)(2,1)S(1)}, bf16[256,1280]{1,0:T(8,128)(2,1)S(1)}, u32[]{:S(2)}, u32[]{:S(2)}) collective-permute-start(bf16[256,1280]{1,0:T(8,128)(2,1)S(1)} %get-tuple-element.41), channel_id=1, source_target_pairs={{0,4},{4,8},{1,5},{5,9},{2,6},{6,10},{3,7},{7,11},{16,20},{20,24},... | collective-permute-start | bytes 1966088 | tf_op jit(solution)/shard_map/ppermute | solution.py:79
  117.0 1.9 collective-permute-start.20
  119.0 13.0 %collective-permute-done.20 = bf16[256,256]{1,0:T(8,128)(2,1)S(1)} collective-permute-done((bf16[256,256]{1,0:T(8,128)(2,1)S(1)}, bf16[256,256]{1,0:T(8,128)(2,1)S(1)}, u32[]{:S(2)}, u32[]{:S(2)}) %collective-permute-start.20) | collective-permute-done | bytes 131104 | tf_op jit(solution)/shard_map/ppermute | solution.py:79
  132.0 1.0 add_convert_fusion.7
  133.6 1.7 add_convert_fusion.3
  136.8 5.0 %collective-permute-start.21 = (bf16[256,256]{1,0:T(8,128)(2,1)}, bf16[256,256]{1,0:T(8,128)(2,1)S(1)}, u32[]{:S(2)}, u32[]{:S(2)}) collective-permute-start(bf16[256,256]{1,0:T(8,128)(2,1)} %get-tuple-element.6), channel_id=1, source_target_pairs={{0,4},{4,8},{8,12},{1,5},{5,9},{9,13},{2,6},{6,10},{10,14},{3,7},{... | collective-permute-start | bytes 393224 | tf_op jit(solution)/shard_map/ppermute | solution.py:79
  142.5 1.3 collective-permute-start.24
  143.8 1.0 add_convert_fusion.2
  145.7 5.4 %fusion.51 = f32[1024,1280]{1,0:T(8,128)S(1)} fusion(bf16[1024,1024]{1,0:T(8,128)(2,1)} %all-gather.2.cloned.1.call-done, bf16[1280,1024]{1,0:T(8,128)(2,1)} %param.8), kind=kOutput, calls=%fused_computation.106 | convolution fusion | flops 2684354560 | bytes 9961472 | tf_op jit(solution)/shard_map/dot_general | solution.py:36
  151.1 10.3 %collective-permute-start.15 = (bf16[256,1280]{1,0:T(8,128)(2,1)S(1)}, bf16[256,1280]{1,0:T(8,128)(2,1)S(1)}, u32[]{:S(2)}, u32[]{:S(2)}) collective-permute-start(bf16[256,1280]{1,0:T(8,128)(2,1)S(1)} %copy-done.10), channel_id=1, source_target_pairs={{0,4},{4,8},{8,12},{1,5},{5,9},{9,13},{2,6},{6,10},{10,14},{3,7},{... | collective-permute-start | bytes 1966088 | tf_op jit(solution)/shard_map/ppermute | solution.py:79
  161.4 0.9 copy-done.11
  162.3 1.2 add_convert_fusion.1
  163.6 1.4 collective-permute-start.18
  165.0 5.2 %add_convert_fusion = bf16[1024,1280]{1,0:T(8,128)(2,1)} fusion(f32[1024,1280]{1,0:T(8,128)S(1)} %fusion.51, bf16[1280,1024]{1,0:T(8,128)(2,1)S(1)} %copy-done.19, bf16[1280,1280]{1,0:T(8,128)(2,1)S(1)} %copy-done.14), kind=kOutput, calls=%fused_computation | convolution fusion | flops 3360686080 | bytes 13762560 | tf_op jit(solution)/shard_map/dot_general | solution.py:40
  170.2 1.7 convert_add_fusion.1
  171.9 24.7 %collective-permute-done.18 = bf16[256,1280]{1,0:T(8,128)(2,1)S(1)} collective-permute-done((bf16[256,1280]{1,0:T(8,128)(2,1)S(1)}, bf16[256,1280]{1,0:T(8,128)(2,1)S(1)}, u32[]{:S(2)}, u32[]{:S(2)}) %collective-permute-start.18) | collective-permute-done | bytes 655392 | tf_op jit(solution)/shard_map/ppermute | solution.py:84
  196.6 1.3 convert_add_fusion
  197.9 3.6 %fusion.25 = bf16[1024,256]{1,0:T(8,128)(2,1)} fusion(f32[1024,256]{1,0:T(8,128)} %reduce-scatter.2.cloned.1.call-done, bf16[256,1024]{1,0:T(8,128)(2,1)} %bitcast.96, bf16[256,1024]{1,0:T(8,128)(2,1)S(1)} %bitcast.82, bf16[256,1024]{1,0:T(8,128)(2,1)} %bitcast.94, bf16[256,1024]{1,0:T(8,128)(2,1)} %bitcast.87, bf16[256,256]{1,0:T(8,128)(2,1)} %copy-done.16, ...), kind=kOutput, calls=%fused_computation.23 | convolution fusion | flops 548667392 | bytes 4194304 | tf_op jit(solution)/shard_map/dot_general | solution.py:40
  (126 shorter events, 13.4 us)
Async XLA Ops:
  7.2 22.1 %copy-start = (bf16[1024,1280]{1,0:T(8,128)(2,1)S(1)}, bf16[1024,1280]{1,0:T(8,128)(2,1)}, u32[]{:S(2)}) copy-start(bf16[1024,1280]{1,0:T(8,128)(2,1)} %param.6) | copy-start | bytes 7864324
  7.2 20.8 %copy-start.2 = (bf16[1024,256]{1,0:T(8,128)(2,1)S(1)}, bf16[1024,256]{1,0:T(8,128)(2,1)}, u32[]{:S(2)}) copy-start(bf16[1024,256]{1,0:T(8,128)(2,1)} %param.11) | copy-start | bytes 1572868
  7.2 138.5 %all-gather.2.cloned.1.call-start = ((), (), s32[]{:S(2)}) async-start(), calls=%async_computation.2 | async-start | bytes 2621440 | tf_op jit(solution)/shard_map/all_gather | solution.py:123
  7.2 19.2 %collective-permute-start.9 = (bf16[256,256]{1,0:T(8,128)(2,1)}, bf16[256,256]{1,0:T(8,128)(2,1)S(1)}, u32[]{:S(2)}, u32[]{:S(2)}) collective-permute-start(bf16[256,256]{1,0:T(8,128)(2,1)} %bitcast.106), channel_id=1, source_target_pairs={{8,0},{12,4},{0,8},{4,12},{9,1},{13,5},{1,9},{5,13},{10,2},{14,6},... | collective-permute-start | bytes 393224 | tf_op jit(solution)/shard_map/ppermute | solution.py:46
  11.3 17.1 %collective-permute-start.10 = (bf16[256,256]{1,0:T(8,128)(2,1)}, bf16[256,256]{1,0:T(8,128)(2,1)S(1)}, u32[]{:S(2)}, u32[]{:S(2)}) collective-permute-start(bf16[256,256]{1,0:T(8,128)(2,1)} %bitcast.107), channel_id=1, source_target_pairs={{12,0},{0,4},{4,8},{8,12},{13,1},{1,5},{5,9},{9,13},{14,2},{2,6},{... | collective-permute-start | bytes 393224 | tf_op jit(solution)/shard_map/ppermute | solution.py:46
  12.9 15.0 %collective-permute-start.8 = (bf16[256,256]{1,0:T(8,128)(2,1)}, bf16[256,256]{1,0:T(8,128)(2,1)S(1)}, u32[]{:S(2)}, u32[]{:S(2)}) collective-permute-start(bf16[256,256]{1,0:T(8,128)(2,1)} %bitcast.108), channel_id=1, source_target_pairs={{4,0},{8,4},{12,8},{0,12},{5,1},{9,5},{13,9},{1,13},{6,2},{10,6},{... | collective-permute-start | bytes 393224 | tf_op jit(solution)/shard_map/ppermute | solution.py:46
  15.2 24.3 %collective-permute-start.1 = (bf16[256,1280]{1,0:T(8,128)(2,1)}, bf16[256,1280]{1,0:T(8,128)(2,1)}, u32[]{:S(2)}, u32[]{:S(2)}) collective-permute-start(bf16[256,1280]{1,0:T(8,128)(2,1)} %bitcast.101), channel_id=1, source_target_pairs={{4,0},{8,4},{12,8},{5,1},{9,5},{13,9},{6,2},{10,6},{14,10},{7,3},{... | collective-permute-start | bytes 1966088 | tf_op jit(solution)/shard_map/ppermute | solution.py:59
  16.5 30.5 %collective-permute-start = (bf16[256,1280]{1,0:T(8,128)(2,1)}, bf16[256,1280]{1,0:T(8,128)(2,1)}, u32[]{:S(2)}, u32[]{:S(2)}) collective-permute-start(bf16[256,1280]{1,0:T(8,128)(2,1)} %bitcast.102), channel_id=1, source_target_pairs={{0,4},{4,8},{8,12},{1,5},{5,9},{9,13},{2,6},{6,10},{10,14},{3,7},{... | collective-permute-start | bytes 1966088 | tf_op jit(solution)/shard_map/ppermute | solution.py:56
  21.9 176.0 %reduce-scatter.2.cloned.1.call-start = ((), (), s32[]{:S(2)}) async-start(), calls=%async_computation.1 | async-start | bytes 5242880 | tf_op jit(solution)/shard_map/reduce_scatter | solution.py:122
  25.0 3.9 %copy-start.22 = (pred[4,1024]{1,0:T(4,128)(4,1)}, pred[4,1024]{1,0:T(4,128)(4,1)S(1)}, u32[]{:S(2)}) copy-start(pred[4,1024]{1,0:T(4,128)(4,1)S(1)} %get-tuple-element.37) | copy-start | bytes 12292
  25.0 3.9 %copy-start.24 = (pred[4,1024]{1,0:T(4,128)(4,1)}, pred[4,1024]{1,0:T(4,128)(4,1)S(1)}, u32[]{:S(2)}) copy-start(pred[4,1024]{1,0:T(4,128)(4,1)S(1)} %get-tuple-element.38) | copy-start | bytes 12292
  29.2 5.6 %collective-permute-start.11 = (f32[64,1024]{1,0:T(8,128)S(1)}, f32[64,1024]{1,0:T(8,128)}, u32[]{:S(2)}, u32[]{:S(2)}) collective-permute-start(f32[64,1024]{1,0:T(8,128)S(1)} %add_add_fusion), channel_id=1, source_target_pairs={{0,1},{1,0},{2,3},{3,2},{4,5},{5,4},{6,7},{7,6},{8,9},{9,8},{10,11... | collective-permute-start | bytes 786440 | tf_op jit(solution)/shard_map/ppermute | solution.py:96
  34.8 4.6 %copy-start.12 = (bf16[4,1280,64]{1,2,0:T(8,128)(2,1)S(1)}, bf16[4,1280,64]{1,2,0:T(8,128)(2,1)}, u32[]{:S(2)}) copy-start(bf16[4,1280,64]{1,2,0:T(8,128)(2,1)} %param.9) | copy-start | bytes 1966084
  35.8 11.1 %collective-permute-start.12 = (f32[64,1024]{1,0:T(8,128)S(1)}, f32[64,1024]{1,0:T(8,128)S(1)}, u32[]{:S(2)}, u32[]{:S(2)}) collective-permute-start(f32[64,1024]{1,0:T(8,128)S(1)} %add.258), channel_id=1, source_target_pairs={{0,2},{1,3},{2,0},{3,1},{4,6},{5,7},{6,4},{7,5},{8,10},{9,11},{10,... | collective-permute-start | bytes 786440 | tf_op jit(solution)/shard_map/ppermute | solution.py:96
  39.4 18.0 %collective-permute-start.2 = (bf16[256,1280]{1,0:T(8,128)(2,1)}, bf16[256,1280]{1,0:T(8,128)(2,1)S(1)}, u32[]{:S(2)}, u32[]{:S(2)}) collective-permute-start(bf16[256,1280]{1,0:T(8,128)(2,1)} %collective-permute-done.1), channel_id=1, source_target_pairs={{4,0},{8,4},{5,1},{9,5},{6,2},{10,6},{7,3},{11,7},{20,16},{24,20},... | collective-permute-start | bytes 1966088 | tf_op jit(solution)/shard_map/ppermute | solution.py:59
  47.0 11.7 %collective-permute-start.3 = (bf16[256,1280]{1,0:T(8,128)(2,1)}, bf16[256,1280]{1,0:T(8,128)(2,1)S(1)}, u32[]{:S(2)}, u32[]{:S(2)}) collective-permute-start(bf16[256,1280]{1,0:T(8,128)(2,1)} %collective-permute-done), channel_id=1, source_target_pairs={{4,8},{8,12},{5,9},{9,13},{6,10},{10,14},{7,11},{11,15},{20,24},{2... | collective-permute-start | bytes 1966088 | tf_op jit(solution)/shard_map/ppermute | solution.py:56
  57.4 16.8 %collective-permute-start.4 = (bf16[256,1280]{1,0:T(8,128)(2,1)S(1)}, bf16[256,1280]{1,0:T(8,128)(2,1)S(1)}, u32[]{:S(2)}, u32[]{:S(2)}) collective-permute-start(bf16[256,1280]{1,0:T(8,128)(2,1)S(1)} %collective-permute-done.2), channel_id=1, source_target_pairs={{4,0},{5,1},{6,2},{7,3},{20,16},{21,17},{22,18},{23,19}} | collective-permute-start | bytes 1966088 | tf_op jit(solution)/shard_map/ppermute | solution.py:59
  58.7 15.5 %collective-permute-start.5 = (bf16[256,1280]{1,0:T(8,128)(2,1)S(1)}, bf16[256,1280]{1,0:T(8,128)(2,1)S(1)}, u32[]{:S(2)}, u32[]{:S(2)}) collective-permute-start(bf16[256,1280]{1,0:T(8,128)(2,1)S(1)} %collective-permute-done.3), channel_id=1, source_target_pairs={{8,12},{9,13},{10,14},{11,15},{24,28},{25,29},{26,30},{27,31}} | collective-permute-start | bytes 1966088 | tf_op jit(solution)/shard_map/ppermute | solution.py:56
  75.5 16.3 %copy-start.21 = (pred[4,1024]{1,0:T(4,128)(4,1)S(1)}, pred[4,1024]{1,0:T(4,128)(4,1)}, u32[]{:S(2)}) copy-start(pred[4,1024]{1,0:T(4,128)(4,1)} %copy-done.20) | copy-start | bytes 12292
  75.5 16.3 %copy-start.23 = (pred[4,1024]{1,0:T(4,128)(4,1)S(1)}, pred[4,1024]{1,0:T(4,128)(4,1)}, u32[]{:S(2)}) copy-start(pred[4,1024]{1,0:T(4,128)(4,1)} %copy-done.22) | copy-start | bytes 12292
  75.5 16.3 %copy-start.25 = (pred[4,1024]{1,0:T(4,128)(4,1)S(1)}, pred[4,1024]{1,0:T(4,128)(4,1)}, u32[]{:S(2)}) copy-start(pred[4,1024]{1,0:T(4,128)(4,1)} %copy-done.24) | copy-start | bytes 12292
  75.5 16.3 %copy-start.27 = (pred[4,1024]{1,0:T(4,128)(4,1)S(1)}, pred[4,1024]{1,0:T(4,128)(4,1)}, u32[]{:S(2)}) copy-start(pred[4,1024]{1,0:T(4,128)(4,1)} %copy-done.26) | copy-start | bytes 12292
  75.6 1.6 collective-permute-start.6
  77.2 14.6 %collective-permute-start.7 = (f32[64,1024]{1,0:T(8,128)S(1)}, f32[64,1024]{1,0:T(8,128)S(1)}, u32[]{:S(2)}, u32[]{:S(2)}) collective-permute-start(f32[64,1024]{1,0:T(8,128)S(1)} %add.243), channel_id=1, source_target_pairs={{0,2},{1,3},{2,0},{3,1},{4,6},{5,7},{6,4},{7,5},{8,10},{9,11},{10,... | collective-permute-start | bytes 786440 | tf_op jit(solution)/shard_map/ppermute | solution.py:96
  78.0 13.7 %copy-start.13 = (bf16[1280,1280]{1,0:T(8,128)(2,1)}, bf16[1280,1280]{1,0:T(8,128)(2,1)S(1)}, u32[]{:S(2)}) copy-start(bf16[1280,1280]{1,0:T(8,128)(2,1)S(1)} %fusion.43) | copy-start | bytes 9830404
  92.5 3.7 %copy-start.9 = (bf16[4,64,1024]{2,1,0:T(8,128)(2,1)}, bf16[4,64,1024]{2,1,0:T(8,128)(2,1)S(1)}, u32[]{:S(2)}) copy-start(bf16[4,64,1024]{2,1,0:T(8,128)(2,1)S(1)} %get-tuple-element.20) | copy-start | bytes 1572868
  92.5 5.1 %copy-start.7 = (bf16[4,64,1024]{2,1,0:T(8,128)(2,1)}, bf16[4,64,1024]{2,1,0:T(8,128)(2,1)S(1)}, u32[]{:S(2)}) copy-start(bf16[4,64,1024]{2,1,0:T(8,128)(2,1)S(1)} %get-tuple-element.17) | copy-start | bytes 1572868
  92.5 24.1 %copy-start.5 = (bf16[4,64,1024]{2,1,0:T(8,128)(2,1)}, bf16[4,64,1024]{2,1,0:T(8,128)(2,1)S(1)}, u32[]{:S(2)}) copy-start(bf16[4,64,1024]{2,1,0:T(8,128)(2,1)S(1)} %get-tuple-element.19) | copy-start | bytes 1572868
  92.5 39.4 %copy-start.8 = (bf16[4,64,1024]{2,1,0:T(8,128)(2,1)}, bf16[4,64,1024]{2,1,0:T(8,128)(2,1)S(1)}, u32[]{:S(2)}) copy-start(bf16[4,64,1024]{2,1,0:T(8,128)(2,1)S(1)} %get-tuple-element.18) | copy-start | bytes 1572868
  92.9 23.8 %collective-permute-start.19 = (bf16[256,256]{1,0:T(8,128)(2,1)S(1)}, bf16[256,256]{1,0:T(8,128)(2,1)S(1)}, u32[]{:S(2)}, u32[]{:S(2)}) collective-permute-start(bf16[256,256]{1,0:T(8,128)(2,1)S(1)} %get-tuple-element.43), channel_id=1, source_target_pairs={{0,4},{1,5},{2,6},{3,7},{16,20},{17,21},{18,22},{19,23}} | collective-permute-start | bytes 393224 | tf_op jit(solution)/shard_map/ppermute | solution.py:79
  96.2 14.9 %collective-permute-start.13 = (bf16[256,1280]{1,0:T(8,128)(2,1)S(1)}, bf16[256,1280]{1,0:T(8,128)(2,1)S(1)}, u32[]{:S(2)}, u32[]{:S(2)}) collective-permute-start(bf16[256,1280]{1,0:T(8,128)(2,1)S(1)} %get-tuple-element.39), channel_id=1, source_target_pairs={{0,4},{1,5},{2,6},{3,7},{16,20},{17,21},{18,22},{19,23}} | collective-permute-start | bytes 1966088 | tf_op jit(solution)/shard_map/ppermute | solution.py:79
  112.0 21.6 %collective-permute-start.14 = (bf16[256,1280]{1,0:T(8,128)(2,1)S(1)}, bf16[256,1280]{1,0:T(8,128)(2,1)S(1)}, u32[]{:S(2)}, u32[]{:S(2)}) collective-permute-start(bf16[256,1280]{1,0:T(8,128)(2,1)S(1)} %get-tuple-element.41), channel_id=1, source_target_pairs={{0,4},{4,8},{1,5},{5,9},{2,6},{6,10},{3,7},{7,11},{16,20},{20,24},... | collective-permute-start | bytes 1966088 | tf_op jit(solution)/shard_map/ppermute | solution.py:79
  117.0 15.0 %collective-permute-start.20 = (bf16[256,256]{1,0:T(8,128)(2,1)S(1)}, bf16[256,256]{1,0:T(8,128)(2,1)S(1)}, u32[]{:S(2)}, u32[]{:S(2)}) collective-permute-start(bf16[256,256]{1,0:T(8,128)(2,1)S(1)} %get-tuple-element.45), channel_id=1, source_target_pairs={{0,4},{4,8},{1,5},{5,9},{2,6},{6,10},{3,7},{7,11},{16,20},{20,24},... | collective-permute-start | bytes 393224 | tf_op jit(solution)/shard_map/ppermute | solution.py:79
  132.9 3.1 %collective-permute-start.22 = (bf16[256,256]{1,0:T(8,128)(2,1)S(1)}, bf16[256,256]{1,0:T(8,128)(2,1)S(1)}, u32[]{:S(2)}, u32[]{:S(2)}) collective-permute-start(bf16[256,256]{1,0:T(8,128)(2,1)S(1)} %get-tuple-element.7), channel_id=1, source_target_pairs={{12,8},{13,9},{14,10},{15,11},{28,24},{29,25},{30,26},{31,27}} | collective-permute-start | bytes 393224 | tf_op jit(solution)/shard_map/ppermute | solution.py:84
  135.3 8.5 %collective-permute-start.16 = (bf16[256,1280]{1,0:T(8,128)(2,1)S(1)}, bf16[256,1280]{1,0:T(8,128)(2,1)S(1)}, u32[]{:S(2)}, u32[]{:S(2)}) collective-permute-start(bf16[256,1280]{1,0:T(8,128)(2,1)S(1)} %get-tuple-element.5), channel_id=1, source_target_pairs={{12,8},{13,9},{14,10},{15,11},{28,24},{29,25},{30,26},{31,27}} | collective-permute-start | bytes 1966088 | tf_op jit(solution)/shard_map/ppermute | solution.py:84
  136.0 5.8 %collective-permute-start.23 = (bf16[256,256]{1,0:T(8,128)(2,1)S(1)}, bf16[256,256]{1,0:T(8,128)(2,1)S(1)}, u32[]{:S(2)}, u32[]{:S(2)}) collective-permute-start(bf16[256,256]{1,0:T(8,128)(2,1)S(1)} %add_convert_fusion.6), channel_id=1, source_target_pairs={{8,4},{12,8},{9,5},{13,9},{10,6},{14,10},{11,7},{15,11},{24,20},{2... | collective-permute-start | bytes 393224 | tf_op jit(solution)/shard_map/ppermute | solution.py:84
  136.8 8.0 %copy-start.18 = (bf16[1280,1024]{1,0:T(8,128)(2,1)}, bf16[1280,1024]{1,0:T(8,128)(2,1)S(1)}, u32[]{:S(2)}) copy-start(bf16[1280,1024]{1,0:T(8,128)(2,1)S(1)} %constant_dynamic-update-slice_fusion) | copy-start | bytes 7864324
  136.8 33.4 %collective-permute-start.21 = (bf16[256,256]{1,0:T(8,128)(2,1)}, bf16[256,256]{1,0:T(8,128)(2,1)S(1)}, u32[]{:S(2)}, u32[]{:S(2)}) collective-permute-start(bf16[256,256]{1,0:T(8,128)(2,1)} %get-tuple-element.6), channel_id=1, source_target_pairs={{0,4},{4,8},{8,12},{1,5},{5,9},{9,13},{2,6},{6,10},{10,14},{3,7},{... | collective-permute-start | bytes 393224 | tf_op jit(solution)/shard_map/ppermute | solution.py:79
  142.5 27.7 %collective-permute-start.24 = (bf16[256,256]{1,0:T(8,128)(2,1)}, bf16[256,256]{1,0:T(8,128)(2,1)}, u32[]{:S(2)}, u32[]{:S(2)}) collective-permute-start(bf16[256,256]{1,0:T(8,128)(2,1)} %add_convert_fusion.5), channel_id=1, source_target_pairs={{4,0},{8,4},{12,8},{5,1},{9,5},{13,9},{6,2},{10,6},{14,10},{7,3},{... | collective-permute-start | bytes 393224 | tf_op jit(solution)/shard_map/ppermute | solution.py:84
  144.8 6.3 %copy-start.10 = (bf16[256,1280]{1,0:T(8,128)(2,1)S(1)}, bf16[256,1280]{1,0:T(8,128)(2,1)}, u32[]{:S(2)}) copy-start(bf16[256,1280]{1,0:T(8,128)(2,1)} %get-tuple-element.4) | copy-start | bytes 1966084
  144.8 17.5 %copy-start.3 = (f32[256,1280]{1,0:T(8,128)S(1)}, f32[256,1280]{1,0:T(8,128)}, u32[]{:S(2)}) copy-start(f32[256,1280]{1,0:T(8,128)} %get-tuple-element.40) | copy-start | bytes 3932164
  144.8 16.6 %collective-permute-start.17 = (bf16[256,1280]{1,0:T(8,128)(2,1)}, bf16[256,1280]{1,0:T(8,128)(2,1)S(1)}, u32[]{:S(2)}, u32[]{:S(2)}) collective-permute-start(bf16[256,1280]{1,0:T(8,128)(2,1)} %add_convert_fusion.2), channel_id=1, source_target_pairs={{8,4},{12,8},{9,5},{13,9},{10,6},{14,10},{11,7},{15,11},{24,20},{2... | collective-permute-start | bytes 1966088 | tf_op jit(solution)/shard_map/ppermute | solution.py:84
  145.7 19.3 %copy-start.14 = (bf16[1280,1280]{1,0:T(8,128)(2,1)S(1)}, bf16[1280,1280]{1,0:T(8,128)(2,1)}, u32[]{:S(2)}) copy-start(bf16[1280,1280]{1,0:T(8,128)(2,1)} %copy-done.13) | copy-start | bytes 9830404
  151.1 13.9 %copy-start.19 = (bf16[1280,1024]{1,0:T(8,128)(2,1)S(1)}, bf16[1280,1024]{1,0:T(8,128)(2,1)}, u32[]{:S(2)}) copy-start(bf16[1280,1024]{1,0:T(8,128)(2,1)} %copy-done.18) | copy-start | bytes 7864324
  151.1 20.8 %collective-permute-start.15 = (bf16[256,1280]{1,0:T(8,128)(2,1)S(1)}, bf16[256,1280]{1,0:T(8,128)(2,1)S(1)}, u32[]{:S(2)}, u32[]{:S(2)}) collective-permute-start(bf16[256,1280]{1,0:T(8,128)(2,1)S(1)} %copy-done.10), channel_id=1, source_target_pairs={{0,4},{4,8},{8,12},{1,5},{5,9},{9,13},{2,6},{6,10},{10,14},{3,7},{... | collective-permute-start | bytes 1966088 | tf_op jit(solution)/shard_map/ppermute | solution.py:79
  163.5 33.1 %copy-start.4 = (f32[256,1280]{1,0:T(8,128)S(1)}, f32[256,1280]{1,0:T(8,128)}, u32[]{:S(2)}) copy-start(f32[256,1280]{1,0:T(8,128)} %fusion.55) | copy-start | bytes 3932164
  163.6 33.1 %collective-permute-start.18 = (bf16[256,1280]{1,0:T(8,128)(2,1)S(1)}, bf16[256,1280]{1,0:T(8,128)(2,1)S(1)}, u32[]{:S(2)}, u32[]{:S(2)}) collective-permute-start(bf16[256,1280]{1,0:T(8,128)(2,1)S(1)} %add_convert_fusion.1), channel_id=1, source_target_pairs={{4,0},{8,4},{12,8},{5,1},{9,5},{13,9},{6,2},{10,6},{14,10},{7,3},{... | collective-permute-start | bytes 1966088 | tf_op jit(solution)/shard_map/ppermute | solution.py:84
  170.2 27.7 %copy-start.6 = (bf16[4,64,1024]{2,1,0:T(8,128)(2,1)S(1)}, bf16[4,64,1024]{2,1,0:T(8,128)(2,1)}, u32[]{:S(2)}) copy-start(bf16[4,64,1024]{2,1,0:T(8,128)(2,1)} %copy-done.5) | copy-start | bytes 1572868
  (9 other events, 20.1 us)
Sparse Core Ops, SparseCore 0:
  22.0 24.1 all-gather.1
  48.7 52.6 reduce-scatter.1

commit v2 on v1

v2 whole, which is shorter than its diff:
```python
import functools

import jax
import jax.numpy as jnp
from jax import lax
from jax.experimental import pallas as pl
from jax.experimental.pallas import tpu as pltpu
from jax.sharding import PartitionSpec as P

ADAPTER_SCALE = 2.0
F32 = jnp.float32
BF16 = jnp.bfloat16
VMEM_BYTES = 16 * 1024 * 1024
FILLER_FLOPS = 8 * 10**9
BACK_FLOPS = 4 * 10**9


def dot_nn(left, right):
    return jnp.dot(left, right, preferred_element_type=F32)


def dot_nt(left, right):
    return lax.dot_general(left, right, (((1,), (1,)), ((), ())), preferred_element_type=F32)


def dot_tn(left, right):
    return lax.dot_general(left, right, (((0,), (0,)), ((), ())), preferred_element_type=F32)


def tie(*values):
    return lax.optimization_barrier(values)


def local_kernel(name, kernel, outs, *operands, late=(), flops=0):
    late = [entry if isinstance(entry, tuple) else (entry,) for entry in late]
    sources = [array for entry in late for array in entry[:2]]
    slots = [jax.ShapeDtypeStruct(entry[0].shape, entry[0].dtype) for entry in late]

    def fetching(*refs):
        ins, refs = refs[: len(sources)], refs[len(sources) :]
        direct, refs = refs[: len(operands)], refs[len(operands) :]
        results, refs = refs[: len(outs)], refs[len(outs) :]
        fetched, semaphores = refs[: len(late)], refs[-1]
        ins, waits = iter(ins), []
        for i, entry in enumerate(late):
            copies = [
                pltpu.make_async_copy(next(ins), fetched[i], semaphores.at[i]) for _ in entry[:2]
            ]
            if len(copies) == 1:
                copies[0].start()
            else:
                first = entry[2]()
                pl.when(first)(copies[0].start)
                pl.when(jnp.logical_not(first))(copies[1].start)
            waits.append(copies[0])
        for copy in waits:
            copy.wait()
        kernel(*fetched, *direct, *results)

    scratch = [pltpu.VMEM(slot.shape, slot.dtype) for slot in slots]
    return pl.pallas_call(
        fetching if late else kernel,
        name=name,
        out_shape=[jax.ShapeDtypeStruct(s, t) for s, t in outs],
        in_specs=[pl.BlockSpec(memory_space=pl.ANY)] * len(sources)
        + [pl.BlockSpec(memory_space=pltpu.VMEM)] * len(operands),
        out_specs=[pl.BlockSpec(memory_space=pltpu.VMEM)] * len(outs),
        scratch_shapes=scratch + ([pltpu.SemaphoreType.DMA((len(late),))] if late else []),
        compiler_params=pltpu.CompilerParams(vmem_limit_bytes=VMEM_BYTES),
        cost_estimate=pl.CostEstimate(flops=flops, bytes_accessed=0, transcendentals=0),
    )(*sources, *operands)


def tile_of(extent):
    return 256 if extent % 256 == 0 else 128


def spread_tile(values, places, offset, per_owner):
    return jnp.concatenate(
        [
            jnp.where(places == offset * per_owner + a, values, jnp.zeros((), values.dtype))
            for a in range(per_owner)
        ],
        axis=0,
    )


def pick_kernel(offsets, per_owner, has_start, halved, *refs):
    count = len(offsets)
    pieces, (places, rhs), rest = refs[:count], refs[count : count + 2], refs[count + 2 :]
    start, outs = (rest[0], rest[1:]) if has_start else (None, rest)
    tokens = rhs.shape[0]
    tile = tile_of(tokens)
    rank = pieces[0].shape[0] // per_owner
    core = lax.axis_index("narrow") % 2
    for i in range(tokens // tile):
        at = pl.ds(i * tile, tile)
        here, right = places[:, at], rhs[at, :]
        total = jnp.zeros((rank, tile), F32) if start is None else start[:, at]
        for piece, offset in zip(pieces, offsets):
            products = dot_nt(piece[...], right)
            for a in range(per_owner):
                total += jnp.where(
                    here == offset() * per_owner + a, products[a * rank : (a + 1) * rank], 0.0
                )
        if halved:
            low, high = total[: rank // 2], total[rank // 2 :]
            outs[0][:, at] = jnp.where(core == 0, low, high)
            outs[1][:, at] = jnp.where(core == 0, high, low)
        else:
            outs[0][:, at] = total


def pick(name, pieces, places, rhs, per_owner, start=None, halved=False, flops=0):
    rows = (pieces[0][0][0] if isinstance(pieces[0][0], tuple) else pieces[0][0]).shape[0]
    rank, tokens = rows // per_owner, rhs.shape[0]
    kernel = functools.partial(
        pick_kernel, [o for _, o in pieces], per_owner, start is not None, halved
    )
    more = [] if start is None else [start]
    outs = [((rank // 2, tokens), F32)] * 2 if halved else [((rank, tokens), F32)]
    outs = local_kernel(
        name, kernel, outs, places, rhs, *more, late=[p for p, _ in pieces], flops=flops
    )
    return outs if halved else outs[0]


def whole(mine, other):
    first = lax.axis_index("narrow") % 2 == 0
    return jnp.concatenate(
        [jnp.where(first, mine[...], other[...]), jnp.where(first, other[...], mine[...])], axis=0
    )


def terms_kernel(offsets, per_owner, scale, other, mine, places, rhs, *outs):
    tile = tile_of(rhs.shape[1])
    values = whole(mine, other)
    for offset, out in zip(offsets, outs):
        wide = spread_tile(values, places[...], offset(), per_owner)

        def step(i, carry, wide=wide, out=out):
            at = pl.ds(pl.multiple_of(i * tile, tile), tile)
            out[:, at] = (scale * dot_nn(wide, rhs[:, at])).astype(out.dtype)
            return carry

        lax.fori_loop(0, rhs.shape[1] // tile, step, 0, unroll=True)


def outer_terms(name, values, places, rhs, offsets, types, per_owner, scale):
    mine, other = values
    shape = (2 * mine.shape[0] * per_owner, rhs.shape[1])
    kernel = functools.partial(terms_kernel, offsets, per_owner, scale)
    return local_kernel(
        name, kernel, [(shape, t) for t in types], mine, places, rhs, late=[other]
    )


def send_kernel(sides, owners, *refs):
    me = lax.axis_index("wide")
    got, terms, outs = refs[:2], refs[2:4], refs[4:]
    tile = 64
    for (step, even_to_right, moving, summing), came, term, out in zip(sides, got, terms, outs):
        to_right = (me % 2 == 0) == even_to_right
        passes_on = jnp.where(to_right, me >= step, me + step < owners)
        for i in range(out.shape[0] // tile):
            at = pl.ds(i * tile, tile)
            value = came[at, :]
            if summing:
                total = (term[at, :] + value.astype(F32)).astype(BF16)
                value = jnp.where(passes_on, value, total) if moving else total
            out[at, :] = value


def base_kernel(x, weight, *outs):
    part, width = lax.axis_index("narrow"), outs[0].shape[1]
    for s, out in enumerate(outs):
        columns = pl.ds(pl.multiple_of((part ^ s) * width, width), width)

        def step(i, carry, out=out, columns=columns):
            at = pl.ds(pl.multiple_of(i * 256, 256), 256)
            out[at, :] = dot_nn(x[at, :], weight[:, columns])
            return carry

        lax.fori_loop(0, x.shape[0] // 256, step, 0, unroll=True)


def input_grad_kernel(offsets, per_owner, parts, *refs):
    count = len(offsets)
    pieces, cots = refs[:count], refs[count : count + parts]
    weight, mine, other, places, out = refs[count + parts :]
    part, width = lax.axis_index("narrow"), cots[0].shape[1]
    tile = 256
    values = whole(mine, other)

    for i in range(out.shape[0] // tile):
        at = pl.ds(i * tile, tile)
        term = jnp.zeros((tile, out.shape[1]), F32)
        for piece, offset in zip(pieces, offsets):
            term += dot_tn(
                spread_tile(
                    values[:, i * tile : (i + 1) * tile], places[:, at], offset(), per_owner
                ),
                piece[...],
            )
        total = term.astype(BF16).astype(F32)
        for s, cot in enumerate(cots):
            columns = pl.ds(pl.multiple_of((part ^ s) * width, width), width)
            total += dot_nt(cot[at, :], weight[:, columns])
        out[at, :] = total.astype(out.dtype)


def projected_kernel(offsets, per_owner, *refs):
    ups = refs[: len(offsets)]
    base, mine, other, places, out = refs[len(offsets) :]
    values = whole(mine, other)
    tile = 256
    for i in range(out.shape[0] // tile):
        at = pl.ds(i * tile, tile)
        update = jnp.zeros((tile, out.shape[1]), F32)
        for offset, up in zip(offsets, ups):
            here = values[:, i * tile : (i + 1) * tile]
            update += dot_tn(spread_tile(here, places[:, at], offset(), per_owner), up[...])
        update = (ADAPTER_SCALE * update).astype(BF16).astype(F32)
        out[at, :] = (base[at, :] + update).astype(out.dtype)


def pair_lists(right_senders, left_senders):
    return [
        [(d, d + 1) for d in right_senders if d % 2 == odd]
        + [(d, d - 1) for d in left_senders if d % 2 != odd]
        for odd in (0, 1)
    ]


def shift(value, pairs):
    return lax.ppermute(value, "wide", pairs) if pairs else None


def swap_narrow(value, bit):
    size = lax.axis_size("narrow")
    return lax.ppermute(value, "narrow", [(d, d ^ bit) for d in range(size)])


def narrow_bits():
    size, bits = lax.axis_size("narrow"), []
    while 1 << len(bits) < size:
        bits.append(1 << len(bits))
    return bits


def sum_narrow(mine, other, scale, held=()):
    bits = narrow_bits()
    mine = mine + swap_narrow(other, bits[0])
    mine, *held = tie(mine, *held)
    for bit in bits[1:]:
        mine = mine + swap_narrow(mine, bit)
    mine = (scale * mine).astype(BF16)
    return (mine, swap_narrow(mine, bits[0])), held


def body(x, token_adapter_index, weight, down, up, cot):
    owners, me = lax.axis_size("wide"), lax.axis_index("wide")
    parts = lax.axis_size("narrow")
    per_owner, width_part, rank = down.shape
    value_part = up.shape[2]
    rows = per_owner * rank
    tokens = x.shape[0]
    adapters = owners * per_owner
    last = owners - 1
    down_own = jnp.swapaxes(down, 1, 2).reshape(rows, width_part)
    up_own = up.reshape(rows, value_part)
    places = token_adapter_index[:, 0][None, :] - me * per_owner
    places = jnp.where(places < 0, places + adapters, places)

    def fixed(offset):
        return lambda: offset

    def by_side(at_even, at_odd):
        return lambda: jnp.where(lax.axis_index("wide") % 2 == 0, at_even, at_odd)

    def arriving(step, even_from_right):
        def offset():
            me = lax.axis_index("wide")
            from_right = (me % 2 == 0) == even_from_right
            right = jnp.where(me + step < owners, step, -owners)
            left = jnp.where(me >= step, owners - step, -owners)
            return jnp.where(from_right, right, left)

        return offset

    def from_a(step):
        def valid():
            me = lax.axis_index("wide")
            return jnp.where(me % 2 == 0, me + step < owners, me >= step)

        return valid

    def gather_pairs(step):
        return pair_lists(range(step - 1, last), range(1, owners - step + 1))

    def reduce_pairs(step):
        return pair_lists(range(min(step, last)), range(max(owners - step, 1), owners))

    right, left = range(last), range(1, owners)
    pairs_a, pairs_b = pair_lists(right, left)

    def across(bits):
        def offset():
            me = lax.axis_index("wide")
            return (me ^ bits) - me + jnp.where((me ^ bits) < me, owners, 0)

        return offset

    up_all = [(up_own, fixed(0))] + [
        (shift(up_own, [(d ^ bits, d) for d in range(owners)]), across(bits))
        for bits in range(1, owners)
    ]
    got_b = shift(down_own, pairs_b)
    got_a = shift(down_own, pairs_a)
    near, x_late = tie(up_all[1][0], x)
    up_all[1] = (near, up_all[1][1])
    low = pick("pick_own", [(down_own, fixed(0))], places, x_late, per_owner)

    cot_here, low = tie(cot, low)
    back = pick("pick_back", up_all, places, cot_here, per_owner, halved=True, flops=BACK_FLOPS)
    back, (got_a, got_b) = sum_narrow(*back, ADAPTER_SCALE, (got_a, got_b))

    (term_first,) = outer_terms(
        "terms_first", back, places, x, [by_side(owners - 1, 1)], [F32], per_owner, 1.0
    )
    offsets = [fixed(0)] + [by_side(owners - s, s) for s in range(2, owners)]
    terms = outer_terms("terms_rest", back, places, x, offsets, [F32] * len(offsets), per_owner, 1.0)
    terms = [terms[0], term_first, *terms[1:]]

    base = local_kernel("base", base_kernel, [((tokens, value_part), F32)] * parts, x_late, weight)
    sums = dict(enumerate(base))
    cots = {0: cot}
    near_bit, *far_bits = narrow_bits()

    def sum_base(bit):
        for s in [s for s in sums if s & bit]:
            value = sums.pop(s)
            value = value if bit == near_bit else value.astype(BF16)
            sums[s ^ bit] = sums[s ^ bit] + swap_narrow(value, bit).astype(F32)

    def gather_cots(bit):
        for s in list(cots):
            cots[s | bit] = swap_narrow(cots[s], bit)

    pieces = {}
    for step in range(1, owners):
        gathers, reduces = gather_pairs(step + 1), reduce_pairs(step)
        sides = [
            (step, True, bool(gathers[0]), bool(reduces[0])),
            (step, False, bool(gathers[1]), bool(reduces[1])),
        ]
        if sides[0][3] and sides[1][3]:
            send_a, send_b = local_kernel(
                f"send_{step}",
                functools.partial(send_kernel, sides, owners),
                [(down_own.shape, BF16)] * 2,
                terms[step],
                terms[owners - step],
                late=[got_b, got_a],
            )
        else:
            send_a = got_b
            if sides[0][3]:
                (send_a,) = local_kernel(
                    f"send_{step}",
                    lambda came, term, out, sides=sides: send_kernel(
                        sides[:1], owners, came, came, term, term, out
                    ),
                    [(down_own.shape, BF16)],
                    terms[step],
                    late=[got_b],
                )
            send_b = got_a
        send_a, send_b, got_a, got_b = tie(send_a, send_b, got_a, got_b)
        if step == 1:
            sum_base(near_bit)
            for bit in far_bits:
                gather_cots(bit)
        elif step == 2:
            held = [(cots, s) for s in cots] + [(sums, s) for s in sums]
            send_a, send_b, low, *values = tie(send_a, send_b, low, *[d[s] for d, s in held])
            for (d, s), value in zip(held, values):
                d[s] = value
            for bit in far_bits:
                sum_base(bit)
            gather_cots(near_bit)
        elif step == last:
            held = [(cots, s) for s in cots] + [(sums, s) for s in sums]
            send_a, send_b, low, *values = tie(send_a, send_b, low, *[d[s] for d, s in held])
            for (d, s), value in zip(held, values):
                d[s] = value
        live_a, live_b = gather_pairs(step)
        if live_a:
            pieces["a", step] = got_a
        if live_b:
            pieces["b", step] = got_b
        if step < last:
            arrived = [
                (pieces[side, step], arriving(step, side == "a"))
                for side in "ab"
                if (side, step) in pieces
            ]
        if 2 * step == owners:
            arrived = [((got_a, got_b, from_a(step)), by_side(step, owners - step))]
        elif step == last:
            arrived = [(got_a, arriving(step, True))]
        got_b = shift(send_b, pairs_b)
        got_a = shift(send_a, pairs_a)
        low = pick(f"pick_{step}", arrived, places, x, per_owner, low, step == last)
    places_late, got_a, got_b = tie(places, got_a, got_b)
    grad_down = terms[0] + got_a.astype(F32) + got_b.astype(F32)

    low, _ = sum_narrow(*low, 1.0)
    grad_up, *up_terms = outer_terms(
        "up_terms",
        low,
        places,
        cot,
        [fixed(m) for m in range(owners)],
        [F32] + [BF16] * last,
        per_owner,
        ADAPTER_SCALE,
    )
    got_up = [
        shift(term, [(d, (d + m) % owners) for d in range(owners)])
        for m, term in enumerate(up_terms, 1)
    ]

    projected = local_kernel(
        "projected",
        functools.partial(projected_kernel, [o for _, o in up_all], per_owner),
        [((tokens, value_part), BF16)],
        sums[0],
        *low,
        places_late,
        late=[u for u, _ in up_all],
    )[0]
    slots = [(down_own, fixed(0))]
    for step in range(1, owners):
        a, b = pieces.get(("a", step)), pieces.get(("b", owners - step))
        slots.append(((a, b, from_a(step)) if b is not None else a, by_side(step, owners - step)))
    input_grad = local_kernel(
        "input_grad",
        functools.partial(input_grad_kernel, [o for _, o in slots], per_owner, parts),
        [((tokens, width_part), BF16)],
        *[cots[s] for s in range(parts)],
        weight,
        *back,
        places_late,
        late=[d for d, _ in slots],
        flops=FILLER_FLOPS,
    )[0]

    input_grad, projected, *got_up = tie(input_grad, projected, *got_up)
    for got in got_up:
        grad_up += got.astype(F32)
    return (
        projected,
        input_grad,
        jnp.swapaxes(grad_down.reshape(per_owner, rank, width_part), 1, 2),
        grad_up.reshape(per_owner, rank, value_part),
    )


def solution(mesh):
    in_specs = (
        P(("groups", "wide"), "narrow"),
        P(("groups", "wide"), None),
        P("narrow", None),
        P(("groups", "wide"), "narrow", None),
        P(("groups", "wide"), None, "narrow"),
        P(("groups", "wide"), "narrow"),
    )
    out_specs = (
        P(("groups", "wide"), "narrow"),
        P(("groups", "wide"), "narrow"),
        P(("groups", "wide"), "narrow", None),
        P(("groups", "wide"), None, "narrow"),
    )
    return jax.shard_map(body, mesh=mesh, in_specs=in_specs, out_specs=out_specs, check_vma=False)
```

time: 209 us -> 113 us (0.54)
  waiting for transfers between devices: 87.5 us -> 44.4 us
  matrix products: 38.2 us -> 0 us
  Pallas kernels: 0 us -> 25.9 us
  starting transfers between devices: 51.1 us -> 35 us
  between operations: 14.9 us -> 0.96 us
  other arithmetic: 12 us -> 3.19 us
    ppermute x25 -> x26, waiting for transfers between devices: 87.4 us -> 44.4 us  [the longest x14 26 us: shift(): return lax.ppermute(value, 'wide', pairs) if pairs else None]
    dot_general x21 -> x0, matrix products: 38.2 us -> none  [the longest x10 16.7 us: matmul_nt(): lax.dot_general(left, right, (((1,), (1,)), ((), ())), preferred_element_...]
    pallas_call x0 -> x14, Pallas kernels: none -> 25.9 us  [local_kernel(): pl.pallas_call(fetching if late else kernel, name=name, out_shape=[jax.Sh...]
    ppermute x25 -> x26, starting transfers between devices: 51 us -> 35 us  [the longest x14 29.2 us: shift(): return lax.ppermute(value, 'wide', pairs) if pairs else None]
    add x15 -> x7, other arithmetic: 5.76 us -> 2.46 us  [the longest x1 1.25 us: body(): grad_down = terms[0] + got_a.astype(F32) + got_b.astype(F32)]
    convert_element_type x6 -> x2, other arithmetic: 2.94 us -> 0.03 us  [sum_narrow(): mine = (scale * mine).astype(BF16)]
    unnamed x67 -> x14, local copies, waits for them, and re-layouts: 4.59 us -> 2.85 us
  transfers between devices with their start and end apart: 27 -> 26, of which waited for: 8 -> 11; matrix products, arithmetic and copies ran while one was open for 24% -> 1% of each run, Pallas kernels for 0% -> 23%
where the time goes in v2:
time: 113 us; the launch traced here: 112 us
  waiting for transfers between devices  44.4 us (39%)
  starting transfers between devices  35 us (31%)
  Pallas kernels  25.9 us (23%)
  other arithmetic  3.19 us (3%)
  local copies, waits for them, and re-layouts  2.85 us (3%)
    ppermute x14, starting transfers between devices, shift(): return lax.ppermute(value, 'wide', pairs) if pairs else None  29.2 us
    ppermute x14, waiting for transfers between devices, shift(): return lax.ppermute(value, 'wide', pairs) if pairs else None  26 us
    pallas_call x14, Pallas kernels, local_kernel(): pl.pallas_call(fetching if late else kernel, name=name, out_shape=[jax.Sh...  25.9 us
    ppermute x12, waiting for transfers between devices, swap_narrow(): return lax.ppermute(value, 'narrow', [(d, d ^ bit) for d in range(size)])  18.4 us
    ppermute x12, starting transfers between devices, swap_narrow(): return lax.ppermute(value, 'narrow', [(d, d ^ bit) for d in range(size)])  5.78 us
    unnamed x14, local copies, waits for them, and re-layouts  2.85 us
  transfers between devices with their start and end apart: 26, of which 11 were waited for; matrix products, arithmetic and copies ran while one was open for 1% of the time, Pallas kernels for 23%

profile of v2, /device:TPU:0, one launch (start us, length us, event | category | flops | bytes accessed | tf_op | source)
XLA Modules:
  0.0 112.3 jit_solution(13787648246547709745)
XLA Ops:
  0.6 3.1 %collective-permute-start = (bf16[256,256]{1,0:T(8,128)(2,1)}, bf16[256,256]{1,0:T(8,128)(2,1)S(1)}, u32[]{:S(2)}, u32[]{:S(2)}) collective-permute-start(bf16[256,256]{1,0:T(8,128)(2,1)} %bitcast.14), channel_id=1, source_target_pairs={{4,0},{0,4},{12,8},{8,12},{5,1},{1,5},{13,9},{9,13},{6,2},{2,6},{1... | collective-permute-start | bytes 393224 | tf_op jit(solution)/shard_map/ppermute | solution.py:236
  3.7 2.6 %collective-permute-start.1 = (bf16[256,256]{1,0:T(8,128)(2,1)}, bf16[256,256]{1,0:T(8,128)(2,1)S(1)}, u32[]{:S(2)}, u32[]{:S(2)}) collective-permute-start(bf16[256,256]{1,0:T(8,128)(2,1)} %bitcast.15), channel_id=1, source_target_pairs={{8,0},{12,4},{0,8},{4,12},{9,1},{13,5},{1,9},{5,13},{10,2},{14,6},... | collective-permute-start | bytes 393224 | tf_op jit(solution)/shard_map/ppermute | solution.py:236
  6.3 0.9 collective-permute-start.4
  7.2 0.7 collective-permute-start.5
  7.9 0.7 compare_select_fusion.refs_1_.refs_4_.refs_2_.refs_13_.refs_7_
  8.6 0.7 collective-permute-done.refs_1_
  9.3 1.7 %copy-done = bf16[1024,1280]{1,0:T(8,128)(2,1)S(1)} copy-done((bf16[1024,1280]{1,0:T(8,128)(2,1)S(1)}, bf16[1024,1280]{1,0:T(8,128)(2,1)}, u32[]{:S(2)}) %copy-start) | copy-done | bytes 2621464
  11.1 1.1 copy-done.3
  12.2 1.1 pick_own.1.refs_4_
  13.3 3.6 %collective-permute-done.1.refs_2_ = bf16[256,256]{1,0:T(8,128)(2,1)S(1)} collective-permute-done((bf16[256,256]{1,0:T(8,128)(2,1)}, bf16[256,256]{1,0:T(8,128)(2,1)S(1)}, u32[]{:S(2)}, u32[]{:S(2)}) %collective-permute-start.1) | collective-permute-done | bytes 131104 | tf_op jit(solution)/shard_map/ppermute | solution.py:236
  16.9 1.5 %pick_back.1 = (f32[32,1024]{1,0:T(8,128)S(1)}, f32[32,1024]{1,0:T(8,128)S(1)}) custom-call(bf16[256,256]{1,0:T(8,128)(2,1)S(1)} %bitcast.17, bf16[256,256]{1,0:T(8,128)(2,1)S(1)} %collective-permute-done.refs_1_, bf16[256,256]{1,0:T(8,128)(2,1)S(1)} %collective-permute-done.1.refs_2_, bf16[256,256]{1,0:T(8,128)(2,1)S(1)} %collective-permute-done.2.refs_3_, ...), custom_call_target="tpu_custom_call" | custom-call | flops 4000000000 | tf_op jit(solution)/shard_map/pick_back/pallas_call | solution.py:61
  18.5 1.3 %collective-permute-done.3 = f32[32,1024]{1,0:T(8,128)S(1)} collective-permute-done((f32[32,1024]{1,0:T(8,128)S(1)}, f32[32,1024]{1,0:T(8,128)S(1)}, u32[]{:S(2)}, u32[]{:S(2)}) %collective-permute-start.3) | collective-permute-done | bytes 131104 | tf_op jit(solution)/shard_map/ppermute | solution.py:241
  19.8 7.3 %collective-permute-done.4.refs_0_.refs_1_ = bf16[256,1280]{1,0:T(8,128)(2,1)S(1)} collective-permute-done((bf16[256,1280]{1,0:T(8,128)(2,1)}, bf16[256,1280]{1,0:T(8,128)(2,1)S(1)}, u32[]{:S(2)}, u32[]{:S(2)}) %collective-permute-start.4) | collective-permute-done | bytes 655392 | tf_op jit(solution)/shard_map/ppermute | solution.py:236
  27.1 1.7 %collective-permute-start.6 = (f32[32,1024]{1,0:T(8,128)S(1)}, f32[32,1024]{1,0:T(8,128)S(1)}, u32[]{:S(2)}, u32[]{:S(2)}) collective-permute-start(f32[32,1024]{1,0:T(8,128)S(1)} %add.52), channel_id=1, source_target_pairs={{0,2},{1,3},{2,0},{3,1},{4,6},{5,7},{6,4},{7,5},{8,10},{9,11},{10,... | collective-permute-start | bytes 393224 | tf_op jit(solution)/shard_map/ppermute | solution.py:241
  28.8 2.9 %base.1 = (f32[1024,256]{1,0:T(8,128)S(1)}, f32[1024,256]{1,0:T(8,128)S(1)}, f32[1024,256]{1,0:T(8,128)S(1)}, f32[1024,256]{1,0:T(8,128)S(1)}) custom-call(bf16[1024,1280]{1,0:T(8,128)(2,1)S(1)} %copy-done.1, bf16[1280,1024]{1,0:T(8,128)(2,1)S(1)} %copy-done.2), custom_call_target="tpu_custom_call" | custom-call | tf_op jit(solution)/shard_map/base/pallas_call | solution.py:61
  31.7 0.5 collective-permute-start.12
  32.4 3.6 %collective-permute-done.7.refs_0_.refs_12_ = bf16[32,1024]{1,0:T(8,128)(2,1)S(1)} collective-permute-done((bf16[32,1024]{1,0:T(8,128)(2,1)S(1)}, bf16[32,1024]{1,0:T(8,128)(2,1)S(1)}, u32[]{:S(2)}, u32[]{:S(2)}) %collective-permute-start.7) | collective-permute-done | bytes 65568 | tf_op jit(solution)/shard_map/ppermute | solution.py:241
  36.0 0.9 terms_first.1.refs_1_.refs_3_
  36.9 0.4 send_1.1
  37.3 0.7 collective-permute-start.8
  38.0 8.5 %collective-permute-start.9 = (bf16[256,1280]{1,0:T(8,128)(2,1)S(1)}, bf16[256,1280]{1,0:T(8,128)(2,1)S(1)}, u32[]{:S(2)}, u32[]{:S(2)}) collective-permute-start(bf16[256,1280]{1,0:T(8,128)(2,1)S(1)} %send_1.1), channel_id=1, source_target_pairs={{0,4},{8,12},{4,0},{12,8},{1,5},{9,13},{5,1},{13,9},{2,6},{10,14},... | collective-permute-start | bytes 1966088 | tf_op jit(solution)/shard_map/ppermute | solution.py:236
  46.5 0.5 collective-permute-start.10
  47.0 2.0 %pick_1.1.refs_4_ = f32[64,1024]{1,0:T(8,128)S(1)} custom-call(bf16[256,1280]{1,0:T(8,128)(2,1)S(1)} %collective-permute-done.4.refs_0_.refs_1_, bf16[256,1280]{1,0:T(8,128)(2,1)S(1)} %collective-permute-done.5.refs_0_.refs_1_.refs_5_, s32[1,1024]{1,0:T(1,128)S(1)} %compare_select_fusion.refs_1_.refs_4_.refs_2_.refs_13_.refs_7_, ...), custom_call_target="tpu_custom_call" | custom-call | tf_op jit(solution)/shard_map/pick_1/pallas_call | solution.py:61
  49.0 2.3 %terms_rest.1 = (f32[256,1280]{1,0:T(8,128)S(1)}, f32[256,1280]{1,0:T(8,128)S(1)}, f32[256,1280]{1,0:T(8,128)S(1)}) custom-call(bf16[32,1024]{1,0:T(8,128)(2,1)S(1)} %collective-permute-done.7.refs_0_.refs_12_, bf16[32,1024]{1,0:T(8,128)(2,1)S(1)} %multiply_convert_fusion.refs_1_.refs_11_, ...), custom_call_target="tpu_custom_call" | custom-call | tf_op jit(solution)/shard_map/terms_rest/pallas_call | solution.py:61
  51.6 9.6 %collective-permute-done.9.refs_1_.refs_0_.refs_2_ = bf16[256,1280]{1,0:T(8,128)(2,1)S(1)} collective-permute-done((bf16[256,1280]{1,0:T(8,128)(2,1)S(1)}, bf16[256,1280]{1,0:T(8,128)(2,1)S(1)}, u32[]{:S(2)}, u32[]{:S(2)}) %collective-permute-start.9) | collective-permute-done | bytes 655392 | tf_op jit(solution)/shard_map/ppermute | solution.py:236
  61.2 0.7 send_2.1
  61.9 0.6 collective-permute-start.17
  62.5 0.7 collective-permute-start.13
  63.2 3.4 %collective-permute-start.14 = (bf16[256,1280]{1,0:T(8,128)(2,1)S(1)}, bf16[256,1280]{1,0:T(8,128)(2,1)S(1)}, u32[]{:S(2)}, u32[]{:S(2)}) collective-permute-start(bf16[256,1280]{1,0:T(8,128)(2,1)S(1)} %get-tuple-element.89), channel_id=1, source_target_pairs={{0,4},{8,12},{4,0},{12,8},{1,5},{9,13},{5,1},{13,9},{2,6},{10,14},... | collective-permute-start | bytes 1966088 | tf_op jit(solution)/shard_map/ppermute | solution.py:236
  66.6 0.5 collective-permute-start.16
  67.1 1.1 pick_2.1.refs_3_
  68.2 6.8 %collective-permute-done.17 = bf16[1024,256]{1,0:T(8,128)(2,1)S(1)} collective-permute-done((bf16[1024,256]{1,0:T(8,128)(2,1)S(1)}, bf16[1024,256]{1,0:T(8,128)(2,1)S(1)}, u32[]{:S(2)}, u32[]{:S(2)}) %collective-permute-start.17) | collective-permute-done | bytes 524320 | tf_op jit(solution)/shard_map/ppermute | solution.py:241
  75.2 4.8 %collective-permute-done.14.refs_1_.refs_4_.refs_0_ = bf16[256,1280]{1,0:T(8,128)(2,1)S(1)} collective-permute-done((bf16[256,1280]{1,0:T(8,128)(2,1)S(1)}, bf16[256,1280]{1,0:T(8,128)(2,1)S(1)}, u32[]{:S(2)}, u32[]{:S(2)}) %collective-permute-start.14) | collective-permute-done | bytes 655392 | tf_op jit(solution)/shard_map/ppermute | solution.py:236
  80.0 0.7 send_3.1
  80.8 1.8 %collective-permute-start.18 = (bf16[256,1280]{1,0:T(8,128)(2,1)S(1)}, bf16[256,1280]{1,0:T(8,128)(2,1)S(1)}, u32[]{:S(2)}, u32[]{:S(2)}) collective-permute-start(bf16[256,1280]{1,0:T(8,128)(2,1)S(1)} %get-tuple-element.105), channel_id=1, source_target_pairs={{0,4},{8,12},{4,0},{12,8},{1,5},{9,13},{5,1},{13,9},{2,6},{10,14},... | collective-permute-start | bytes 1966088 | tf_op jit(solution)/shard_map/ppermute | solution.py:236
  82.6 0.7 collective-permute-start.19
  83.3 1.1 pick_3.1
  84.5 1.3 %collective-permute-done.20 = f32[32,1024]{1,0:T(8,128)S(1)} collective-permute-done((f32[32,1024]{1,0:T(8,128)S(1)}, f32[32,1024]{1,0:T(8,128)S(1)}, u32[]{:S(2)}, u32[]{:S(2)}) %collective-permute-start.20) | collective-permute-done | bytes 131104 | tf_op jit(solution)/shard_map/ppermute | solution.py:241
  85.8 1.6 %collective-permute-start.21 = (f32[32,1024]{1,0:T(8,128)S(1)}, f32[32,1024]{1,0:T(8,128)S(1)}, u32[]{:S(2)}, u32[]{:S(2)}) collective-permute-start(f32[32,1024]{1,0:T(8,128)S(1)} %add.57), channel_id=1, source_target_pairs={{0,2},{1,3},{2,0},{3,1},{4,6},{5,7},{6,4},{7,5},{8,10},{9,11},{10,... | collective-permute-start | bytes 393224 | tf_op jit(solution)/shard_map/ppermute | solution.py:241
  87.4 4.1 %collective-permute-done.21 = f32[32,1024]{1,0:T(8,128)S(1)} collective-permute-done((f32[32,1024]{1,0:T(8,128)S(1)}, f32[32,1024]{1,0:T(8,128)S(1)}, u32[]{:S(2)}, u32[]{:S(2)}) %collective-permute-start.21) | collective-permute-done | bytes 131104 | tf_op jit(solution)/shard_map/ppermute | solution.py:241
  91.5 1.2 %collective-permute-done.22.refs_6_.refs_0_ = bf16[32,1024]{1,0:T(8,128)(2,1)S(1)} collective-permute-done((bf16[32,1024]{1,0:T(8,128)(2,1)S(1)}, bf16[32,1024]{1,0:T(8,128)(2,1)S(1)}, u32[]{:S(2)}, u32[]{:S(2)}) %collective-permute-start.22) | collective-permute-done | bytes 65568 | tf_op jit(solution)/shard_map/ppermute | solution.py:241
  92.8 0.8 up_terms.1
  93.6 3.2 %collective-permute-start.23 = (bf16[256,256]{1,0:T(8,128)(2,1)S(1)}, bf16[256,256]{1,0:T(8,128)(2,1)S(1)}, u32[]{:S(2)}, u32[]{:S(2)}) collective-permute-start(bf16[256,256]{1,0:T(8,128)(2,1)S(1)} %get-tuple-element.112), channel_id=1, source_target_pairs={{0,4},{4,8},{8,12},{12,0},{1,5},{5,9},{9,13},{13,1},{2,6},{6,10},{... | collective-permute-start | bytes 393224 | tf_op jit(solution)/shard_map/ppermute | solution.py:236
  96.8 2.8 %collective-permute-start.25 = (bf16[256,256]{1,0:T(8,128)(2,1)S(1)}, bf16[256,256]{1,0:T(8,128)(2,1)S(1)}, u32[]{:S(2)}, u32[]{:S(2)}) collective-permute-start(bf16[256,256]{1,0:T(8,128)(2,1)S(1)} %get-tuple-element.114), channel_id=1, source_target_pairs={{0,12},{4,0},{8,4},{12,8},{1,13},{5,1},{9,5},{13,9},{2,14},{6,2},{... | collective-permute-start | bytes 393224 | tf_op jit(solution)/shard_map/ppermute | solution.py:236
  99.7 8.2 %input_grad.1 = bf16[1024,1280]{1,0:T(8,128)(2,1)} custom-call(bf16[256,1280]{1,0:T(8,128)(2,1)S(1)} %bitcast.13, bf16[256,1280]{1,0:T(8,128)(2,1)S(1)} %collective-permute-done.4.refs_0_.refs_1_, bf16[256,1280]{1,0:T(8,128)(2,1)S(1)} %collective-permute-done.9.refs_1_.refs_0_.refs_2_, bf16[256,1280]{1,0:T(8,128)(2,1)S(1)} %collective-permute-done.8.refs_0_.refs_1_.refs_3_, ...), custom_call_target="tpu_custom_call" | custom-call | flops 8000000000 | tf_op jit(solution)/shard_map/input_grad/pallas_call | solution.py:61
  107.9 2.3 %projected.1 = bf16[1024,256]{1,0:T(8,128)(2,1)} custom-call(bf16[256,256]{1,0:T(8,128)(2,1)S(1)} %bitcast.18, bf16[256,256]{1,0:T(8,128)(2,1)S(1)} %collective-permute-done.refs_1_, bf16[256,256]{1,0:T(8,128)(2,1)S(1)} %collective-permute-done.1.refs_2_, bf16[256,256]{1,0:T(8,128)(2,1)S(1)} %collective-permute-done.2.refs_3_, ...), custom_call_target="tpu_custom_call" | custom-call | tf_op jit(solution)/shard_map/projected/pallas_call | solution.py:61
  110.2 1.2 %convert_add_fusion = f32[256,1280]{1,0:T(8,128)} fusion(bf16[256,1280]{1,0:T(8,128)(2,1)S(1)} %collective-permute-done.19, f32[256,1280]{1,0:T(8,128)S(1)} %get-tuple-element.117, bf16[256,1280]{1,0:T(8,128)(2,1)S(1)} %collective-permute-done.18), kind=kLoop, calls=%fused_computation | loop fusion | flops 1310720 | bytes 3932160 | tf_op jit(solution)/shard_map/add | solution.py:416
  111.5 0.8 convert_add_fusion.2
  (42 shorter events, 1.0 us)
Async XLA Ops:
  0.6 8.7 %collective-permute-start = (bf16[256,256]{1,0:T(8,128)(2,1)}, bf16[256,256]{1,0:T(8,128)(2,1)S(1)}, u32[]{:S(2)}, u32[]{:S(2)}) collective-permute-start(bf16[256,256]{1,0:T(8,128)(2,1)} %bitcast.14), channel_id=1, source_target_pairs={{4,0},{0,4},{12,8},{8,12},{5,1},{1,5},{13,9},{9,13},{6,2},{2,6},{1... | collective-permute-start | bytes 393224 | tf_op jit(solution)/shard_map/ppermute | solution.py:236
  3.7 13.2 %collective-permute-start.1 = (bf16[256,256]{1,0:T(8,128)(2,1)}, bf16[256,256]{1,0:T(8,128)(2,1)S(1)}, u32[]{:S(2)}, u32[]{:S(2)}) collective-permute-start(bf16[256,256]{1,0:T(8,128)(2,1)} %bitcast.15), channel_id=1, source_target_pairs={{8,0},{12,4},{0,8},{4,12},{9,1},{13,5},{1,9},{5,13},{10,2},{14,6},... | collective-permute-start | bytes 393224 | tf_op jit(solution)/shard_map/ppermute | solution.py:236
  6.3 10.6 %collective-permute-start.2 = (bf16[256,256]{1,0:T(8,128)(2,1)}, bf16[256,256]{1,0:T(8,128)(2,1)S(1)}, u32[]{:S(2)}, u32[]{:S(2)}) collective-permute-start(bf16[256,256]{1,0:T(8,128)(2,1)} %bitcast.16), channel_id=1, source_target_pairs={{12,0},{8,4},{4,8},{0,12},{13,1},{9,5},{5,9},{1,13},{14,2},{10,6},... | collective-permute-start | bytes 393224 | tf_op jit(solution)/shard_map/ppermute | solution.py:236
  6.3 20.8 %collective-permute-start.4 = (bf16[256,1280]{1,0:T(8,128)(2,1)}, bf16[256,1280]{1,0:T(8,128)(2,1)S(1)}, u32[]{:S(2)}, u32[]{:S(2)}) collective-permute-start(bf16[256,1280]{1,0:T(8,128)(2,1)} %bitcast.10), channel_id=1, source_target_pairs={{0,4},{8,12},{4,0},{12,8},{1,5},{9,13},{5,1},{13,9},{2,6},{10,14},... | collective-permute-start | bytes 1966088 | tf_op jit(solution)/shard_map/ppermute | solution.py:236
  7.2 19.9 %collective-permute-start.5 = (bf16[256,1280]{1,0:T(8,128)(2,1)}, bf16[256,1280]{1,0:T(8,128)(2,1)S(1)}, u32[]{:S(2)}, u32[]{:S(2)}) collective-permute-start(bf16[256,1280]{1,0:T(8,128)(2,1)} %bitcast.11), channel_id=1, source_target_pairs={{4,8},{8,4},{5,9},{9,5},{6,10},{10,6},{7,11},{11,7},{20,24},{24,20... | collective-permute-start | bytes 1966088 | tf_op jit(solution)/shard_map/ppermute | solution.py:236
  9.3 1.7 %copy-start = (bf16[1024,1280]{1,0:T(8,128)(2,1)S(1)}, bf16[1024,1280]{1,0:T(8,128)(2,1)}, u32[]{:S(2)}) copy-start(bf16[1024,1280]{1,0:T(8,128)(2,1)} %refs_2_.2) | copy-start | bytes 7864324
  11.1 1.1 copy-start.3
  12.2 4.7 %copy-start.5 = (bf16[1024,256]{1,0:T(8,128)(2,1)S(1)}, bf16[1024,256]{1,0:T(8,128)(2,1)}, u32[]{:S(2)}) copy-start(bf16[1024,256]{1,0:T(8,128)(2,1)} %refs_3_.9) | copy-start | bytes 1572868
  12.2 4.7 %copy-start.6 = (bf16[4,64,256]{2,1,0:T(8,128)(2,1)S(1)}, bf16[4,64,256]{2,1,0:T(8,128)(2,1)}, u32[]{:S(2)}) copy-start(bf16[4,64,256]{2,1,0:T(8,128)(2,1)} %param.10) | copy-start | bytes 393220
  16.9 11.9 %copy-start.1 = (bf16[1024,1280]{1,0:T(8,128)(2,1)S(1)}, bf16[1024,1280]{1,0:T(8,128)(2,1)}, u32[]{:S(2)}) copy-start(bf16[1024,1280]{1,0:T(8,128)(2,1)} %refs_2_.2) | copy-start | bytes 7864324
  16.9 11.9 %copy-start.2 = (bf16[1280,1024]{1,0:T(8,128)(2,1)S(1)}, bf16[1280,1024]{1,0:T(8,128)(2,1)}, u32[]{:S(2)}) copy-start(bf16[1280,1024]{1,0:T(8,128)(2,1)} %refs_10_.1) | copy-start | bytes 7864324
  18.4 1.4 %collective-permute-start.3 = (f32[32,1024]{1,0:T(8,128)S(1)}, f32[32,1024]{1,0:T(8,128)S(1)}, u32[]{:S(2)}, u32[]{:S(2)}) collective-permute-start(f32[32,1024]{1,0:T(8,128)S(1)} %get-tuple-element.68), channel_id=1, source_target_pairs={{0,1},{1,0},{2,3},{3,2},{4,5},{5,4},{6,7},{7,6},{8,9},{9,8},{10,11... | collective-permute-start | bytes 393224 | tf_op jit(solution)/shard_map/ppermute | solution.py:241
  27.1 5.1 %collective-permute-start.6 = (f32[32,1024]{1,0:T(8,128)S(1)}, f32[32,1024]{1,0:T(8,128)S(1)}, u32[]{:S(2)}, u32[]{:S(2)}) collective-permute-start(f32[32,1024]{1,0:T(8,128)S(1)} %add.52), channel_id=1, source_target_pairs={{0,2},{1,3},{2,0},{3,1},{4,6},{5,7},{6,4},{7,5},{8,10},{9,11},{10,... | collective-permute-start | bytes 393224 | tf_op jit(solution)/shard_map/ppermute | solution.py:241
  31.7 19.6 %collective-permute-start.11 = (f32[1024,256]{1,0:T(8,128)S(1)}, f32[1024,256]{1,0:T(8,128)S(1)}, u32[]{:S(2)}, u32[]{:S(2)}) collective-permute-start(f32[1024,256]{1,0:T(8,128)S(1)} %get-tuple-element.85), channel_id=1, source_target_pairs={{0,1},{1,0},{2,3},{3,2},{4,5},{5,4},{6,7},{7,6},{8,9},{9,8},{10,11... | collective-permute-start | bytes 3145736 | tf_op jit(solution)/shard_map/ppermute | solution.py:241
  31.7 19.7 %collective-permute-start.12 = (f32[1024,256]{1,0:T(8,128)S(1)}, f32[1024,256]{1,0:T(8,128)S(1)}, u32[]{:S(2)}, u32[]{:S(2)}) collective-permute-start(f32[1024,256]{1,0:T(8,128)S(1)} %get-tuple-element.87), channel_id=1, source_target_pairs={{0,1},{1,0},{2,3},{3,2},{4,5},{5,4},{6,7},{7,6},{8,9},{9,8},{10,11... | collective-permute-start | bytes 3145736 | tf_op jit(solution)/shard_map/ppermute | solution.py:241
  32.3 3.7 %collective-permute-start.7 = (bf16[32,1024]{1,0:T(8,128)(2,1)S(1)}, bf16[32,1024]{1,0:T(8,128)(2,1)S(1)}, u32[]{:S(2)}, u32[]{:S(2)}) collective-permute-start(bf16[32,1024]{1,0:T(8,128)(2,1)S(1)} %multiply_convert_fusion.refs_1_.refs_11_), channel_id=1, source_target_pairs={{0,1},{1,0},{2,3},{3,2},{4,5},{5,4},{6,7},{7,6},{8,9},{9,8},{10,11... | collective-permute-start | bytes 196616 | tf_op jit(solution)/shard_map/ppermute | solution.py:241
  37.3 14.4 %collective-permute-start.8 = (bf16[256,1280]{1,0:T(8,128)(2,1)S(1)}, bf16[256,1280]{1,0:T(8,128)(2,1)S(1)}, u32[]{:S(2)}, u32[]{:S(2)}) collective-permute-start(bf16[256,1280]{1,0:T(8,128)(2,1)S(1)} %collective-permute-done.4.refs_0_.refs_1_), channel_id=1, source_target_pairs={{4,8},{8,4},{5,9},{9,5},{6,10},{10,6},{7,11},{11,7},{20,24},{24,20... | collective-permute-start | bytes 1966088 | tf_op jit(solution)/shard_map/ppermute | solution.py:236
  38.0 23.2 %collective-permute-start.9 = (bf16[256,1280]{1,0:T(8,128)(2,1)S(1)}, bf16[256,1280]{1,0:T(8,128)(2,1)S(1)}, u32[]{:S(2)}, u32[]{:S(2)}) collective-permute-start(bf16[256,1280]{1,0:T(8,128)(2,1)S(1)} %send_1.1), channel_id=1, source_target_pairs={{0,4},{8,12},{4,0},{12,8},{1,5},{9,13},{5,1},{13,9},{2,6},{10,14},... | collective-permute-start | bytes 1966088 | tf_op jit(solution)/shard_map/ppermute | solution.py:236
  46.5 15.4 %collective-permute-start.10 = (bf16[1024,256]{1,0:T(8,128)(2,1)S(1)}, bf16[1024,256]{1,0:T(8,128)(2,1)S(1)}, u32[]{:S(2)}, u32[]{:S(2)}) collective-permute-start(bf16[1024,256]{1,0:T(8,128)(2,1)S(1)} %copy-done.5), channel_id=1, source_target_pairs={{0,2},{1,3},{2,0},{3,1},{4,6},{5,7},{6,4},{7,5},{8,10},{9,11},{10,... | collective-permute-start | bytes 1572872 | tf_op jit(solution)/shard_map/ppermute | solution.py:241
  61.9 13.2 %collective-permute-start.17 = (bf16[1024,256]{1,0:T(8,128)(2,1)S(1)}, bf16[1024,256]{1,0:T(8,128)(2,1)S(1)}, u32[]{:S(2)}, u32[]{:S(2)}) collective-permute-start(bf16[1024,256]{1,0:T(8,128)(2,1)S(1)} %add.55), channel_id=1, source_target_pairs={{0,2},{1,3},{2,0},{3,1},{4,6},{5,7},{6,4},{7,5},{8,10},{9,11},{10,... | collective-permute-start | bytes 1572872 | tf_op jit(solution)/shard_map/ppermute | solution.py:241
  62.5 12.7 %collective-permute-start.13 = (bf16[256,1280]{1,0:T(8,128)(2,1)S(1)}, bf16[256,1280]{1,0:T(8,128)(2,1)S(1)}, u32[]{:S(2)}, u32[]{:S(2)}) collective-permute-start(bf16[256,1280]{1,0:T(8,128)(2,1)S(1)} %get-tuple-element.88), channel_id=1, source_target_pairs={{4,8},{8,4},{5,9},{9,5},{6,10},{10,6},{7,11},{11,7},{20,24},{24,20... | collective-permute-start | bytes 1966088 | tf_op jit(solution)/shard_map/ppermute | solution.py:236
  63.2 16.8 %collective-permute-start.14 = (bf16[256,1280]{1,0:T(8,128)(2,1)S(1)}, bf16[256,1280]{1,0:T(8,128)(2,1)S(1)}, u32[]{:S(2)}, u32[]{:S(2)}) collective-permute-start(bf16[256,1280]{1,0:T(8,128)(2,1)S(1)} %get-tuple-element.89), channel_id=1, source_target_pairs={{0,4},{8,12},{4,0},{12,8},{1,5},{9,13},{5,1},{13,9},{2,6},{10,14},... | collective-permute-start | bytes 1966088 | tf_op jit(solution)/shard_map/ppermute | solution.py:236
  66.6 14.1 %collective-permute-start.15 = (bf16[1024,256]{1,0:T(8,128)(2,1)S(1)}, bf16[1024,256]{1,0:T(8,128)(2,1)S(1)}, u32[]{:S(2)}, u32[]{:S(2)}) collective-permute-start(bf16[1024,256]{1,0:T(8,128)(2,1)S(1)} %copy-done.5), channel_id=1, source_target_pairs={{0,1},{1,0},{2,3},{3,2},{4,5},{5,4},{6,7},{7,6},{8,9},{9,8},{10,11... | collective-permute-start | bytes 1572872 | tf_op jit(solution)/shard_map/ppermute | solution.py:241
  66.6 14.1 %collective-permute-start.16 = (bf16[1024,256]{1,0:T(8,128)(2,1)S(1)}, bf16[1024,256]{1,0:T(8,128)(2,1)S(1)}, u32[]{:S(2)}, u32[]{:S(2)}) collective-permute-start(bf16[1024,256]{1,0:T(8,128)(2,1)S(1)} %collective-permute-done.10.refs_8_), channel_id=1, source_target_pairs={{0,1},{1,0},{2,3},{3,2},{4,5},{5,4},{6,7},{7,6},{8,9},{9,8},{10,11... | collective-permute-start | bytes 1572872 | tf_op jit(solution)/shard_map/ppermute | solution.py:241
  80.8 18.9 %collective-permute-start.18 = (bf16[256,1280]{1,0:T(8,128)(2,1)S(1)}, bf16[256,1280]{1,0:T(8,128)(2,1)S(1)}, u32[]{:S(2)}, u32[]{:S(2)}) collective-permute-start(bf16[256,1280]{1,0:T(8,128)(2,1)S(1)} %get-tuple-element.105), channel_id=1, source_target_pairs={{0,4},{8,12},{4,0},{12,8},{1,5},{9,13},{5,1},{13,9},{2,6},{10,14},... | collective-permute-start | bytes 1966088 | tf_op jit(solution)/shard_map/ppermute | solution.py:236
  82.6 17.1 %collective-permute-start.19 = (bf16[256,1280]{1,0:T(8,128)(2,1)S(1)}, bf16[256,1280]{1,0:T(8,128)(2,1)S(1)}, u32[]{:S(2)}, u32[]{:S(2)}) collective-permute-start(bf16[256,1280]{1,0:T(8,128)(2,1)S(1)} %get-tuple-element.106), channel_id=1, source_target_pairs={{4,8},{8,4},{5,9},{9,5},{6,10},{10,6},{7,11},{11,7},{20,24},{24,20... | collective-permute-start | bytes 1966088 | tf_op jit(solution)/shard_map/ppermute | solution.py:236
  84.4 15.3 %copy-start.4 = (bf16[4,1280,64]{1,2,0:T(8,128)(2,1)S(1)}, bf16[4,1280,64]{1,2,0:T(8,128)(2,1)}, u32[]{:S(2)}) copy-start(bf16[4,1280,64]{1,2,0:T(8,128)(2,1)} %param.9) | copy-start | bytes 1966084
  84.4 1.4 %collective-permute-start.20 = (f32[32,1024]{1,0:T(8,128)S(1)}, f32[32,1024]{1,0:T(8,128)S(1)}, u32[]{:S(2)}, u32[]{:S(2)}) collective-permute-start(f32[32,1024]{1,0:T(8,128)S(1)} %get-tuple-element.111), channel_id=1, source_target_pairs={{0,1},{1,0},{2,3},{3,2},{4,5},{5,4},{6,7},{7,6},{8,9},{9,8},{10,11... | collective-permute-start | bytes 393224 | tf_op jit(solution)/shard_map/ppermute | solution.py:241
  85.8 5.6 %collective-permute-start.21 = (f32[32,1024]{1,0:T(8,128)S(1)}, f32[32,1024]{1,0:T(8,128)S(1)}, u32[]{:S(2)}, u32[]{:S(2)}) collective-permute-start(f32[32,1024]{1,0:T(8,128)S(1)} %add.57), channel_id=1, source_target_pairs={{0,2},{1,3},{2,0},{3,1},{4,6},{5,7},{6,4},{7,5},{8,10},{9,11},{10,... | collective-permute-start | bytes 393224 | tf_op jit(solution)/shard_map/ppermute | solution.py:241
  91.5 1.3 %collective-permute-start.22 = (bf16[32,1024]{1,0:T(8,128)(2,1)S(1)}, bf16[32,1024]{1,0:T(8,128)(2,1)S(1)}, u32[]{:S(2)}, u32[]{:S(2)}) collective-permute-start(bf16[32,1024]{1,0:T(8,128)(2,1)S(1)} %add_convert_fusion.refs_5_.refs_1_), channel_id=1, source_target_pairs={{0,1},{1,0},{2,3},{3,2},{4,5},{5,4},{6,7},{7,6},{8,9},{9,8},{10,11... | collective-permute-start | bytes 196616 | tf_op jit(solution)/shard_map/ppermute | solution.py:241
  93.6 16.7 %collective-permute-start.23 = (bf16[256,256]{1,0:T(8,128)(2,1)S(1)}, bf16[256,256]{1,0:T(8,128)(2,1)S(1)}, u32[]{:S(2)}, u32[]{:S(2)}) collective-permute-start(bf16[256,256]{1,0:T(8,128)(2,1)S(1)} %get-tuple-element.112), channel_id=1, source_target_pairs={{0,4},{4,8},{8,12},{12,0},{1,5},{5,9},{9,13},{13,1},{2,6},{6,10},{... | collective-permute-start | bytes 393224 | tf_op jit(solution)/shard_map/ppermute | solution.py:236
  96.8 13.4 %collective-permute-start.24 = (bf16[256,256]{1,0:T(8,128)(2,1)S(1)}, bf16[256,256]{1,0:T(8,128)(2,1)S(1)}, u32[]{:S(2)}, u32[]{:S(2)}) collective-permute-start(bf16[256,256]{1,0:T(8,128)(2,1)S(1)} %get-tuple-element.113), channel_id=1, source_target_pairs={{0,8},{4,12},{8,0},{12,4},{1,9},{5,13},{9,1},{13,5},{2,10},{6,14},... | collective-permute-start | bytes 393224 | tf_op jit(solution)/shard_map/ppermute | solution.py:236
  96.8 13.4 %collective-permute-start.25 = (bf16[256,256]{1,0:T(8,128)(2,1)S(1)}, bf16[256,256]{1,0:T(8,128)(2,1)S(1)}, u32[]{:S(2)}, u32[]{:S(2)}) collective-permute-start(bf16[256,256]{1,0:T(8,128)(2,1)S(1)} %get-tuple-element.114), channel_id=1, source_target_pairs={{0,12},{4,0},{8,4},{12,8},{1,13},{5,1},{9,5},{13,9},{2,14},{6,2},{... | collective-permute-start | bytes 393224 | tf_op jit(solution)/shard_map/ppermute | solution.py:236

commit v3 on v2

--- a/solution.py
+++ b/solution.py
@@ -13,6 +13,7 @@
 VMEM_BYTES = 16 * 1024 * 1024
 FILLER_FLOPS = 8 * 10**9
 BACK_FLOPS = 4 * 10**9
+PICK_FLOPS = 4 * 10**9
 
 
 def dot_nn(left, right):
@@ -31,7 +32,7 @@
     return lax.optimization_barrier(values)
 
 
-def local_kernel(name, kernel, outs, *operands, late=(), flops=0):
+def local_kernel(name, kernel, outs, *operands, late=(), flops=0, stacked=False, scratch=()):
     late = [entry if isinstance(entry, tuple) else (entry,) for entry in late]
     sources = [array for entry in late for array in entry[:2]]
     slots = [jax.ShapeDtypeStruct(entry[0].shape, entry[0].dtype) for entry in late]
@@ -40,7 +41,12 @@
         ins, refs = refs[: len(sources)], refs[len(sources) :]
         direct, refs = refs[: len(operands)], refs[len(operands) :]
         results, refs = refs[: len(outs)], refs[len(outs) :]
-        fetched, semaphores = refs[: len(late)], refs[-1]
+        extra, refs = refs[: len(scratch)], refs[len(scratch) :]
+        semaphores = refs[-1]
+        fetched = refs[:-1]
+        if stacked:
+            rows = slots[0].shape[0]
+            fetched = [fetched[0].at[pl.ds(i * rows, rows)] for i in range(len(late))]
         ins, waits = iter(ins), []
         for i, entry in enumerate(late):
             copies = [
@@ -55,9 +61,12 @@
             waits.append(copies[0])
         for copy in waits:
             copy.wait()
-        kernel(*fetched, *direct, *results)
-
-    scratch = [pltpu.VMEM(slot.shape, slot.dtype) for slot in slots]
+        kernel(*(refs[:1] if stacked else fetched), *direct, *results, *extra)
+
+    buffers = [pltpu.VMEM(slot.shape, slot.dtype) for slot in slots]
+    if stacked:
+        rows, columns = slots[0].shape
+        buffers = [pltpu.VMEM((len(slots) * rows, columns), slots[0].dtype)]
     return pl.pallas_call(
         fetching if late else kernel,
         name=name,
@@ -65,7 +74,11 @@
         in_specs=[pl.BlockSpec(memory_space=pl.ANY)] * len(sources)
         + [pl.BlockSpec(memory_space=pltpu.VMEM)] * len(operands),
         out_specs=[pl.BlockSpec(memory_space=pltpu.VMEM)] * len(outs),
-        scratch_shapes=scratch + ([pltpu.SemaphoreType.DMA((len(late),))] if late else []),
+        scratch_shapes=[
+            *scratch,
+            *buffers,
+            *([pltpu.SemaphoreType.DMA((len(late),))] if late else []),
+        ],
         compiler_params=pltpu.CompilerParams(vmem_limit_bytes=VMEM_BYTES),
         cost_estimate=pl.CostEstimate(flops=flops, bytes_accessed=0, transcendentals=0),
     )(*sources, *operands)
@@ -184,29 +197,38 @@
         lax.fori_loop(0, x.shape[0] // 256, step, 0, unroll=True)
 
 
-def input_grad_kernel(offsets, per_owner, parts, *refs):
-    count = len(offsets)
-    pieces, cots = refs[:count], refs[count : count + parts]
-    weight, mine, other, places, out = refs[count + parts :]
+def input_most_kernel(offsets, per_owner, parts, pieces, *refs):
+    cots, (weight, mine, other, places, out, features) = refs[:parts], refs[parts:]
     part, width = lax.axis_index("narrow"), cots[0].shape[1]
     tile = 256
     values = whole(mine, other)
-
+    for s, cot in enumerate(cots):
+        columns = pl.ds(pl.multiple_of((part ^ s) * width, width), width)
+        features[:, columns] = cot[...]
     for i in range(out.shape[0] // tile):
         at = pl.ds(i * tile, tile)
-        term = jnp.zeros((tile, out.shape[1]), F32)
-        for piece, offset in zip(pieces, offsets):
-            term += dot_tn(
-                spread_tile(
-                    values[:, i * tile : (i + 1) * tile], places[:, at], offset(), per_owner
-                ),
-                piece[...],
-            )
-        total = term.astype(BF16).astype(F32)
-        for s, cot in enumerate(cots):
-            columns = pl.ds(pl.multiple_of((part ^ s) * width, width), width)
-            total += dot_nt(cot[at, :], weight[:, columns])
-        out[at, :] = total.astype(out.dtype)
+        here = values[:, i * tile : (i + 1) * tile]
+        wide = [spread_tile(here, places[:, at], offset(), per_owner) for offset in offsets]
+        term = dot_tn(jnp.concatenate(wide, axis=0), pieces[...])
+        out[at, :] = dot_nt(features[at, :], weight[...]) + term
+
+
+def input_last_kernel(offset, per_owner, piece, partial, mine, other, places, out):
+    tile = 256
+    values = whole(mine, other)
+    for i in range(out.shape[0] // tile):
+        at = pl.ds(i * tile, tile)
+        wide = spread_tile(
+            values[:, i * tile : (i + 1) * tile], places[:, at], offset(), per_owner
+        )
+        out[at, :] = (partial[at, :] + dot_tn(wide, piece[...])).astype(out.dtype)
+
+
+def grad_down_kernel(from_a, from_b, term, out):
+    tile = 64
+    for i in range(out.shape[0] // tile):
+        at = pl.ds(i * tile, tile)
+        out[at, :] = term[at, :] + from_a[at, :].astype(F32) + from_b[at, :].astype(F32)
 
 
 def projected_kernel(offsets, per_owner, *refs):
@@ -251,11 +273,11 @@
 def sum_narrow(mine, other, scale, held=()):
     bits = narrow_bits()
     mine = mine + swap_narrow(other, bits[0])
-    mine, *held = tie(mine, *held)
     for bit in bits[1:]:
         mine = mine + swap_narrow(mine, bit)
     mine = (scale * mine).astype(BF16)
-    return (mine, swap_narrow(mine, bits[0])), held
+    other, *held = tie(swap_narrow(mine, bits[0]), *held)
+    return (mine, other), held
 
 
 def body(x, token_adapter_index, weight, down, up, cot):
@@ -317,11 +339,11 @@
     ]
     got_b = shift(down_own, pairs_b)
     got_a = shift(down_own, pairs_a)
-    near, x_late = tie(up_all[1][0], x)
-    up_all[1] = (near, up_all[1][1])
-    low = pick("pick_own", [(down_own, fixed(0))], places, x_late, per_owner)
-
-    cot_here, low = tie(cot, low)
+    low = pick("pick_own", [(down_own, fixed(0))], places, x, per_owner, flops=2 * 10**9)
+
+    outs = [((tokens, value_part), F32)] * parts
+    base = local_kernel("base", base_kernel, outs, x, weight, flops=3 * 10**9)
+    cot_here, low, *base = tie(cot, low, *base)
     back = pick("pick_back", up_all, places, cot_here, per_owner, halved=True, flops=BACK_FLOPS)
     back, (got_a, got_b) = sum_narrow(*back, ADAPTER_SCALE, (got_a, got_b))
 
@@ -332,23 +354,29 @@
     terms = outer_terms("terms_rest", back, places, x, offsets, [F32] * len(offsets), per_owner, 1.0)
     terms = [terms[0], term_first, *terms[1:]]
 
-    base = local_kernel("base", base_kernel, [((tokens, value_part), F32)] * parts, x_late, weight)
     sums = dict(enumerate(base))
     cots = {0: cot}
     near_bit, *far_bits = narrow_bits()
 
-    def sum_base(bit):
-        for s in [s for s in sums if s & bit]:
-            value = sums.pop(s)
-            value = value if bit == near_bit else value.astype(BF16)
-            sums[s ^ bit] = sums[s ^ bit] + swap_narrow(value, bit).astype(F32)
-
-    def gather_cots(bit):
+    def send_base(bit):
+        values = {s: sums.pop(s) for s in list(sums) if s & bit}
+        return {
+            s ^ bit: swap_narrow(v if bit == near_bit else v.astype(BF16), bit)
+            for s, v in values.items()
+        }
+
+    def add_base(came):
+        for s, value in came.items():
+            sums[s] = sums[s] + value.astype(F32)
+
+    def gather_cots(cots, bit):
         for s in list(cots):
             cots[s | bit] = swap_narrow(cots[s], bit)
 
     pieces = {}
     for step in range(1, owners):
+        if step > 1:
+            got_a, got_b, low = tie(got_a, got_b, low)
         gathers, reduces = gather_pairs(step + 1), reduce_pairs(step)
         sides = [
             (step, True, bool(gathers[0]), bool(reduces[0])),
@@ -377,23 +405,11 @@
                 )
             send_b = got_a
         send_a, send_b, got_a, got_b = tie(send_a, send_b, got_a, got_b)
-        if step == 1:
-            sum_base(near_bit)
-            for bit in far_bits:
-                gather_cots(bit)
-        elif step == 2:
-            held = [(cots, s) for s in cots] + [(sums, s) for s in sums]
-            send_a, send_b, low, *values = tie(send_a, send_b, low, *[d[s] for d, s in held])
-            for (d, s), value in zip(held, values):
-                d[s] = value
-            for bit in far_bits:
-                sum_base(bit)
-            gather_cots(near_bit)
-        elif step == last:
-            held = [(cots, s) for s in cots] + [(sums, s) for s in sums]
-            send_a, send_b, low, *values = tie(send_a, send_b, low, *[d[s] for d, s in held])
-            for (d, s), value in zip(held, values):
-                d[s] = value
+        if step == 2:
+            send_a, send_b, *values = tie(send_a, send_b, *cots.values())
+            cots = dict(zip(cots, values))
+        if step == last:
+            send_a, send_b, back_partial = tie(send_a, send_b, back_partial)
         live_a, live_b = gather_pairs(step)
         if live_a:
             pieces["a", step] = got_a
@@ -411,9 +427,46 @@
             arrived = [(got_a, arriving(step, True))]
         got_b = shift(send_b, pairs_b)
         got_a = shift(send_a, pairs_a)
-        low = pick(f"pick_{step}", arrived, places, x, per_owner, low, step == last)
-    places_late, got_a, got_b = tie(places, got_a, got_b)
-    grad_down = terms[0] + got_a.astype(F32) + got_b.astype(F32)
+        low = pick(
+            f"pick_{step}", arrived, places, x, per_owner, low, step == last, flops=PICK_FLOPS
+        )
+        if step == last:
+            add_base(base_came)
+            *low, sums[0] = tie(*low, sums[0])
+        elif step <= 2:
+            after = term_first if step == 1 else low
+            after, *values = tie(after, *sums.values())
+            sums.update(zip(list(sums), values))
+            if step == 1:
+                base_came = send_base(near_bit)
+                for bit in far_bits:
+                    gather_cots(cots, bit)
+            else:
+                low = after
+                add_base(base_came)
+                for bit in far_bits[:-1]:
+                    add_base(send_base(bit))
+                base_came = send_base(far_bits[-1])
+                gather_cots(cots, near_bit)
+        if step == last - 1:
+            gathered = [(down_own, fixed(0))]
+            for k in range(1, last):
+                a, b = pieces.get(("a", k)), pieces.get(("b", owners - k))
+                piece = a if b is None else (a, b, from_a(k))
+                gathered.append((piece, by_side(k, owners - k)))
+            gathered.append((pieces["b", 1], by_side(last, 1)))
+            (back_partial,) = local_kernel(
+                "input_grad_most",
+                functools.partial(input_most_kernel, [o for _, o in gathered], per_owner, parts),
+                [((tokens, width_part), F32)],
+                *[cots[s] for s in range(parts)],
+                weight,
+                *back,
+                places,
+                late=[d for d, _ in gathered],
+                stacked=True,
+                scratch=[pltpu.VMEM((tokens, parts * value_part), BF16)],
+            )
 
     low, _ = sum_narrow(*low, 1.0)
     grad_up, *up_terms = outer_terms(
@@ -426,6 +479,7 @@
         per_owner,
         ADAPTER_SCALE,
     )
+    places_late, *up_terms = tie(places, *up_terms)
     got_up = [
         shift(term, [(d, (d + m) % owners) for d in range(owners)])
         for m, term in enumerate(up_terms, 1)
@@ -440,23 +494,26 @@
         places_late,
         late=[u for u, _ in up_all],
     )[0]
-    slots = [(down_own, fixed(0))]
-    for step in range(1, owners):
-        a, b = pieces.get(("a", step)), pieces.get(("b", owners - step))
-        slots.append(((a, b, from_a(step)) if b is not None else a, by_side(step, owners - step)))
-    input_grad = local_kernel(
+    (input_grad,) = local_kernel(
         "input_grad",
-        functools.partial(input_grad_kernel, [o for _, o in slots], per_owner, parts),
+        functools.partial(input_last_kernel, arriving(last, True), per_owner),
         [((tokens, width_part), BF16)],
-        *[cots[s] for s in range(parts)],
-        weight,
+        back_partial,
         *back,
         places_late,
-        late=[d for d, _ in slots],
+        late=[pieces["a", last]],
+    )
+    input_grad, projected, got_a, got_b = tie(input_grad, projected, got_a, got_b)
+    (grad_down,) = local_kernel(
+        "grad_down",
+        grad_down_kernel,
+        [((rows, width_part), F32)],
+        terms[0],
+        late=[got_a, got_b],
         flops=FILLER_FLOPS,
-    )[0]
-
-    input_grad, projected, *got_up = tie(input_grad, projected, *got_up)
+    )
+
+    grad_down, *got_up = tie(grad_down, *got_up)
     for got in got_up:
         grad_up += got.astype(F32)
     return (

time: 113 us -> 100 us (0.88)
  waiting for transfers between devices: 44.4 us -> 29.1 us
  Pallas kernels: 25.9 us -> 29 us
  other arithmetic: 3.19 us -> 1.85 us
    ppermute x14, waiting for transfers between devices: 26 us -> 15.7 us  [shift(): return lax.ppermute(value, 'wide', pairs) if pairs else None]
    ppermute x12, waiting for transfers between devices: 18.4 us -> 13.4 us  [swap_narrow(): return lax.ppermute(value, 'narrow', [(d, d ^ bit) for d in range(size)])]
    pallas_call x14 -> x16, Pallas kernels: 25.9 us -> 29 us  [local_kernel(): pl.pallas_call(fetching if late else kernel, name=name, out_shape=[jax.Sh...]
    add x4 -> x1, other arithmetic: 1.66 us -> 0.17 us  [add_base(): sums[s] = sums[s] + value.astype(F32)]
    ppermute x12, starting transfers between devices: 5.78 us -> 7.15 us  [swap_narrow(): return lax.ppermute(value, 'narrow', [(d, d ^ bit) for d in range(size)])]
  transfers between devices with their start and end apart: 26 -> 26, of which waited for: 11 -> 12; matrix products, arithmetic and copies ran while one was open for 1% -> 1% of each run, Pallas kernels for 23% -> 28%
where the time goes in v3:
time: 100 us; the launch traced here: 99.9 us
  starting transfers between devices  35.4 us (35%)
  waiting for transfers between devices  29.1 us (29%)
  Pallas kernels  29 us (29%)
  local copies, waits for them, and re-layouts  3.51 us (4%)
  other arithmetic  1.85 us (2%)
  between operations  1.01 us (1%)
    pallas_call x16, Pallas kernels, local_kernel(): pl.pallas_call(fetching if late else kernel, name=name, out_shape=[jax.Sh...  29 us
    ppermute x14, starting transfers between devices, shift(): return lax.ppermute(value, 'wide', pairs) if pairs else None  28.3 us
    ppermute x14, waiting for transfers between devices, shift(): return lax.ppermute(value, 'wide', pairs) if pairs else None  15.7 us
    ppermute x12, waiting for transfers between devices, swap_narrow(): return lax.ppermute(value, 'narrow', [(d, d ^ bit) for d in range(size)])  13.4 us
    ppermute x12, starting transfers between devices, swap_narrow(): return lax.ppermute(value, 'narrow', [(d, d ^ bit) for d in range(size)])  7.15 us
    unnamed x14, local copies, waits for them, and re-layouts  3.51 us
  transfers between devices with their start and end apart: 26, of which 12 were waited for; matrix products, arithmetic and copies ran while one was open for 1% of the time, Pallas kernels for 28%

profile of v3, /device:TPU:0, one launch (start us, length us, event | category | flops | bytes accessed | tf_op | source)
XLA Modules:
  0.0 99.9 jit_solution(9208914010466812297)
XLA Ops:
  0.6 3.1 %collective-permute-start = (bf16[256,256]{1,0:T(8,128)(2,1)}, bf16[256,256]{1,0:T(8,128)(2,1)S(1)}, u32[]{:S(2)}, u32[]{:S(2)}) collective-permute-start(bf16[256,256]{1,0:T(8,128)(2,1)} %bitcast.14), channel_id=1, source_target_pairs={{4,0},{0,4},{12,8},{8,12},{5,1},{1,5},{13,9},{9,13},{6,2},{2,6},{1... | collective-permute-start | bytes 393224 | tf_op jit(solution)/shard_map/ppermute | solution.py:258
  3.7 2.6 %collective-permute-start.1 = (bf16[256,256]{1,0:T(8,128)(2,1)}, bf16[256,256]{1,0:T(8,128)(2,1)S(1)}, u32[]{:S(2)}, u32[]{:S(2)}) collective-permute-start(bf16[256,256]{1,0:T(8,128)(2,1)} %bitcast.15), channel_id=1, source_target_pairs={{8,0},{12,4},{0,8},{4,12},{9,1},{13,5},{1,9},{5,13},{10,2},{14,6},... | collective-permute-start | bytes 393224 | tf_op jit(solution)/shard_map/ppermute | solution.py:258
  6.3 0.9 collective-permute-start.6
  7.2 0.7 collective-permute-start.7
  7.9 0.7 compare_select_fusion.refs_1_.refs_4_.refs_2_.refs_12_.refs_7_
  8.6 1.7 %copy-done = bf16[1024,1280]{1,0:T(8,128)(2,1)S(1)} copy-done((bf16[1024,1280]{1,0:T(8,128)(2,1)S(1)}, bf16[1024,1280]{1,0:T(8,128)(2,1)}, u32[]{:S(2)}) %copy-start) | copy-done | bytes 2621464
  10.4 1.7 %copy-done.2 = bf16[1280,1024]{1,0:T(8,128)(2,1)S(1)} copy-done((bf16[1280,1024]{1,0:T(8,128)(2,1)S(1)}, bf16[1280,1024]{1,0:T(8,128)(2,1)}, u32[]{:S(2)}) %copy-start.2) | copy-done | bytes 2621464
  12.1 2.9 %base.1 = (f32[1024,256]{1,0:T(8,128)S(1)}, f32[1024,256]{1,0:T(8,128)S(1)}, f32[1024,256]{1,0:T(8,128)S(1)}, f32[1024,256]{1,0:T(8,128)S(1)}) custom-call(bf16[1024,1280]{1,0:T(8,128)(2,1)S(1)} %copy-done, bf16[1280,1024]{1,0:T(8,128)(2,1)S(1)} %copy-done.2), custom_call_target="tpu_custom_call" | custom-call | flops 3000000000 | tf_op jit(solution)/shard_map/base/pallas_call | solution.py:70
  15.0 1.1 %pick_own.1.refs_4_ = f32[64,1024]{1,0:T(8,128)S(1)} custom-call(bf16[256,1280]{1,0:T(8,128)(2,1)S(1)} %bitcast.12, s32[1,1024]{1,0:T(1,128)S(1)} %compare_select_fusion.refs_1_.refs_4_.refs_2_.refs_12_.refs_7_, bf16[1024,1280]{1,0:T(8,128)(2,1)S(1)} %copy-done), custom_call_target="tpu_custom_call" | custom-call | flops 2000000000 | tf_op jit(solution)/shard_map/pick_own/pallas_call | solution.py:70
  16.1 0.7 collective-permute-done.1.refs_2_
  16.9 1.5 %pick_back.1 = (f32[32,1024]{1,0:T(8,128)S(1)}, f32[32,1024]{1,0:T(8,128)S(1)}) custom-call(bf16[256,256]{1,0:T(8,128)(2,1)S(1)} %bitcast.17, bf16[256,256]{1,0:T(8,128)(2,1)S(1)} %collective-permute-done.refs_1_, bf16[256,256]{1,0:T(8,128)(2,1)S(1)} %collective-permute-done.1.refs_2_, bf16[256,256]{1,0:T(8,128)(2,1)S(1)} %collective-permute-done.2.refs_3_, ...), custom_call_target="tpu_custom_call" | custom-call | flops 4000000000 | tf_op jit(solution)/shard_map/pick_back/pallas_call | solution.py:70
  18.5 1.3 %collective-permute-done.3 = f32[32,1024]{1,0:T(8,128)S(1)} collective-permute-done((f32[32,1024]{1,0:T(8,128)S(1)}, f32[32,1024]{1,0:T(8,128)S(1)}, u32[]{:S(2)}, u32[]{:S(2)}) %collective-permute-start.3) | collective-permute-done | bytes 131104 | tf_op jit(solution)/shard_map/ppermute | solution.py:263
  19.8 1.5 %collective-permute-start.4 = (f32[32,1024]{1,0:T(8,128)S(1)}, f32[32,1024]{1,0:T(8,128)S(1)}, u32[]{:S(2)}, u32[]{:S(2)}) collective-permute-start(f32[32,1024]{1,0:T(8,128)S(1)} %add.46), channel_id=1, source_target_pairs={{0,2},{1,3},{2,0},{3,1},{4,6},{5,7},{6,4},{7,5},{8,10},{9,11},{10,... | collective-permute-start | bytes 393224 | tf_op jit(solution)/shard_map/ppermute | solution.py:263
  21.4 4.1 %collective-permute-done.4 = f32[32,1024]{1,0:T(8,128)S(1)} collective-permute-done((f32[32,1024]{1,0:T(8,128)S(1)}, f32[32,1024]{1,0:T(8,128)S(1)}, u32[]{:S(2)}, u32[]{:S(2)}) %collective-permute-start.4) | collective-permute-done | bytes 131104 | tf_op jit(solution)/shard_map/ppermute | solution.py:263
  25.5 1.2 %collective-permute-done.5.refs_0_.refs_11_.refs_3_ = bf16[32,1024]{1,0:T(8,128)(2,1)S(1)} collective-permute-done((bf16[32,1024]{1,0:T(8,128)(2,1)S(1)}, bf16[32,1024]{1,0:T(8,128)(2,1)S(1)}, u32[]{:S(2)}, u32[]{:S(2)}) %collective-permute-start.5) | collective-permute-done | bytes 65568 | tf_op jit(solution)/shard_map/ppermute | solution.py:263
  26.8 0.3 collective-permute-done.6.refs_0_.refs_1_
  27.1 0.9 terms_first.1.refs_1_.refs_3_
  28.1 0.4 send_1.1
  28.5 5.8 %collective-permute-start.8 = (bf16[256,1280]{1,0:T(8,128)(2,1)S(1)}, bf16[256,1280]{1,0:T(8,128)(2,1)S(1)}, u32[]{:S(2)}, u32[]{:S(2)}) collective-permute-start(bf16[256,1280]{1,0:T(8,128)(2,1)S(1)} %send_1.1), channel_id=1, source_target_pairs={{0,4},{8,12},{4,0},{12,8},{1,5},{9,13},{5,1},{13,9},{2,6},{10,14},... | collective-permute-start | bytes 1966088 | tf_op jit(solution)/shard_map/ppermute | solution.py:258
  34.3 0.7 collective-permute-start.9
  35.0 1.6 %collective-permute-start.10 = (bf16[1024,256]{1,0:T(8,128)(2,1)S(1)}, bf16[1024,256]{1,0:T(8,128)(2,1)S(1)}, u32[]{:S(2)}, u32[]{:S(2)}) collective-permute-start(bf16[1024,256]{1,0:T(8,128)(2,1)S(1)} %copy-done.4), channel_id=1, source_target_pairs={{0,2},{1,3},{2,0},{3,1},{4,6},{5,7},{6,4},{7,5},{8,10},{9,11},{10,... | collective-permute-start | bytes 1572872 | tf_op jit(solution)/shard_map/ppermute | solution.py:263
  36.6 2.3 %terms_rest.1 = (f32[256,1280]{1,0:T(8,128)S(1)}, f32[256,1280]{1,0:T(8,128)S(1)}, f32[256,1280]{1,0:T(8,128)S(1)}) custom-call(bf16[32,1024]{1,0:T(8,128)(2,1)S(1)} %collective-permute-done.5.refs_0_.refs_11_.refs_3_, bf16[32,1024]{1,0:T(8,128)(2,1)S(1)} %multiply_convert_fusion.refs_1_.refs_10_.refs_2_, ...), custom_call_target="tpu_custom_call" | custom-call | tf_op jit(solution)/shard_map/terms_rest/pallas_call | solution.py:70
  38.9 2.0 %pick_1.1.refs_4_ = f32[64,1024]{1,0:T(8,128)S(1)} custom-call(bf16[256,1280]{1,0:T(8,128)(2,1)S(1)} %collective-permute-done.6.refs_0_.refs_1_, bf16[256,1280]{1,0:T(8,128)(2,1)S(1)} %collective-permute-done.7.refs_0_.refs_1_.refs_4_, s32[1,1024]{1,0:T(1,128)S(1)} %compare_select_fusion.refs_1_.refs_4_.refs_2_.refs_12_.refs_7_, ...), custom_call_target="tpu_custom_call" | custom-call | flops 4000000000 | tf_op jit(solution)/shard_map/pick_1/pallas_call | solution.py:70
  40.9 8.8 %collective-permute-done.8.refs_1_.refs_0_.refs_2_ = bf16[256,1280]{1,0:T(8,128)(2,1)S(1)} collective-permute-done((bf16[256,1280]{1,0:T(8,128)(2,1)S(1)}, bf16[256,1280]{1,0:T(8,128)(2,1)S(1)}, u32[]{:S(2)}, u32[]{:S(2)}) %collective-permute-start.8) | collective-permute-done | bytes 655392 | tf_op jit(solution)/shard_map/ppermute | solution.py:258
  49.7 0.7 send_2.1
  50.4 3.7 %collective-permute-start.11 = (bf16[256,1280]{1,0:T(8,128)(2,1)S(1)}, bf16[256,1280]{1,0:T(8,128)(2,1)S(1)}, u32[]{:S(2)}, u32[]{:S(2)}) collective-permute-start(bf16[256,1280]{1,0:T(8,128)(2,1)S(1)} %get-tuple-element.100), channel_id=1, source_target_pairs={{0,4},{8,12},{4,0},{12,8},{1,5},{9,13},{5,1},{13,9},{2,6},{10,14},... | collective-permute-start | bytes 1966088 | tf_op jit(solution)/shard_map/ppermute | solution.py:258
  54.1 0.7 collective-permute-start.12
  54.9 0.5 collective-permute-start.14
  55.4 1.1 %pick_2.1.refs_3_ = f32[64,1024]{1,0:T(8,128)S(1)} custom-call(bf16[256,1280]{1,0:T(8,128)(2,1)S(1)} %collective-permute-done.8.refs_1_.refs_0_.refs_2_, bf16[256,1280]{1,0:T(8,128)(2,1)S(1)} %collective-permute-done.9.refs_0_.refs_1_.refs_3_, s32[1,1024]{1,0:T(1,128)S(1)} %compare_select_fusion.refs_1_.refs_4_.refs_2_.refs_12_.refs_7_, ...), custom_call_target="tpu_custom_call" | custom-call | flops 4000000000 | tf_op jit(solution)/shard_map/pick_2/pallas_call | solution.py:70
  56.8 1.5 %collective-permute-start.17 = (bf16[1024,256]{1,0:T(8,128)(2,1)S(1)}, bf16[1024,256]{1,0:T(8,128)(2,1)S(1)}, u32[]{:S(2)}, u32[]{:S(2)}) collective-permute-start(bf16[1024,256]{1,0:T(8,128)(2,1)S(1)} %add_convert_fusion), channel_id=1, source_target_pairs={{0,2},{1,3},{2,0},{3,1},{4,6},{5,7},{6,4},{7,5},{8,10},{9,11},{10,... | collective-permute-start | bytes 1572872 | tf_op jit(solution)/shard_map/ppermute | solution.py:263
  58.3 6.9 %input_grad_most.1.refs_1_ = f32[1024,1280]{1,0:T(8,128)S(1)} custom-call(bf16[256,1280]{1,0:T(8,128)(2,1)S(1)} %bitcast.13, bf16[256,1280]{1,0:T(8,128)(2,1)S(1)} %collective-permute-done.6.refs_0_.refs_1_, bf16[256,1280]{1,0:T(8,128)(2,1)S(1)} %collective-permute-done.8.refs_1_.refs_0_.refs_2_, ...), custom_call_target="tpu_custom_call" | custom-call | tf_op jit(solution)/shard_map/input_grad_most/pallas_call | solution.py:70
  65.2 3.5 %collective-permute-done.11.refs_1_.refs_0_ = bf16[256,1280]{1,0:T(8,128)(2,1)S(1)} collective-permute-done((bf16[256,1280]{1,0:T(8,128)(2,1)S(1)}, bf16[256,1280]{1,0:T(8,128)(2,1)S(1)}, u32[]{:S(2)}, u32[]{:S(2)}) %collective-permute-start.11) | collective-permute-done | bytes 655392 | tf_op jit(solution)/shard_map/ppermute | solution.py:258
  68.7 0.8 send_3.1
  69.5 3.7 %collective-permute-start.21 = (bf16[256,1280]{1,0:T(8,128)(2,1)S(1)}, bf16[256,1280]{1,0:T(8,128)(2,1)S(1)}, u32[]{:S(2)}, u32[]{:S(2)}) collective-permute-start(bf16[256,1280]{1,0:T(8,128)(2,1)S(1)} %get-tuple-element.137), channel_id=1, source_target_pairs={{0,4},{8,12},{4,0},{12,8},{1,5},{9,13},{5,1},{13,9},{2,6},{10,14},... | collective-permute-start | bytes 1966088 | tf_op jit(solution)/shard_map/ppermute | solution.py:258
  73.2 0.7 collective-permute-start.22
  73.9 1.1 %pick_3.1 = (f32[32,1024]{1,0:T(8,128)S(1)}, f32[32,1024]{1,0:T(8,128)S(1)}) custom-call(bf16[256,1280]{1,0:T(8,128)(2,1)S(1)} %collective-permute-done.11.refs_1_.refs_0_, s32[1,1024]{1,0:T(1,128)S(1)} %compare_select_fusion.refs_1_.refs_4_.refs_2_.refs_12_.refs_7_, bf16[1024,1280]{1,0:T(8,128)(2,1)S(1)} %copy-done.1, f32[64,1024]{1,0:T(8,128)S(1)} %pick_2.1.refs_3_), custom_call_target="tpu_custom_call" | custom-call | flops 4000000000 | tf_op jit(solution)/shard_map/pick_3/pallas_call | solution.py:70
  75.3 1.3 %collective-permute-done.18 = f32[32,1024]{1,0:T(8,128)S(1)} collective-permute-done((f32[32,1024]{1,0:T(8,128)S(1)}, f32[32,1024]{1,0:T(8,128)S(1)}, u32[]{:S(2)}, u32[]{:S(2)}) %collective-permute-start.18) | collective-permute-done | bytes 131104 | tf_op jit(solution)/shard_map/ppermute | solution.py:263
  76.6 1.6 %collective-permute-start.19 = (f32[32,1024]{1,0:T(8,128)S(1)}, f32[32,1024]{1,0:T(8,128)S(1)}, u32[]{:S(2)}, u32[]{:S(2)}) collective-permute-start(f32[32,1024]{1,0:T(8,128)S(1)} %add.51), channel_id=1, source_target_pairs={{0,2},{1,3},{2,0},{3,1},{4,6},{5,7},{6,4},{7,5},{8,10},{9,11},{10,... | collective-permute-start | bytes 393224 | tf_op jit(solution)/shard_map/ppermute | solution.py:263
  78.2 4.1 %collective-permute-done.19 = f32[32,1024]{1,0:T(8,128)S(1)} collective-permute-done((f32[32,1024]{1,0:T(8,128)S(1)}, f32[32,1024]{1,0:T(8,128)S(1)}, u32[]{:S(2)}, u32[]{:S(2)}) %collective-permute-start.19) | collective-permute-done | bytes 131104 | tf_op jit(solution)/shard_map/ppermute | solution.py:263
  82.3 1.2 %collective-permute-done.20.refs_0_.refs_6_ = bf16[32,1024]{1,0:T(8,128)(2,1)S(1)} collective-permute-done((bf16[32,1024]{1,0:T(8,128)(2,1)S(1)}, bf16[32,1024]{1,0:T(8,128)(2,1)S(1)}, u32[]{:S(2)}, u32[]{:S(2)}) %collective-permute-start.20) | collective-permute-done | bytes 65568 | tf_op jit(solution)/shard_map/ppermute | solution.py:263
  83.6 0.8 up_terms.1
  84.4 2.9 %collective-permute-start.23 = (bf16[256,256]{1,0:T(8,128)(2,1)S(1)}, bf16[256,256]{1,0:T(8,128)(2,1)S(1)}, u32[]{:S(2)}, u32[]{:S(2)}) collective-permute-start(bf16[256,256]{1,0:T(8,128)(2,1)S(1)} %get-tuple-element.144), channel_id=1, source_target_pairs={{0,4},{4,8},{8,12},{12,0},{1,5},{5,9},{9,13},{13,1},{2,6},{6,10},{... | collective-permute-start | bytes 393224 | tf_op jit(solution)/shard_map/ppermute | solution.py:258
  87.5 2.6 %collective-permute-start.25 = (bf16[256,256]{1,0:T(8,128)(2,1)S(1)}, bf16[256,256]{1,0:T(8,128)(2,1)S(1)}, u32[]{:S(2)}, u32[]{:S(2)}) collective-permute-start(bf16[256,256]{1,0:T(8,128)(2,1)S(1)} %get-tuple-element.146), channel_id=1, source_target_pairs={{0,12},{4,0},{8,4},{12,8},{1,13},{5,1},{9,5},{13,9},{2,14},{6,2},{... | collective-permute-start | bytes 393224 | tf_op jit(solution)/shard_map/ppermute | solution.py:258
  90.0 2.7 %input_grad.1 = bf16[1024,1280]{1,0:T(8,128)(2,1)} custom-call(bf16[256,1280]{1,0:T(8,128)(2,1)S(1)} %collective-permute-done.11.refs_1_.refs_0_, f32[1024,1280]{1,0:T(8,128)S(1)} %input_grad_most.1.refs_1_, bf16[32,1024]{1,0:T(8,128)(2,1)S(1)} %multiply_convert_fusion.refs_1_.refs_10_.refs_2_, ...), custom_call_target="tpu_custom_call" | custom-call | tf_op jit(solution)/shard_map/input_grad/pallas_call | solution.py:70
  92.7 2.3 %projected.1 = bf16[1024,256]{1,0:T(8,128)(2,1)} custom-call(bf16[256,256]{1,0:T(8,128)(2,1)S(1)} %bitcast.18, bf16[256,256]{1,0:T(8,128)(2,1)S(1)} %collective-permute-done.refs_1_, bf16[256,256]{1,0:T(8,128)(2,1)S(1)} %collective-permute-done.1.refs_2_, bf16[256,256]{1,0:T(8,128)(2,1)S(1)} %collective-permute-done.2.refs_3_, ...), custom_call_target="tpu_custom_call" | custom-call | tf_op jit(solution)/shard_map/projected/pallas_call | solution.py:70
  95.0 1.7 %grad_down.1 = f32[256,1280]{1,0:T(8,128)} custom-call(bf16[256,1280]{1,0:T(8,128)(2,1)S(1)} %collective-permute-done.21.refs_0_, bf16[256,1280]{1,0:T(8,128)(2,1)S(1)} %collective-permute-done.22.refs_1_, f32[256,1280]{1,0:T(8,128)S(1)} %get-tuple-element.143.refs_2_), custom_call_target="tpu_custom_call" | custom-call | flops 8000000000 | tf_op jit(solution)/shard_map/grad_down/pallas_call | solution.py:70
  96.8 2.4 %collective-permute-done.24 = bf16[256,256]{1,0:T(8,128)(2,1)S(1)} collective-permute-done((bf16[256,256]{1,0:T(8,128)(2,1)S(1)}, bf16[256,256]{1,0:T(8,128)(2,1)S(1)}, u32[]{:S(2)}, u32[]{:S(2)}) %collective-permute-start.24) | collective-permute-done | bytes 131104 | tf_op jit(solution)/shard_map/ppermute | solution.py:258
  99.1 0.8 convert_add_fusion.1
  (42 shorter events, 1.3 us)
Async XLA Ops:
  0.6 15.5 %collective-permute-start = (bf16[256,256]{1,0:T(8,128)(2,1)}, bf16[256,256]{1,0:T(8,128)(2,1)S(1)}, u32[]{:S(2)}, u32[]{:S(2)}) collective-permute-start(bf16[256,256]{1,0:T(8,128)(2,1)} %bitcast.14), channel_id=1, source_target_pairs={{4,0},{0,4},{12,8},{8,12},{5,1},{1,5},{13,9},{9,13},{6,2},{2,6},{1... | collective-permute-start | bytes 393224 | tf_op jit(solution)/shard_map/ppermute | solution.py:258
  3.7 13.2 %collective-permute-start.1 = (bf16[256,256]{1,0:T(8,128)(2,1)}, bf16[256,256]{1,0:T(8,128)(2,1)S(1)}, u32[]{:S(2)}, u32[]{:S(2)}) collective-permute-start(bf16[256,256]{1,0:T(8,128)(2,1)} %bitcast.15), channel_id=1, source_target_pairs={{8,0},{12,4},{0,8},{4,12},{9,1},{13,5},{1,9},{5,13},{10,2},{14,6},... | collective-permute-start | bytes 393224 | tf_op jit(solution)/shard_map/ppermute | solution.py:258
  6.3 10.6 %collective-permute-start.2 = (bf16[256,256]{1,0:T(8,128)(2,1)}, bf16[256,256]{1,0:T(8,128)(2,1)S(1)}, u32[]{:S(2)}, u32[]{:S(2)}) collective-permute-start(bf16[256,256]{1,0:T(8,128)(2,1)} %bitcast.16), channel_id=1, source_target_pairs={{12,0},{8,4},{4,8},{0,12},{13,1},{9,5},{5,9},{1,13},{14,2},{10,6},... | collective-permute-start | bytes 393224 | tf_op jit(solution)/shard_map/ppermute | solution.py:258
  6.3 20.8 %collective-permute-start.6 = (bf16[256,1280]{1,0:T(8,128)(2,1)}, bf16[256,1280]{1,0:T(8,128)(2,1)S(1)}, u32[]{:S(2)}, u32[]{:S(2)}) collective-permute-start(bf16[256,1280]{1,0:T(8,128)(2,1)} %bitcast.10), channel_id=1, source_target_pairs={{0,4},{8,12},{4,0},{12,8},{1,5},{9,13},{5,1},{13,9},{2,6},{10,14},... | collective-permute-start | bytes 1966088 | tf_op jit(solution)/shard_map/ppermute | solution.py:258
  7.2 19.9 %collective-permute-start.7 = (bf16[256,1280]{1,0:T(8,128)(2,1)}, bf16[256,1280]{1,0:T(8,128)(2,1)S(1)}, u32[]{:S(2)}, u32[]{:S(2)}) collective-permute-start(bf16[256,1280]{1,0:T(8,128)(2,1)} %bitcast.11), channel_id=1, source_target_pairs={{4,8},{8,4},{5,9},{9,5},{6,10},{10,6},{7,11},{11,7},{20,24},{24,20... | collective-permute-start | bytes 1966088 | tf_op jit(solution)/shard_map/ppermute | solution.py:258
  8.6 1.7 %copy-start = (bf16[1024,1280]{1,0:T(8,128)(2,1)S(1)}, bf16[1024,1280]{1,0:T(8,128)(2,1)}, u32[]{:S(2)}) copy-start(bf16[1024,1280]{1,0:T(8,128)(2,1)} %refs_2_.3) | copy-start | bytes 7864324
  10.3 1.7 %copy-start.2 = (bf16[1280,1024]{1,0:T(8,128)(2,1)S(1)}, bf16[1280,1024]{1,0:T(8,128)(2,1)}, u32[]{:S(2)}) copy-start(bf16[1280,1024]{1,0:T(8,128)(2,1)} %refs_9_.1) | copy-start | bytes 7864324
  12.1 2.9 %copy-start.5 = (bf16[4,1280,64]{1,2,0:T(8,128)(2,1)S(1)}, bf16[4,1280,64]{1,2,0:T(8,128)(2,1)}, u32[]{:S(2)}) copy-start(bf16[4,1280,64]{1,2,0:T(8,128)(2,1)} %param.9) | copy-start | bytes 1966084
  15.0 1.9 %copy-start.4 = (bf16[1024,256]{1,0:T(8,128)(2,1)S(1)}, bf16[1024,256]{1,0:T(8,128)(2,1)}, u32[]{:S(2)}) copy-start(bf16[1024,256]{1,0:T(8,128)(2,1)} %refs_3_.9) | copy-start | bytes 1572868
  15.0 1.9 %copy-start.6 = (bf16[4,64,256]{2,1,0:T(8,128)(2,1)S(1)}, bf16[4,64,256]{2,1,0:T(8,128)(2,1)}, u32[]{:S(2)}) copy-start(bf16[4,64,256]{2,1,0:T(8,128)(2,1)} %param.10) | copy-start | bytes 393220
  16.9 10.2 %copy-start.1 = (bf16[1024,1280]{1,0:T(8,128)(2,1)S(1)}, bf16[1024,1280]{1,0:T(8,128)(2,1)}, u32[]{:S(2)}) copy-start(bf16[1024,1280]{1,0:T(8,128)(2,1)} %refs_2_.3) | copy-start | bytes 7864324
  18.4 1.4 %collective-permute-start.3 = (f32[32,1024]{1,0:T(8,128)S(1)}, f32[32,1024]{1,0:T(8,128)S(1)}, u32[]{:S(2)}, u32[]{:S(2)}) collective-permute-start(f32[32,1024]{1,0:T(8,128)S(1)} %get-tuple-element.84), channel_id=1, source_target_pairs={{0,1},{1,0},{2,3},{3,2},{4,5},{5,4},{6,7},{7,6},{8,9},{9,8},{10,11... | collective-permute-start | bytes 393224 | tf_op jit(solution)/shard_map/ppermute | solution.py:263
  19.8 5.6 %collective-permute-start.4 = (f32[32,1024]{1,0:T(8,128)S(1)}, f32[32,1024]{1,0:T(8,128)S(1)}, u32[]{:S(2)}, u32[]{:S(2)}) collective-permute-start(f32[32,1024]{1,0:T(8,128)S(1)} %add.46), channel_id=1, source_target_pairs={{0,2},{1,3},{2,0},{3,1},{4,6},{5,7},{6,4},{7,5},{8,10},{9,11},{10,... | collective-permute-start | bytes 393224 | tf_op jit(solution)/shard_map/ppermute | solution.py:263
  25.5 1.3 %collective-permute-start.5 = (bf16[32,1024]{1,0:T(8,128)(2,1)S(1)}, bf16[32,1024]{1,0:T(8,128)(2,1)S(1)}, u32[]{:S(2)}, u32[]{:S(2)}) collective-permute-start(bf16[32,1024]{1,0:T(8,128)(2,1)S(1)} %multiply_convert_fusion.refs_1_.refs_10_.refs_2_), channel_id=1, source_target_pairs={{0,1},{1,0},{2,3},{3,2},{4,5},{5,4},{6,7},{7,6},{8,9},{9,8},{10,11... | collective-permute-start | bytes 196616 | tf_op jit(solution)/shard_map/ppermute | solution.py:263
  28.0 26.8 %collective-permute-start.16 = (f32[1024,256]{1,0:T(8,128)S(1)}, f32[1024,256]{1,0:T(8,128)S(1)}, u32[]{:S(2)}, u32[]{:S(2)}) collective-permute-start(f32[1024,256]{1,0:T(8,128)S(1)} %get-tuple-element.129), channel_id=1, source_target_pairs={{0,1},{1,0},{2,3},{3,2},{4,5},{5,4},{6,7},{7,6},{8,9},{9,8},{10,11... | collective-permute-start | bytes 3145736 | tf_op jit(solution)/shard_map/ppermute | solution.py:263
  28.5 21.2 %collective-permute-start.8 = (bf16[256,1280]{1,0:T(8,128)(2,1)S(1)}, bf16[256,1280]{1,0:T(8,128)(2,1)S(1)}, u32[]{:S(2)}, u32[]{:S(2)}) collective-permute-start(bf16[256,1280]{1,0:T(8,128)(2,1)S(1)} %send_1.1), channel_id=1, source_target_pairs={{0,4},{8,12},{4,0},{12,8},{1,5},{9,13},{5,1},{13,9},{2,6},{10,14},... | collective-permute-start | bytes 1966088 | tf_op jit(solution)/shard_map/ppermute | solution.py:258
  34.3 15.4 %collective-permute-start.9 = (bf16[256,1280]{1,0:T(8,128)(2,1)S(1)}, bf16[256,1280]{1,0:T(8,128)(2,1)S(1)}, u32[]{:S(2)}, u32[]{:S(2)}) collective-permute-start(bf16[256,1280]{1,0:T(8,128)(2,1)S(1)} %collective-permute-done.6.refs_0_.refs_1_), channel_id=1, source_target_pairs={{4,8},{8,4},{5,9},{9,5},{6,10},{10,6},{7,11},{11,7},{20,24},{24,20... | collective-permute-start | bytes 1966088 | tf_op jit(solution)/shard_map/ppermute | solution.py:258
  35.0 15.4 %collective-permute-start.10 = (bf16[1024,256]{1,0:T(8,128)(2,1)S(1)}, bf16[1024,256]{1,0:T(8,128)(2,1)S(1)}, u32[]{:S(2)}, u32[]{:S(2)}) collective-permute-start(bf16[1024,256]{1,0:T(8,128)(2,1)S(1)} %copy-done.4), channel_id=1, source_target_pairs={{0,2},{1,3},{2,0},{3,1},{4,6},{5,7},{6,4},{7,5},{8,10},{9,11},{10,... | collective-permute-start | bytes 1572872 | tf_op jit(solution)/shard_map/ppermute | solution.py:263
  38.9 36.1 %collective-permute-start.15 = (f32[1024,256]{1,0:T(8,128)S(1)}, f32[1024,256]{1,0:T(8,128)S(1)}, u32[]{:S(2)}, u32[]{:S(2)}) collective-permute-start(f32[1024,256]{1,0:T(8,128)S(1)} %get-tuple-element.127), channel_id=1, source_target_pairs={{0,1},{1,0},{2,3},{3,2},{4,5},{5,4},{6,7},{7,6},{8,9},{9,8},{10,11... | collective-permute-start | bytes 3145736 | tf_op jit(solution)/shard_map/ppermute | solution.py:263
  50.4 18.3 %collective-permute-start.11 = (bf16[256,1280]{1,0:T(8,128)(2,1)S(1)}, bf16[256,1280]{1,0:T(8,128)(2,1)S(1)}, u32[]{:S(2)}, u32[]{:S(2)}) collective-permute-start(bf16[256,1280]{1,0:T(8,128)(2,1)S(1)} %get-tuple-element.100), channel_id=1, source_target_pairs={{0,4},{8,12},{4,0},{12,8},{1,5},{9,13},{5,1},{13,9},{2,6},{10,14},... | collective-permute-start | bytes 1966088 | tf_op jit(solution)/shard_map/ppermute | solution.py:258
  54.1 14.6 %collective-permute-start.12 = (bf16[256,1280]{1,0:T(8,128)(2,1)S(1)}, bf16[256,1280]{1,0:T(8,128)(2,1)S(1)}, u32[]{:S(2)}, u32[]{:S(2)}) collective-permute-start(bf16[256,1280]{1,0:T(8,128)(2,1)S(1)} %get-tuple-element.101), channel_id=1, source_target_pairs={{4,8},{8,4},{5,9},{9,5},{6,10},{10,6},{7,11},{11,7},{20,24},{24,20... | collective-permute-start | bytes 1966088 | tf_op jit(solution)/shard_map/ppermute | solution.py:258
  54.8 2.0 %collective-permute-start.13 = (bf16[1024,256]{1,0:T(8,128)(2,1)S(1)}, bf16[1024,256]{1,0:T(8,128)(2,1)S(1)}, u32[]{:S(2)}, u32[]{:S(2)}) collective-permute-start(bf16[1024,256]{1,0:T(8,128)(2,1)S(1)} %copy-done.4), channel_id=1, source_target_pairs={{0,1},{1,0},{2,3},{3,2},{4,5},{5,4},{6,7},{7,6},{8,9},{9,8},{10,11... | collective-permute-start | bytes 1572872 | tf_op jit(solution)/shard_map/ppermute | solution.py:263
  54.9 3.4 %collective-permute-start.14 = (bf16[1024,256]{1,0:T(8,128)(2,1)S(1)}, bf16[1024,256]{1,0:T(8,128)(2,1)S(1)}, u32[]{:S(2)}, u32[]{:S(2)}) collective-permute-start(bf16[1024,256]{1,0:T(8,128)(2,1)S(1)} %collective-permute-done.10.refs_7_), channel_id=1, source_target_pairs={{0,1},{1,0},{2,3},{3,2},{4,5},{5,4},{6,7},{7,6},{8,9},{9,8},{10,11... | collective-permute-start | bytes 1572872 | tf_op jit(solution)/shard_map/ppermute | solution.py:263
  56.5 1.8 %copy-start.3 = (bf16[1280,1024]{1,0:T(8,128)(2,1)S(1)}, bf16[1280,1024]{1,0:T(8,128)(2,1)}, u32[]{:S(2)}) copy-start(bf16[1280,1024]{1,0:T(8,128)(2,1)} %refs_9_.1) | copy-start | bytes 7864324
  56.8 18.2 %collective-permute-start.17 = (bf16[1024,256]{1,0:T(8,128)(2,1)S(1)}, bf16[1024,256]{1,0:T(8,128)(2,1)S(1)}, u32[]{:S(2)}, u32[]{:S(2)}) collective-permute-start(bf16[1024,256]{1,0:T(8,128)(2,1)S(1)} %add_convert_fusion), channel_id=1, source_target_pairs={{0,2},{1,3},{2,0},{3,1},{4,6},{5,7},{6,4},{7,5},{8,10},{9,11},{10,... | collective-permute-start | bytes 1572872 | tf_op jit(solution)/shard_map/ppermute | solution.py:263
  69.5 25.5 %collective-permute-start.21 = (bf16[256,1280]{1,0:T(8,128)(2,1)S(1)}, bf16[256,1280]{1,0:T(8,128)(2,1)S(1)}, u32[]{:S(2)}, u32[]{:S(2)}) collective-permute-start(bf16[256,1280]{1,0:T(8,128)(2,1)S(1)} %get-tuple-element.137), channel_id=1, source_target_pairs={{0,4},{8,12},{4,0},{12,8},{1,5},{9,13},{5,1},{13,9},{2,6},{10,14},... | collective-permute-start | bytes 1966088 | tf_op jit(solution)/shard_map/ppermute | solution.py:258
  73.2 21.8 %collective-permute-start.22 = (bf16[256,1280]{1,0:T(8,128)(2,1)S(1)}, bf16[256,1280]{1,0:T(8,128)(2,1)S(1)}, u32[]{:S(2)}, u32[]{:S(2)}) collective-permute-start(bf16[256,1280]{1,0:T(8,128)(2,1)S(1)} %get-tuple-element.138), channel_id=1, source_target_pairs={{4,8},{8,4},{5,9},{9,5},{6,10},{10,6},{7,11},{11,7},{20,24},{24,20... | collective-permute-start | bytes 1966088 | tf_op jit(solution)/shard_map/ppermute | solution.py:258
  75.2 1.4 %collective-permute-start.18 = (f32[32,1024]{1,0:T(8,128)S(1)}, f32[32,1024]{1,0:T(8,128)S(1)}, u32[]{:S(2)}, u32[]{:S(2)}) collective-permute-start(f32[32,1024]{1,0:T(8,128)S(1)} %get-tuple-element.131), channel_id=1, source_target_pairs={{0,1},{1,0},{2,3},{3,2},{4,5},{5,4},{6,7},{7,6},{8,9},{9,8},{10,11... | collective-permute-start | bytes 393224 | tf_op jit(solution)/shard_map/ppermute | solution.py:263
  76.6 5.6 %collective-permute-start.19 = (f32[32,1024]{1,0:T(8,128)S(1)}, f32[32,1024]{1,0:T(8,128)S(1)}, u32[]{:S(2)}, u32[]{:S(2)}) collective-permute-start(f32[32,1024]{1,0:T(8,128)S(1)} %add.51), channel_id=1, source_target_pairs={{0,2},{1,3},{2,0},{3,1},{4,6},{5,7},{6,4},{7,5},{8,10},{9,11},{10,... | collective-permute-start | bytes 393224 | tf_op jit(solution)/shard_map/ppermute | solution.py:263
  82.3 1.3 %collective-permute-start.20 = (bf16[32,1024]{1,0:T(8,128)(2,1)S(1)}, bf16[32,1024]{1,0:T(8,128)(2,1)S(1)}, u32[]{:S(2)}, u32[]{:S(2)}) collective-permute-start(bf16[32,1024]{1,0:T(8,128)(2,1)S(1)} %add_convert_fusion.1.refs_1_.refs_5_), channel_id=1, source_target_pairs={{0,1},{1,0},{2,3},{3,2},{4,5},{5,4},{6,7},{7,6},{8,9},{9,8},{10,11... | collective-permute-start | bytes 196616 | tf_op jit(solution)/shard_map/ppermute | solution.py:263
  84.4 12.4 %collective-permute-start.23 = (bf16[256,256]{1,0:T(8,128)(2,1)S(1)}, bf16[256,256]{1,0:T(8,128)(2,1)S(1)}, u32[]{:S(2)}, u32[]{:S(2)}) collective-permute-start(bf16[256,256]{1,0:T(8,128)(2,1)S(1)} %get-tuple-element.144), channel_id=1, source_target_pairs={{0,4},{4,8},{8,12},{12,0},{1,5},{5,9},{9,13},{13,1},{2,6},{6,10},{... | collective-permute-start | bytes 393224 | tf_op jit(solution)/shard_map/ppermute | solution.py:258
  87.2 11.9 %collective-permute-start.24 = (bf16[256,256]{1,0:T(8,128)(2,1)S(1)}, bf16[256,256]{1,0:T(8,128)(2,1)S(1)}, u32[]{:S(2)}, u32[]{:S(2)}) collective-permute-start(bf16[256,256]{1,0:T(8,128)(2,1)S(1)} %get-tuple-element.145), channel_id=1, source_target_pairs={{0,8},{4,12},{8,0},{12,4},{1,9},{5,13},{9,1},{13,5},{2,10},{6,14},... | collective-permute-start | bytes 393224 | tf_op jit(solution)/shard_map/ppermute | solution.py:258
  87.5 11.7 %collective-permute-start.25 = (bf16[256,256]{1,0:T(8,128)(2,1)S(1)}, bf16[256,256]{1,0:T(8,128)(2,1)S(1)}, u32[]{:S(2)}, u32[]{:S(2)}) collective-permute-start(bf16[256,256]{1,0:T(8,128)(2,1)S(1)} %get-tuple-element.146), channel_id=1, source_target_pairs={{0,12},{4,0},{8,4},{12,8},{1,13},{5,1},{9,5},{13,9},{2,14},{6,2},{... | collective-permute-start | bytes 393224 | tf_op jit(solution)/shard_map/ppermute | solution.py:258

commit v4 on v3

v4 whole, which is shorter than its diff:
```python
import functools

import jax
import jax.numpy as jnp
from jax import lax
from jax.experimental import pallas as pl
from jax.experimental.pallas import tpu as pltpu
from jax.sharding import PartitionSpec as P

ADAPTER_SCALE = 2.0
F32 = jnp.float32
BF16 = jnp.bfloat16
VMEM_BYTES = 16 * 1024 * 1024

BACK_FLOPS = 4 * 10**9
SLOT_FLOPS = 3 * 10**9
SEND_FLOPS = 0, 10**9


def dot_nn(left, right):
    return jnp.dot(left, right, preferred_element_type=F32)


def dot_nt(left, right):
    return lax.dot_general(left, right, (((1,), (1,)), ((), ())), preferred_element_type=F32)


def dot_tn(left, right):
    return lax.dot_general(left, right, (((0,), (0,)), ((), ())), preferred_element_type=F32)


def tie(*values):
    return lax.optimization_barrier(values)


def alternatives(entry):
    choice = entry[2] if isinstance(entry, tuple) else None
    arrays = entry[:2] if isinstance(entry, tuple) else (entry,)
    return [tuple(a) if isinstance(a, list) else (a,) for a in arrays], choice


def local_kernel(name, kernel, outs, *operands, late=(), flops=0, stacked=False, scratch=()):
    late = [alternatives(entry) for entry in late]
    sources = [array for blocks, _ in late for alternative in blocks for array in alternative]
    slots = [
        jax.ShapeDtypeStruct(
            (sum(a.shape[0] for a in blocks[0]), blocks[0][0].shape[1]), blocks[0][0].dtype
        )
        for blocks, _ in late
    ]
    chunks = [max(len(alternative) for alternative in blocks) for blocks, _ in late]

    def fetching(*refs):
        ins, refs = refs[: len(sources)], refs[len(sources) :]
        direct, refs = refs[: len(operands)], refs[len(operands) :]
        results, refs = refs[: len(outs)], refs[len(outs) :]
        extra, refs = refs[: len(scratch)], refs[len(scratch) :]
        semaphores = refs[-1]
        fetched = refs[:-1]
        if stacked:
            rows = slots[0].shape[0]
            fetched = [fetched[0].at[pl.ds(i * rows, rows)] for i in range(len(late))]
        ins, waits = iter(ins), []
        for (blocks, choice), slot, count in zip(late, fetched, chunks):
            first_semaphore, copies = len(waits), []
            size = slot.shape[0] // count
            for alternative in blocks:
                parts = [
                    source.at[pl.ds(start, size)] if block.shape[0] > size else source
                    for block, source in [(block, next(ins)) for block in alternative]
                    for start in range(0, block.shape[0], size)
                ]
                copies.append(
                    [
                        pltpu.make_async_copy(
                            part, slot.at[pl.ds(i * size, size)], semaphores.at[first_semaphore + i]
                        )
                        for i, part in enumerate(parts)
                    ]
                )
            if choice is None:
                for copy in copies[0]:
                    copy.start()
            else:
                first = choice()
                for one, two in zip(*copies):
                    pl.when(first)(one.start)
                    pl.when(jnp.logical_not(first))(two.start)
            waits += copies[0]
        for copy in waits:
            copy.wait()
        kernel(*(refs[:1] if stacked else fetched), *direct, *results, *extra)

    buffers = [pltpu.VMEM(slot.shape, slot.dtype) for slot in slots]
    if stacked:
        rows, columns = slots[0].shape
        buffers = [pltpu.VMEM((len(slots) * rows, columns), slots[0].dtype)]
    return pl.pallas_call(
        fetching if late else kernel,
        name=name,
        out_shape=[jax.ShapeDtypeStruct(s, t) for s, t in outs],
        in_specs=[pl.BlockSpec(memory_space=pl.ANY)] * len(sources)
        + [pl.BlockSpec(memory_space=pltpu.VMEM)] * len(operands),
        out_specs=[pl.BlockSpec(memory_space=pltpu.VMEM)] * len(outs),
        scratch_shapes=[
            *scratch,
            *buffers,
            *([pltpu.SemaphoreType.DMA((sum(chunks),))] if late else []),
        ],
        compiler_params=pltpu.CompilerParams(vmem_limit_bytes=VMEM_BYTES),
        cost_estimate=pl.CostEstimate(flops=flops, bytes_accessed=0, transcendentals=0),
    )(*sources, *operands)


def tile_of(extent):
    return 256 if extent % 256 == 0 else 128


def spread_tile(values, places, offset, per_owner):
    return jnp.concatenate(
        [
            jnp.where(places == offset * per_owner + a, values, jnp.zeros((), values.dtype))
            for a in range(per_owner)
        ],
        axis=0,
    )


def pick_kernel(offsets, per_owner, has_start, halved, *refs):
    count = len(offsets)
    pieces, (places, rhs), rest = refs[:count], refs[count : count + 2], refs[count + 2 :]
    start, outs = (rest[0], rest[1:]) if has_start else (None, rest)
    tokens = rhs.shape[0]
    tile = tile_of(tokens)
    rank = pieces[0].shape[0] // per_owner
    core = lax.axis_index("narrow") % 2
    for i in range(tokens // tile):
        at = pl.ds(i * tile, tile)
        here, right = places[:, at], rhs[at, :]
        total = jnp.zeros((rank, tile), F32) if start is None else start[:, at]
        for piece, offset in zip(pieces, offsets):
            products = dot_nt(piece[...], right)
            for a in range(per_owner):
                total += jnp.where(
                    here == offset() * per_owner + a, products[a * rank : (a + 1) * rank], 0.0
                )
        if halved:
            low, high = total[: rank // 2], total[rank // 2 :]
            outs[0][:, at] = jnp.where(core == 0, low, high)
            outs[1][:, at] = jnp.where(core == 0, high, low)
        else:
            outs[0][:, at] = total


def pick(name, pieces, places, rhs, per_owner, start=None, halved=False, flops=0):
    rows = sum(block.shape[0] for block in alternatives(pieces[0][0])[0][0])
    rank, tokens = rows // per_owner, rhs.shape[0]
    kernel = functools.partial(
        pick_kernel, [o for _, o in pieces], per_owner, start is not None, halved
    )
    more = [] if start is None else [start]
    outs = [((rank // 2, tokens), F32)] * 2 if halved else [((rank, tokens), F32)]
    outs = local_kernel(
        name, kernel, outs, places, rhs, *more, late=[p for p, _ in pieces], flops=flops
    )
    return outs if halved else outs[0]


def whole(mine, other):
    first = lax.axis_index("narrow") % 2 == 0
    return jnp.concatenate(
        [jnp.where(first, mine[...], other[...]), jnp.where(first, other[...], mine[...])], axis=0
    )


def terms_kernel(offsets, per_owner, scale, other, mine, places, rhs, *outs):
    tile = tile_of(rhs.shape[1])
    values = whole(mine, other)
    for offset, out in zip(offsets, outs):
        wide = spread_tile(values, places[...], offset(), per_owner)

        def step(i, carry, wide=wide, out=out):
            at = pl.ds(pl.multiple_of(i * tile, tile), tile)
            out[:, at] = (scale * dot_nn(wide, rhs[:, at])).astype(out.dtype)
            return carry

        lax.fori_loop(0, rhs.shape[1] // tile, step, 0, unroll=True)


def outer_terms(name, values, places, rhs, offsets, types, per_owner, scale):
    mine, other = values
    shape = (2 * mine.shape[0] * per_owner, rhs.shape[1])
    kernel = functools.partial(terms_kernel, offsets, per_owner, scale)
    return local_kernel(
        name, kernel, [(shape, t) for t in types], mine, places, rhs, late=[other]
    )


def send_kernel(sides, owners, start, *refs):
    me = lax.axis_index("wide")
    got, terms, outs = refs[:2], refs[2:4], refs[4:]
    blocks, tile = len(outs) // 2, 64
    for side, (step, even_to_right, moving, summing) in enumerate(sides):
        to_right = (me % 2 == 0) == even_to_right
        passes_on = jnp.where(to_right, me >= step, me + step < owners)
        came, term, begin = got[side], terms[side], 0
        for out in outs[side * blocks : (side + 1) * blocks]:
            for i in range(out.shape[0] // tile):
                at = pl.ds(begin + i * tile, tile)
                value = came[at, :]
                if summing:
                    here = term[pl.ds(start + begin + i * tile, tile), :]
                    total = (here + value.astype(F32)).astype(BF16)
                    value = jnp.where(passes_on, value, total) if moving else total
                out[pl.ds(i * tile, tile), :] = value
            begin += out.shape[0]


def base_kernel(parts, x, weight, keep, give):
    part, width, rows = lax.axis_index("narrow"), keep.shape[1], x.shape[0]
    for s in range(parts):
        columns = pl.ds(pl.multiple_of((part ^ s) * width, width), width)
        out, start = (keep, give)[s % 2], s // 2 * rows
        for i in range(rows // 256):
            out[pl.ds(start + i * 256, 256), :] = dot_nn(
                x[pl.ds(i * 256, 256), :], weight[:, columns]
            )


def base_back_kernel(parts, *refs):
    cots, (weight, early, out, features) = refs[:parts], refs[parts:]
    part, width = lax.axis_index("narrow"), cots[0].shape[1]
    tile = 256
    for s, cot in enumerate(cots):
        columns = pl.ds(pl.multiple_of((part ^ s) * width, width), width)
        features[:, columns] = cot[...]
    for i in range(out.shape[0] // tile):
        at = pl.ds(i * tile, tile)
        out[at, :] = early[at, :] + dot_nt(features[at, :], weight[...])


def input_early_kernel(offsets, per_owner, pieces, mine, other, places, out):
    tile = 256
    values = whole(mine, other)
    for i in range(out.shape[0] // tile):
        at = pl.ds(i * tile, tile)
        here = values[:, i * tile : (i + 1) * tile]
        wide = [spread_tile(here, places[:, at], offset(), per_owner) for offset in offsets]
        out[at, :] = dot_tn(jnp.concatenate(wide, axis=0), pieces[...])


def input_grad_kernel(offsets, per_owner, pieces, base, mine, other, places, out):
    tile = 256
    values = whole(mine, other)
    for i in range(out.shape[0] // tile):
        at = pl.ds(i * tile, tile)
        here = values[:, i * tile : (i + 1) * tile]
        wide = [spread_tile(here, places[:, at], offset(), per_owner) for offset in offsets]
        term = dot_tn(jnp.concatenate(wide, axis=0), pieces[...])
        out[at, :] = (base[at, :] + term).astype(out.dtype)


def grad_down_kernel(from_a, from_b, term, out):
    tile = 64
    for i in range(out.shape[0] // tile):
        at = pl.ds(i * tile, tile)
        out[at, :] = term[at, :] + from_a[at, :].astype(F32) + from_b[at, :].astype(F32)


def projected_kernel(offsets, per_owner, *refs):
    ups = refs[: len(offsets)]
    base, more, mine, other, places, out = refs[len(offsets) :]
    values = whole(mine, other)
    tile = 256
    for i in range(out.shape[0] // tile):
        at = pl.ds(i * tile, tile)
        update = jnp.zeros((tile, out.shape[1]), F32)
        for offset, up in zip(offsets, ups):
            here = values[:, i * tile : (i + 1) * tile]
            update += dot_tn(spread_tile(here, places[:, at], offset(), per_owner), up[...])
        update = (ADAPTER_SCALE * update).astype(BF16).astype(F32)
        out[at, :] = (base[at, :] + more[at, :].astype(F32) + update).astype(out.dtype)


def pair_lists(right_senders, left_senders):
    return [
        [(d, d + 1) for d in right_senders if d % 2 == odd]
        + [(d, d - 1) for d in left_senders if d % 2 != odd]
        for odd in (0, 1)
    ]


def shift(value, pairs):
    return lax.ppermute(value, "wide", pairs) if pairs else None


def swap_narrow(value, bit):
    size = lax.axis_size("narrow")
    return lax.ppermute(value, "narrow", [(d, d ^ bit) for d in range(size)])


def narrow_bits():
    size, bits = lax.axis_size("narrow"), []
    while 1 << len(bits) < size:
        bits.append(1 << len(bits))
    return bits


def sum_narrow(mine, other, scale, core=(), during=None, chips=(), end=()):
    bits = narrow_bits()
    mine = mine + swap_narrow(other, bits[0])
    mine, *core = tie(mine, *core)
    if during is not None:
        chips = (*chips, *during(*core))
    for bit in bits[1:]:
        mine = mine + swap_narrow(mine, bit)
    mine, *chips = tie(mine, *chips)
    mine = (scale * mine).astype(BF16)
    other, *end = tie(swap_narrow(mine, bits[0]), *end)
    return (mine, other), core, chips, end


def body(x, token_adapter_index, weight, down, up, cot):
    owners, me = lax.axis_size("wide"), lax.axis_index("wide")
    parts = lax.axis_size("narrow")
    per_owner, width_part, rank = down.shape
    value_part = up.shape[2]
    rows = per_owner * rank
    tokens = x.shape[0]
    adapters = owners * per_owner
    last = owners - 1
    down_own = jnp.swapaxes(down, 1, 2).reshape(rows, width_part)
    up_own = up.reshape(rows, value_part)
    places = token_adapter_index[:, 0][None, :] - me * per_owner
    places = jnp.where(places < 0, places + adapters, places)

    def fixed(offset):
        return lambda: offset

    def by_side(at_even, at_odd):
        return lambda: jnp.where(lax.axis_index("wide") % 2 == 0, at_even, at_odd)

    def arriving(step, even_from_right):
        def offset():
            me = lax.axis_index("wide")
            from_right = (me % 2 == 0) == even_from_right
            right = jnp.where(me + step < owners, step, -owners)
            left = jnp.where(me >= step, owners - step, -owners)
            return jnp.where(from_right, right, left)

        return offset

    def from_a(step):
        def valid():
            me = lax.axis_index("wide")
            return jnp.where(me % 2 == 0, me + step < owners, me >= step)

        return valid

    def gather_pairs(step):
        return pair_lists(range(step - 1, last), range(1, owners - step + 1))

    def reduce_pairs(step):
        return pair_lists(range(min(step, last)), range(max(owners - step, 1), owners))

    right, left = range(last), range(1, owners)
    pairs_a, pairs_b = pair_lists(right, left)

    def across(bits):
        def offset():
            me = lax.axis_index("wide")
            return (me ^ bits) - me + jnp.where((me ^ bits) < me, owners, 0)

        return offset

    up_all = [(up_own, fixed(0))] + [
        (shift(up_own, [(d ^ bits, d) for d in range(owners)]), across(bits))
        for bits in range(1, owners)
    ]
    got_b = shift(down_own, pairs_b)
    got_a = shift(down_own, pairs_a)
    low = pick("pick_own", [(down_own, fixed(0))], places, x, per_owner, flops=2 * 10**9)

    near_bit, *far_bits = narrow_bits()

    def base_products(x):
        return local_kernel(
            "base",
            functools.partial(base_kernel, parts),
            [((parts // 2 * tokens, value_part), F32)] * 2,
            x,
            weight,
        )

    cot_here, low = tie(cot, low)
    back = pick("pick_back", up_all, places, cot_here, per_owner, halved=True, flops=BACK_FLOPS)
    back_mine, cot_near = tie(back[0], cot)
    back, cot_near = (back_mine, back[1]), swap_narrow(cot_near, near_bit)
    back, _, (base_keep, base_give), _ = sum_narrow(
        *back, ADAPTER_SCALE, core=(x,), during=base_products
    )

    offsets = [fixed(0)] + [by_side(owners - s, s) for s in range(1, owners)]
    terms = outer_terms("terms", back, places, x, offsets, [F32] * owners, per_owner, 1.0)
    *terms, got_a, got_b = tie(*terms, got_a, got_b)

    half = rows // 2
    got_a, got_b, pieces = [got_a], [got_b], {}
    for step in range(1, owners):
        gathers, reduces = gather_pairs(step + 1), reduce_pairs(step)
        live_a, live_b = gather_pairs(step)
        sides = [
            (step, True, bool(gathers[0]), bool(reduces[0])),
            (step, False, bool(gathers[1]), bool(reduces[1])),
        ]
        next_a, next_b = [], []
        for h in range(len(got_a)):
            if step == 2 and h == 1:
                got_a[h], got_b[h], low = tie(got_a[h], got_b[h], low)
            elif step > 2 and h == 1:
                got_a[h], got_b[h], low = tie(got_a[h], got_b[h], low)
            if step == 2 and h == 0:
                got_a[h], got_b[h], _ = tie(got_a[h], got_b[h], base_sum)
            if step == last and h == 0:
                got_a[h], got_b[h], early = tie(got_a[h], got_b[h], early)
            outs = [((half, width_part), BF16)] * (2 * (2 // len(got_a)))
            sends = local_kernel(
                f"send_{step}_{h}",
                functools.partial(send_kernel, sides, owners, h * half),
                outs,
                terms[step],
                terms[owners - step] if sides[1][3] else terms[step],
                late=[got_b[h], got_a[h]],
                flops=SEND_FLOPS[h],
            )
            *sends, got_a[h], got_b[h], x_late, places_here = tie(
                *sends, got_a[h], got_b[h], x, places
            )
            if step > 1 and h == 0:
                low = pick(
                    f"pick_{step - 1}", arrived, places, x_late, per_owner, low, flops=SLOT_FLOPS
                )
            if step == 1:
                base_give, cot_here, _ = tie(base_give, cot, sends[0])
                base_sum = base_keep + swap_narrow(base_give, near_bit)
                cots = {0: cot_here, near_bit: cot_near}
                for bit in far_bits:
                    block = swap_narrow(jnp.concatenate(list(cots.values()), axis=0), bit)
                    for i, s in enumerate(list(cots)):
                        cots[s | bit] = block[i * tokens : (i + 1) * tokens]
            if step == last - 1 and h == 1:
                near = [(down_own, fixed(0)), (pieces["a", 1], by_side(1, last))]
                near.append((pieces["b", 1], by_side(last, 1)))
                (early,) = local_kernel(
                    "input_early",
                    functools.partial(input_early_kernel, [o for _, o in near], per_owner),
                    [((tokens, width_part), F32)],
                    *back,
                    places_here,
                    late=[d for d, _ in near],
                    stacked=True,
                )
            for i in range(len(sends) // 2):
                next_b.append(shift(sends[len(sends) // 2 + i], pairs_b))
                next_a.append(shift(sends[i], pairs_a))
        if live_a:
            pieces["a", step] = got_a
        if live_b:
            pieces["b", step] = got_b
        arrived = [
            (pieces[side, step], arriving(step, side == "a"))
            for side in "ab"
            if (side, step) in pieces
        ]
        if 2 * step == owners:
            arrived = [((got_a, got_b, from_a(step)), by_side(step, owners - step))]
        got_a, got_b = next_a, next_b
    low = pick(f"pick_{last}", arrived, places, x, per_owner, low, True)
    *low, got_a[0], got_b[0] = tie(*low, got_a[0], got_b[0])


    def base_product(*held):
        cots.update(zip(cots, held[1:]))
        return local_kernel(
            "base_back",
            functools.partial(base_back_kernel, parts),
            [((tokens, width_part), F32)],
            *[cots[s] for s in range(parts)],
            weight,
            held[0],
            scratch=[pltpu.VMEM((tokens, parts * value_part), BF16)],
        )

    low, _, (got_a[1], got_b[1], base_back), _ = sum_narrow(
        *low,
        1.0,
        core=(early, *cots.values()),
        during=base_product,
        chips=(got_a[1], got_b[1]),
    )
    base_sum, _ = tie(base_sum, low[0])
    sums = {2 * i: base_sum[i * tokens : (i + 1) * tokens] for i in range(parts // 2)}
    for bit in far_bits[:-1]:
        for s in [s for s in sums if s & bit]:
            got = swap_narrow(sums.pop(s).astype(BF16), bit)
            sums[s ^ bit] = sums[s ^ bit] + got.astype(F32)
    base_came = swap_narrow(sums[far_bits[-1]].astype(BF16), far_bits[-1])
    grad_up, *up_terms = outer_terms(
        "up_terms",
        low,
        places,
        cot,
        [fixed(m) for m in range(owners)],
        [F32] + [BF16] * last,
        per_owner,
        ADAPTER_SCALE,
    )
    places_late, *up_terms = tie(places, *up_terms)
    got_up = [
        shift(term, [(d, (d + m) % owners) for d in range(owners)])
        for m, term in enumerate(up_terms, 1)
    ]

    projected = local_kernel(
        "projected",
        functools.partial(projected_kernel, [o for _, o in up_all], per_owner),
        [((tokens, value_part), BF16)],
        sums[0],
        base_came,
        *low,
        places_late,
        late=[u for u, _ in up_all],
    )[0]
    slots = [(pieces["a", last], arriving(last, True))]
    for step in range(2, last):
        a, b = pieces.get(("a", step)), pieces.get(("b", owners - step))
        slots.append(((a, b, from_a(step)) if b is not None else a, by_side(step, owners - step)))
    (input_grad,) = local_kernel(
        "input_grad",
        functools.partial(input_grad_kernel, [o for _, o in slots], per_owner),
        [((tokens, width_part), BF16)],
        base_back,
        *back,
        places_late,
        late=[d for d, _ in slots],
        stacked=True,
    )
    (grad_down,) = local_kernel(
        "grad_down",
        grad_down_kernel,
        [((rows, width_part), F32)],
        terms[0],
        late=[got_a, got_b],
    )

    grad_down, input_grad, projected, *got_up = tie(grad_down, input_grad, projected, *got_up)
    for got in got_up:
        grad_up += got.astype(F32)
    return (
        projected,
        input_grad,
        jnp.swapaxes(grad_down.reshape(per_owner, rank, width_part), 1, 2),
        grad_up.reshape(per_owner, rank, value_part),
    )


def solution(mesh):
    in_specs = (
        P(("groups", "wide"), "narrow"),
        P(("groups", "wide"), None),
        P("narrow", None),
        P(("groups", "wide"), "narrow", None),
        P(("groups", "wide"), None, "narrow"),
        P(("groups", "wide"), "narrow"),
    )
    out_specs = (
        P(("groups", "wide"), "narrow"),
        P(("groups", "wide"), "narrow"),
        P(("groups", "wide"), "narrow", None),
        P(("groups", "wide"), None, "narrow"),
    )
    return jax.shard_map(body, mesh=mesh, in_specs=in_specs, out_specs=out_specs, check_vma=False)
```

time: 100 us -> 98.2 us (0.982)
  waiting for transfers between devices: 29.1 us -> 14.8 us
  starting transfers between devices: 35.4 us -> 47.7 us
    ppermute x14 -> x20, starting transfers between devices: 28.3 us -> 40.8 us  [shift(): return lax.ppermute(value, 'wide', pairs) if pairs else None]
    ppermute x14 -> x20, waiting for transfers between devices: 15.7 us -> 7.33 us  [shift(): return lax.ppermute(value, 'wide', pairs) if pairs else None]
    ppermute x12 -> x10, waiting for transfers between devices: 13.4 us -> 7.45 us  [swap_narrow(): return lax.ppermute(value, 'narrow', [(d, d ^ bit) for d in range(size)])]
    pallas_call x16 -> x18, Pallas kernels: 29 us -> 29.3 us  [local_kernel(): pl.pallas_call(fetching if late else kernel, name=name, out_shape=[jax.Sh...]
    ppermute x12 -> x10, starting transfers between devices: 7.15 us -> 6.94 us  [swap_narrow(): return lax.ppermute(value, 'narrow', [(d, d ^ bit) for d in range(size)])]
  transfers between devices with their start and end apart: 26 -> 30, of which waited for: 12 -> 11; matrix products, arithmetic and copies ran while one was open for 1% -> 1% of each run, Pallas kernels for 28% -> 29%
where the time goes in v4:
time: 98.2 us; the launch traced here: 97.8 us
  starting transfers between devices  47.7 us (49%)
  Pallas kernels  29.3 us (30%)
  waiting for transfers between devices  14.8 us (15%)
  local copies, waits for them, and re-layouts  3.04 us (3%)
  other arithmetic  1.88 us (2%)
  between operations  1.06 us (1%)
    ppermute x20, starting transfers between devices, shift(): return lax.ppermute(value, 'wide', pairs) if pairs else None  40.8 us
    pallas_call x18, Pallas kernels, local_kernel(): pl.pallas_call(fetching if late else kernel, name=name, out_shape=[jax.Sh...  29.3 us
    ppermute x10, waiting for transfers between devices, swap_narrow(): return lax.ppermute(value, 'narrow', [(d, d ^ bit) for d in range(size)])  7.45 us
    ppermute x20, waiting for transfers between devices, shift(): return lax.ppermute(value, 'wide', pairs) if pairs else None  7.33 us
    ppermute x10, starting transfers between devices, swap_narrow(): return lax.ppermute(value, 'narrow', [(d, d ^ bit) for d in range(size)])  6.94 us
    unnamed x14, local copies, waits for them, and re-layouts  2.85 us
  transfers between devices with their start and end apart: 30, of which 11 were waited for; matrix products, arithmetic and copies ran while one was open for 1% of the time, Pallas kernels for 29%

profile of v4, /device:TPU:0, one launch (start us, length us, event | category | flops | bytes accessed | tf_op | source)
XLA Modules:
  0.0 97.8 jit_solution(14041393088682185460)
XLA Ops:
  0.6 3.1 %collective-permute-start = (bf16[256,256]{1,0:T(8,128)(2,1)}, bf16[256,256]{1,0:T(8,128)(2,1)S(1)}, u32[]{:S(2)}, u32[]{:S(2)}) collective-permute-start(bf16[256,256]{1,0:T(8,128)(2,1)} %bitcast.14), channel_id=1, source_target_pairs={{4,0},{0,4},{12,8},{8,12},{5,1},{1,5},{13,9},{9,13},{6,2},{2,6},{1... | collective-permute-start | bytes 393224 | tf_op jit(solution)/shard_map/ppermute | solution.py:294
  3.7 2.6 %collective-permute-start.1 = (bf16[256,256]{1,0:T(8,128)(2,1)}, bf16[256,256]{1,0:T(8,128)(2,1)S(1)}, u32[]{:S(2)}, u32[]{:S(2)}) collective-permute-start(bf16[256,256]{1,0:T(8,128)(2,1)} %bitcast.15), channel_id=1, source_target_pairs={{8,0},{12,4},{0,8},{4,12},{9,1},{13,5},{1,9},{5,13},{10,2},{14,6},... | collective-permute-start | bytes 393224 | tf_op jit(solution)/shard_map/ppermute | solution.py:294
  6.3 0.9 collective-permute-start.6
  7.2 0.7 collective-permute-start.7
  7.9 0.7 compare_select_fusion.refs_1_.refs_4_.refs_2_.refs_5_.refs_9_.refs_8_
  8.6 1.7 %copy-done = bf16[1024,1280]{1,0:T(8,128)(2,1)S(1)} copy-done((bf16[1024,1280]{1,0:T(8,128)(2,1)S(1)}, bf16[1024,1280]{1,0:T(8,128)(2,1)}, u32[]{:S(2)}) %copy-start) | copy-done | bytes 2621464
  10.4 1.1 %copy-done.4 = bf16[4,1280,64]{1,2,0:T(8,128)(2,1)S(1)} copy-done((bf16[4,1280,64]{1,2,0:T(8,128)(2,1)S(1)}, bf16[4,1280,64]{1,2,0:T(8,128)(2,1)}, u32[]{:S(2)}) %copy-start.4) | copy-done | bytes 655384
  11.4 1.1 %pick_own.1.refs_4_ = f32[64,1024]{1,0:T(8,128)S(1)} custom-call(bf16[256,1280]{1,0:T(8,128)(2,1)S(1)} %bitcast.12, s32[1,1024]{1,0:T(1,128)S(1)} %compare_select_fusion.refs_1_.refs_4_.refs_2_.refs_5_.refs_9_.refs_8_, bf16[1024,1280]{1,0:T(8,128)(2,1)S(1)} %copy-done), custom_call_target="tpu_custom_call" | custom-call | flops 2000000000 | tf_op jit(solution)/shard_map/pick_own/pallas_call | solution.py:98
  12.5 4.3 %collective-permute-done.1.refs_2_ = bf16[256,256]{1,0:T(8,128)(2,1)S(1)} collective-permute-done((bf16[256,256]{1,0:T(8,128)(2,1)}, bf16[256,256]{1,0:T(8,128)(2,1)S(1)}, u32[]{:S(2)}, u32[]{:S(2)}) %collective-permute-start.1) | collective-permute-done | bytes 131104 | tf_op jit(solution)/shard_map/ppermute | solution.py:294
  16.9 1.5 %pick_back.1 = (f32[32,1024]{1,0:T(8,128)S(1)}, f32[32,1024]{1,0:T(8,128)S(1)}) custom-call(bf16[256,256]{1,0:T(8,128)(2,1)S(1)} %bitcast.17, bf16[256,256]{1,0:T(8,128)(2,1)S(1)} %collective-permute-done.refs_1_, bf16[256,256]{1,0:T(8,128)(2,1)S(1)} %collective-permute-done.1.refs_2_, bf16[256,256]{1,0:T(8,128)(2,1)S(1)} %collective-permute-done.2.refs_3_, ...), custom_call_target="tpu_custom_call" | custom-call | flops 4000000000 | tf_op jit(solution)/shard_map/pick_back/pallas_call | solution.py:98
  18.5 1.3 %collective-permute-done.3 = f32[32,1024]{1,0:T(8,128)S(1)} collective-permute-done((f32[32,1024]{1,0:T(8,128)S(1)}, f32[32,1024]{1,0:T(8,128)S(1)}, u32[]{:S(2)}, u32[]{:S(2)}) %collective-permute-start.3) | collective-permute-done | bytes 131104 | tf_op jit(solution)/shard_map/ppermute | solution.py:299
  19.8 1.6 %collective-permute-start.4 = (f32[32,1024]{1,0:T(8,128)S(1)}, f32[32,1024]{1,0:T(8,128)S(1)}, u32[]{:S(2)}, u32[]{:S(2)}) collective-permute-start(f32[32,1024]{1,0:T(8,128)S(1)} %add.40), channel_id=1, source_target_pairs={{0,2},{1,3},{2,0},{3,1},{4,6},{5,7},{6,4},{7,5},{8,10},{9,11},{10,... | collective-permute-start | bytes 393224 | tf_op jit(solution)/shard_map/ppermute | solution.py:299
  21.4 2.9 %base.1 = (f32[2048,256]{1,0:T(8,128)S(1)}, f32[2048,256]{1,0:T(8,128)S(1)}) custom-call(bf16[1024,1280]{1,0:T(8,128)(2,1)S(1)} %copy-done.1, bf16[1280,1024]{1,0:T(8,128)(2,1)S(1)} %copy-done.2), custom_call_target="tpu_custom_call" | custom-call | tf_op jit(solution)/shard_map/base/pallas_call | solution.py:98
  24.3 1.2 %collective-permute-done.4 = f32[32,1024]{1,0:T(8,128)S(1)} collective-permute-done((f32[32,1024]{1,0:T(8,128)S(1)}, f32[32,1024]{1,0:T(8,128)S(1)}, u32[]{:S(2)}, u32[]{:S(2)}) %collective-permute-start.4) | collective-permute-done | bytes 131104 | tf_op jit(solution)/shard_map/ppermute | solution.py:299
  25.6 1.2 %collective-permute-done.5.refs_0_.refs_4_.refs_8_ = bf16[32,1024]{1,0:T(8,128)(2,1)S(1)} collective-permute-done((bf16[32,1024]{1,0:T(8,128)(2,1)S(1)}, bf16[32,1024]{1,0:T(8,128)(2,1)S(1)}, u32[]{:S(2)}, u32[]{:S(2)}) %collective-permute-start.5) | collective-permute-done | bytes 65568 | tf_op jit(solution)/shard_map/ppermute | solution.py:299
  26.8 2.9 %terms.1 = (f32[256,1280]{1,0:T(8,128)S(1)}, f32[256,1280]{1,0:T(8,128)S(1)}, f32[256,1280]{1,0:T(8,128)S(1)}, f32[256,1280]{1,0:T(8,128)S(1)}) custom-call(bf16[32,1024]{1,0:T(8,128)(2,1)S(1)} %collective-permute-done.5.refs_0_.refs_4_.refs_8_, bf16[32,1024]{1,0:T(8,128)(2,1)S(1)} %multiply_convert_fusion.refs_1_.refs_3_.refs_7_, ...), custom_call_target="tpu_custom_call" | custom-call | tf_op jit(solution)/shard_map/terms/pallas_call | solution.py:98
  31.0 3.3 %collective-permute-start.8 = (bf16[128,1280]{1,0:T(8,128)(2,1)S(1)}, bf16[128,1280]{1,0:T(8,128)(2,1)S(1)}, u32[]{:S(2)}, u32[]{:S(2)}) collective-permute-start(bf16[128,1280]{1,0:T(8,128)(2,1)S(1)} %get-tuple-element.126), channel_id=1, source_target_pairs={{0,4},{8,12},{4,0},{12,8},{1,5},{9,13},{5,1},{13,9},{2,6},{10,14},... | collective-permute-start | bytes 983048 | tf_op jit(solution)/shard_map/ppermute | solution.py:294
  34.3 0.7 collective-permute-start.9
  35.5 1.6 %collective-permute-start.21 = (bf16[2048,256]{1,0:T(8,128)(2,1)S(1)}, bf16[2048,256]{1,0:T(8,128)(2,1)S(1)}, u32[]{:S(2)}, u32[]{:S(2)}) collective-permute-start(bf16[2048,256]{1,0:T(8,128)(2,1)S(1)} %pad_maximum_fusion), channel_id=1, source_target_pairs={{0,2},{1,3},{2,0},{3,1},{4,6},{5,7},{6,4},{7,5},{8,10},{9,11},{10,... | collective-permute-start | bytes 3145736 | tf_op jit(solution)/shard_map/ppermute | solution.py:299
  37.0 3.3 %collective-permute-start.13 = (bf16[128,1280]{1,0:T(8,128)(2,1)S(1)}, bf16[128,1280]{1,0:T(8,128)(2,1)S(1)}, u32[]{:S(2)}, u32[]{:S(2)}) collective-permute-start(bf16[128,1280]{1,0:T(8,128)(2,1)S(1)} %get-tuple-element.140), channel_id=1, source_target_pairs={{0,4},{8,12},{4,0},{12,8},{1,5},{9,13},{5,1},{13,9},{2,6},{10,14},... | collective-permute-start | bytes 983048 | tf_op jit(solution)/shard_map/ppermute | solution.py:294
  40.4 0.7 collective-permute-start.14
  41.3 1.5 %collective-permute-done.8.refs_1_.refs_0_.refs_2_ = bf16[128,1280]{1,0:T(8,128)(2,1)S(1)} collective-permute-done((bf16[128,1280]{1,0:T(8,128)(2,1)S(1)}, bf16[128,1280]{1,0:T(8,128)(2,1)S(1)}, u32[]{:S(2)}, u32[]{:S(2)}) %collective-permute-start.8) | collective-permute-done | bytes 327712 | tf_op jit(solution)/shard_map/ppermute | solution.py:294
  43.2 4.0 %collective-permute-start.11 = (bf16[128,1280]{1,0:T(8,128)(2,1)S(1)}, bf16[128,1280]{1,0:T(8,128)(2,1)S(1)}, u32[]{:S(2)}, u32[]{:S(2)}) collective-permute-start(bf16[128,1280]{1,0:T(8,128)(2,1)S(1)} %get-tuple-element.136), channel_id=1, source_target_pairs={{0,4},{8,12},{4,0},{12,8},{1,5},{9,13},{5,1},{13,9},{2,6},{10,14},... | collective-permute-start | bytes 983048 | tf_op jit(solution)/shard_map/ppermute | solution.py:294
  47.2 0.7 collective-permute-start.12
  47.9 2.0 %pick_1.1.refs_6_ = f32[64,1024]{1,0:T(8,128)S(1)} custom-call(bf16[256,1280]{1,0:T(8,128)(2,1)S(1)} %collective-permute-done.6.refs_1_.refs_0_, bf16[256,1280]{1,0:T(8,128)(2,1)S(1)} %collective-permute-done.7.refs_0_.refs_1_.refs_2_, s32[1,1024]{1,0:T(1,128)S(1)} %compare_select_fusion.refs_1_.refs_4_.refs_2_.refs_5_.refs_9_.refs_8_, ...), custom_call_target="tpu_custom_call" | custom-call | flops 3000000000 | tf_op jit(solution)/shard_map/pick_1/pallas_call | solution.py:98
  50.3 4.0 %collective-permute-start.15 = (bf16[128,1280]{1,0:T(8,128)(2,1)S(1)}, bf16[128,1280]{1,0:T(8,128)(2,1)S(1)}, u32[]{:S(2)}, u32[]{:S(2)}) collective-permute-start(bf16[128,1280]{1,0:T(8,128)(2,1)S(1)} %get-tuple-element.155), channel_id=1, source_target_pairs={{0,4},{8,12},{4,0},{12,8},{1,5},{9,13},{5,1},{13,9},{2,6},{10,14},... | collective-permute-start | bytes 983048 | tf_op jit(solution)/shard_map/ppermute | solution.py:294
  54.2 0.7 collective-permute-start.16
  54.9 2.9 %input_early.1.refs_5_ = f32[1024,1280]{1,0:T(8,128)S(1)} custom-call(bf16[256,1280]{1,0:T(8,128)(2,1)S(1)} %bitcast.13, bf16[256,1280]{1,0:T(8,128)(2,1)S(1)} %collective-permute-done.6.refs_1_.refs_0_, bf16[256,1280]{1,0:T(8,128)(2,1)S(1)} %collective-permute-done.7.refs_0_.refs_1_.refs_2_, ...), custom_call_target="tpu_custom_call" | custom-call | tf_op jit(solution)/shard_map/input_early/pallas_call | solution.py:98
  58.2 3.0 %collective-permute-start.17 = (bf16[128,1280]{1,0:T(8,128)(2,1)S(1)}, bf16[128,1280]{1,0:T(8,128)(2,1)S(1)}, u32[]{:S(2)}, u32[]{:S(2)}) collective-permute-start(bf16[128,1280]{1,0:T(8,128)(2,1)S(1)} %get-tuple-element.171), channel_id=1, source_target_pairs={{0,4},{8,12},{4,0},{12,8},{1,5},{9,13},{5,1},{13,9},{2,6},{10,14},... | collective-permute-start | bytes 983048 | tf_op jit(solution)/shard_map/ppermute | solution.py:294
  61.3 0.7 collective-permute-start.18
  61.9 1.3 %pick_2.1.refs_4_ = f32[64,1024]{1,0:T(8,128)S(1)} custom-call(bf16[128,1280]{1,0:T(8,128)(2,1)S(1)} %collective-permute-done.8.refs_1_.refs_0_.refs_2_, bf16[128,1280]{1,0:T(8,128)(2,1)S(1)} %collective-permute-done.13.refs_1_.refs_3_, bf16[128,1280]{1,0:T(8,128)(2,1)S(1)} %collective-permute-done.9.refs_0_.refs_2_.refs_4_, ...), custom_call_target="tpu_custom_call" | custom-call | flops 3000000000 | tf_op jit(solution)/shard_map/pick_2/pallas_call | solution.py:98
  64.3 4.0 %collective-permute-start.23 = (bf16[128,1280]{1,0:T(8,128)(2,1)S(1)}, bf16[128,1280]{1,0:T(8,128)(2,1)S(1)}, u32[]{:S(2)}, u32[]{:S(2)}) collective-permute-start(bf16[128,1280]{1,0:T(8,128)(2,1)S(1)} %get-tuple-element.180), channel_id=1, source_target_pairs={{0,4},{8,12},{4,0},{12,8},{1,5},{9,13},{5,1},{13,9},{2,6},{10,14},... | collective-permute-start | bytes 983048 | tf_op jit(solution)/shard_map/ppermute | solution.py:294
  69.0 1.1 %pick_3.1 = (f32[32,1024]{1,0:T(8,128)S(1)}, f32[32,1024]{1,0:T(8,128)S(1)}) custom-call(bf16[128,1280]{1,0:T(8,128)(2,1)S(1)} %collective-permute-done.11.refs_1_.refs_0_, bf16[128,1280]{1,0:T(8,128)(2,1)S(1)} %collective-permute-done.15.refs_1_, s32[1,1024]{1,0:T(1,128)S(1)} %compare_select_fusion.refs_1_.refs_4_.refs_2_.refs_5_.refs_9_.refs_8_, ...), custom_call_target="tpu_custom_call" | custom-call | tf_op jit(solution)/shard_map/pick_3/pallas_call | solution.py:98
  70.1 0.8 collective-permute-done.17.refs_0_
  71.0 1.3 %collective-permute-done.19 = f32[32,1024]{1,0:T(8,128)S(1)} collective-permute-done((f32[32,1024]{1,0:T(8,128)S(1)}, f32[32,1024]{1,0:T(8,128)S(1)}, u32[]{:S(2)}, u32[]{:S(2)}) %collective-permute-start.19) | collective-permute-done | bytes 131104 | tf_op jit(solution)/shard_map/ppermute | solution.py:299
  72.3 1.5 %collective-permute-start.22 = (f32[32,1024]{1,0:T(8,128)S(1)}, f32[32,1024]{1,0:T(8,128)S(1)}, u32[]{:S(2)}, u32[]{:S(2)}) collective-permute-start(f32[32,1024]{1,0:T(8,128)S(1)} %add.43), channel_id=1, source_target_pairs={{0,2},{1,3},{2,0},{3,1},{4,6},{5,7},{6,4},{7,5},{8,10},{9,11},{10,... | collective-permute-start | bytes 393224 | tf_op jit(solution)/shard_map/ppermute | solution.py:299
  73.8 3.2 %base_back.1.refs_6_ = f32[1024,1280]{1,0:T(8,128)S(1)} custom-call(bf16[1024,256]{1,0:T(8,128)(2,1)S(1)} %copy-done.3, bf16[1024,256]{1,0:T(8,128)(2,1)S(1)} %collective-permute-done.20.refs_1_, bf16[1024,256]{1,0:T(8,128)(2,1)S(1)} %get-tuple-element.184.refs_2_, bf16[1024,256]{1,0:T(8,128)(2,1)S(1)} %get-tuple-element.185.refs_3_, ...), custom_call_target="tpu_custom_call" | custom-call | tf_op jit(solution)/shard_map/base_back/pallas_call | solution.py:98
  77.1 0.8 collective-permute-done.22
  78.0 1.6 %collective-permute-start.26 = (bf16[1024,256]{1,0:T(8,128)(2,1)S(1)}, bf16[1024,256]{1,0:T(8,128)(2,1)S(1)}, u32[]{:S(2)}, u32[]{:S(2)}) collective-permute-start(bf16[1024,256]{1,0:T(8,128)(2,1)S(1)} %slice.21), channel_id=1, source_target_pairs={{0,2},{1,3},{2,0},{3,1},{4,6},{5,7},{6,4},{7,5},{8,10},{9,11},{10,... | collective-permute-start | bytes 1572872 | tf_op jit(solution)/shard_map/ppermute | solution.py:299
  79.6 1.3 %collective-permute-done.25.refs_0_.refs_7_ = bf16[32,1024]{1,0:T(8,128)(2,1)S(1)} collective-permute-done((bf16[32,1024]{1,0:T(8,128)(2,1)S(1)}, bf16[32,1024]{1,0:T(8,128)(2,1)S(1)}, u32[]{:S(2)}, u32[]{:S(2)}) %collective-permute-start.25) | collective-permute-done | bytes 65568 | tf_op jit(solution)/shard_map/ppermute | solution.py:299
  80.8 0.8 up_terms.1
  81.6 4.0 %collective-permute-start.27 = (bf16[256,256]{1,0:T(8,128)(2,1)S(1)}, bf16[256,256]{1,0:T(8,128)(2,1)S(1)}, u32[]{:S(2)}, u32[]{:S(2)}) collective-permute-start(bf16[256,256]{1,0:T(8,128)(2,1)S(1)} %get-tuple-element.198), channel_id=1, source_target_pairs={{0,4},{4,8},{8,12},{12,0},{1,5},{5,9},{9,13},{13,1},{2,6},{6,10},{... | collective-permute-start | bytes 393224 | tf_op jit(solution)/shard_map/ppermute | solution.py:294
  85.6 0.9 collective-permute-start.28
  86.5 2.8 %collective-permute-start.29 = (bf16[256,256]{1,0:T(8,128)(2,1)S(1)}, bf16[256,256]{1,0:T(8,128)(2,1)S(1)}, u32[]{:S(2)}, u32[]{:S(2)}) collective-permute-start(bf16[256,256]{1,0:T(8,128)(2,1)S(1)} %get-tuple-element.200), channel_id=1, source_target_pairs={{0,12},{4,0},{8,4},{12,8},{1,13},{5,1},{9,5},{13,9},{2,14},{6,2},{... | collective-permute-start | bytes 393224 | tf_op jit(solution)/shard_map/ppermute | solution.py:294
  89.4 1.7 %grad_down.1 = f32[256,1280]{1,0:T(8,128)} custom-call(bf16[128,1280]{1,0:T(8,128)(2,1)S(1)} %collective-permute-done.17.refs_0_, bf16[128,1280]{1,0:T(8,128)(2,1)S(1)} %collective-permute-done.23.refs_1_, bf16[128,1280]{1,0:T(8,128)(2,1)S(1)} %collective-permute-done.18.refs_2_, bf16[128,1280]{1,0:T(8,128)(2,1)S(1)} %collective-permute-done.24.refs_3_, ...), custom_call_target="tpu_custom_call" | custom-call | tf_op jit(solution)/shard_map/grad_down/pallas_call | solution.py:98
  91.1 3.5 %input_grad.1 = bf16[1024,1280]{1,0:T(8,128)(2,1)} custom-call(bf16[128,1280]{1,0:T(8,128)(2,1)S(1)} %collective-permute-done.11.refs_1_.refs_0_, bf16[128,1280]{1,0:T(8,128)(2,1)S(1)} %collective-permute-done.15.refs_1_, bf16[128,1280]{1,0:T(8,128)(2,1)S(1)} %collective-permute-done.8.refs_1_.refs_0_.refs_2_, ...), custom_call_target="tpu_custom_call" | custom-call | tf_op jit(solution)/shard_map/input_grad/pallas_call | solution.py:98
  94.7 2.3 %projected.1 = bf16[1024,256]{1,0:T(8,128)(2,1)} custom-call(bf16[256,256]{1,0:T(8,128)(2,1)S(1)} %bitcast.18, bf16[256,256]{1,0:T(8,128)(2,1)S(1)} %collective-permute-done.refs_1_, bf16[256,256]{1,0:T(8,128)(2,1)S(1)} %collective-permute-done.1.refs_2_, bf16[256,256]{1,0:T(8,128)(2,1)S(1)} %collective-permute-done.2.refs_3_, ...), custom_call_target="tpu_custom_call" | custom-call | tf_op jit(solution)/shard_map/projected/pallas_call | solution.py:98
  97.0 0.8 convert_add_fusion
  (56 shorter events, 5.2 us)
Async XLA Ops:
  0.6 11.9 %collective-permute-start = (bf16[256,256]{1,0:T(8,128)(2,1)}, bf16[256,256]{1,0:T(8,128)(2,1)S(1)}, u32[]{:S(2)}, u32[]{:S(2)}) collective-permute-start(bf16[256,256]{1,0:T(8,128)(2,1)} %bitcast.14), channel_id=1, source_target_pairs={{4,0},{0,4},{12,8},{8,12},{5,1},{1,5},{13,9},{9,13},{6,2},{2,6},{1... | collective-permute-start | bytes 393224 | tf_op jit(solution)/shard_map/ppermute | solution.py:294
  3.7 13.2 %collective-permute-start.1 = (bf16[256,256]{1,0:T(8,128)(2,1)}, bf16[256,256]{1,0:T(8,128)(2,1)S(1)}, u32[]{:S(2)}, u32[]{:S(2)}) collective-permute-start(bf16[256,256]{1,0:T(8,128)(2,1)} %bitcast.15), channel_id=1, source_target_pairs={{8,0},{12,4},{0,8},{4,12},{9,1},{13,5},{1,9},{5,13},{10,2},{14,6},... | collective-permute-start | bytes 393224 | tf_op jit(solution)/shard_map/ppermute | solution.py:294
  6.3 10.6 %collective-permute-start.2 = (bf16[256,256]{1,0:T(8,128)(2,1)}, bf16[256,256]{1,0:T(8,128)(2,1)S(1)}, u32[]{:S(2)}, u32[]{:S(2)}) collective-permute-start(bf16[256,256]{1,0:T(8,128)(2,1)} %bitcast.16), channel_id=1, source_target_pairs={{12,0},{8,4},{4,8},{0,12},{13,1},{9,5},{5,9},{1,13},{14,2},{10,6},... | collective-permute-start | bytes 393224 | tf_op jit(solution)/shard_map/ppermute | solution.py:294
  6.3 23.5 %collective-permute-start.6 = (bf16[256,1280]{1,0:T(8,128)(2,1)}, bf16[256,1280]{1,0:T(8,128)(2,1)S(1)}, u32[]{:S(2)}, u32[]{:S(2)}) collective-permute-start(bf16[256,1280]{1,0:T(8,128)(2,1)} %bitcast.10), channel_id=1, source_target_pairs={{0,4},{8,12},{4,0},{12,8},{1,5},{9,13},{5,1},{13,9},{2,6},{10,14},... | collective-permute-start | bytes 1966088 | tf_op jit(solution)/shard_map/ppermute | solution.py:294
  7.2 22.6 %collective-permute-start.7 = (bf16[256,1280]{1,0:T(8,128)(2,1)}, bf16[256,1280]{1,0:T(8,128)(2,1)S(1)}, u32[]{:S(2)}, u32[]{:S(2)}) collective-permute-start(bf16[256,1280]{1,0:T(8,128)(2,1)} %bitcast.11), channel_id=1, source_target_pairs={{4,8},{8,4},{5,9},{9,5},{6,10},{10,6},{7,11},{11,7},{20,24},{24,20... | collective-permute-start | bytes 1966088 | tf_op jit(solution)/shard_map/ppermute | solution.py:294
  8.6 1.7 %copy-start = (bf16[1024,1280]{1,0:T(8,128)(2,1)S(1)}, bf16[1024,1280]{1,0:T(8,128)(2,1)}, u32[]{:S(2)}) copy-start(bf16[1024,1280]{1,0:T(8,128)(2,1)} %refs_3_.5) | copy-start | bytes 7864324
  10.3 1.1 %copy-start.4 = (bf16[4,1280,64]{1,2,0:T(8,128)(2,1)S(1)}, bf16[4,1280,64]{1,2,0:T(8,128)(2,1)}, u32[]{:S(2)}) copy-start(bf16[4,1280,64]{1,2,0:T(8,128)(2,1)} %param.9) | copy-start | bytes 1966084
  11.4 5.4 %copy-start.3 = (bf16[1024,256]{1,0:T(8,128)(2,1)S(1)}, bf16[1024,256]{1,0:T(8,128)(2,1)}, u32[]{:S(2)}) copy-start(bf16[1024,256]{1,0:T(8,128)(2,1)} %refs_3_.6) | copy-start | bytes 1572868
  11.4 5.4 %copy-start.6 = (bf16[4,64,256]{2,1,0:T(8,128)(2,1)S(1)}, bf16[4,64,256]{2,1,0:T(8,128)(2,1)}, u32[]{:S(2)}) copy-start(bf16[4,64,256]{2,1,0:T(8,128)(2,1)} %param.10) | copy-start | bytes 393220
  16.9 4.5 %copy-start.1 = (bf16[1024,1280]{1,0:T(8,128)(2,1)S(1)}, bf16[1024,1280]{1,0:T(8,128)(2,1)}, u32[]{:S(2)}) copy-start(bf16[1024,1280]{1,0:T(8,128)(2,1)} %refs_3_.5) | copy-start | bytes 7864324
  16.9 4.5 %copy-start.2 = (bf16[1280,1024]{1,0:T(8,128)(2,1)S(1)}, bf16[1280,1024]{1,0:T(8,128)(2,1)}, u32[]{:S(2)}) copy-start(bf16[1280,1024]{1,0:T(8,128)(2,1)} %refs_4_.1) | copy-start | bytes 7864324
  18.4 1.4 %collective-permute-start.3 = (f32[32,1024]{1,0:T(8,128)S(1)}, f32[32,1024]{1,0:T(8,128)S(1)}, u32[]{:S(2)}, u32[]{:S(2)}) collective-permute-start(f32[32,1024]{1,0:T(8,128)S(1)} %get-tuple-element.109), channel_id=1, source_target_pairs={{0,1},{1,0},{2,3},{3,2},{4,5},{5,4},{6,7},{7,6},{8,9},{9,8},{10,11... | collective-permute-start | bytes 393224 | tf_op jit(solution)/shard_map/ppermute | solution.py:299
  19.8 5.6 %collective-permute-start.4 = (f32[32,1024]{1,0:T(8,128)S(1)}, f32[32,1024]{1,0:T(8,128)S(1)}, u32[]{:S(2)}, u32[]{:S(2)}) collective-permute-start(f32[32,1024]{1,0:T(8,128)S(1)} %add.40), channel_id=1, source_target_pairs={{0,2},{1,3},{2,0},{3,1},{4,6},{5,7},{6,4},{7,5},{8,10},{9,11},{10,... | collective-permute-start | bytes 393224 | tf_op jit(solution)/shard_map/ppermute | solution.py:299
  25.5 1.3 %collective-permute-start.5 = (bf16[32,1024]{1,0:T(8,128)(2,1)S(1)}, bf16[32,1024]{1,0:T(8,128)(2,1)S(1)}, u32[]{:S(2)}, u32[]{:S(2)}) collective-permute-start(bf16[32,1024]{1,0:T(8,128)(2,1)S(1)} %multiply_convert_fusion.refs_1_.refs_3_.refs_7_), channel_id=1, source_target_pairs={{0,1},{1,0},{2,3},{3,2},{4,5},{5,4},{6,7},{7,6},{8,9},{9,8},{10,11... | collective-permute-start | bytes 196616 | tf_op jit(solution)/shard_map/ppermute | solution.py:299
  30.4 10.0 %collective-permute-start.10 = (f32[2048,256]{1,0:T(8,128)S(1)}, f32[2048,256]{1,0:T(8,128)S(1)}, u32[]{:S(2)}, u32[]{:S(2)}) collective-permute-start(f32[2048,256]{1,0:T(8,128)S(1)} %get-tuple-element.130), channel_id=1, source_target_pairs={{0,1},{1,0},{2,3},{3,2},{4,5},{5,4},{6,7},{7,6},{8,9},{9,8},{10,11... | collective-permute-start | bytes 6291464 | tf_op jit(solution)/shard_map/ppermute | solution.py:299
  30.6 4.8 %collective-permute-start.20 = (bf16[1024,256]{1,0:T(8,128)(2,1)S(1)}, bf16[1024,256]{1,0:T(8,128)(2,1)S(1)}, u32[]{:S(2)}, u32[]{:S(2)}) collective-permute-start(bf16[1024,256]{1,0:T(8,128)(2,1)S(1)} %copy-done.3), channel_id=1, source_target_pairs={{0,1},{1,0},{2,3},{3,2},{4,5},{5,4},{6,7},{7,6},{8,9},{9,8},{10,11... | collective-permute-start | bytes 1572872 | tf_op jit(solution)/shard_map/ppermute | solution.py:299
  31.0 11.8 %collective-permute-start.8 = (bf16[128,1280]{1,0:T(8,128)(2,1)S(1)}, bf16[128,1280]{1,0:T(8,128)(2,1)S(1)}, u32[]{:S(2)}, u32[]{:S(2)}) collective-permute-start(bf16[128,1280]{1,0:T(8,128)(2,1)S(1)} %get-tuple-element.126), channel_id=1, source_target_pairs={{0,4},{8,12},{4,0},{12,8},{1,5},{9,13},{5,1},{13,9},{2,6},{10,14},... | collective-permute-start | bytes 983048 | tf_op jit(solution)/shard_map/ppermute | solution.py:294
  34.3 8.5 %collective-permute-start.9 = (bf16[128,1280]{1,0:T(8,128)(2,1)S(1)}, bf16[128,1280]{1,0:T(8,128)(2,1)S(1)}, u32[]{:S(2)}, u32[]{:S(2)}) collective-permute-start(bf16[128,1280]{1,0:T(8,128)(2,1)S(1)} %get-tuple-element.127), channel_id=1, source_target_pairs={{4,8},{8,4},{5,9},{9,5},{6,10},{10,6},{7,11},{11,7},{20,24},{24,20... | collective-permute-start | bytes 983048 | tf_op jit(solution)/shard_map/ppermute | solution.py:294
  35.5 35.5 %collective-permute-start.21 = (bf16[2048,256]{1,0:T(8,128)(2,1)S(1)}, bf16[2048,256]{1,0:T(8,128)(2,1)S(1)}, u32[]{:S(2)}, u32[]{:S(2)}) collective-permute-start(bf16[2048,256]{1,0:T(8,128)(2,1)S(1)} %pad_maximum_fusion), channel_id=1, source_target_pairs={{0,2},{1,3},{2,0},{3,1},{4,6},{5,7},{6,4},{7,5},{8,10},{9,11},{10,... | collective-permute-start | bytes 3145736 | tf_op jit(solution)/shard_map/ppermute | solution.py:299
  37.0 12.9 %collective-permute-start.13 = (bf16[128,1280]{1,0:T(8,128)(2,1)S(1)}, bf16[128,1280]{1,0:T(8,128)(2,1)S(1)}, u32[]{:S(2)}, u32[]{:S(2)}) collective-permute-start(bf16[128,1280]{1,0:T(8,128)(2,1)S(1)} %get-tuple-element.140), channel_id=1, source_target_pairs={{0,4},{8,12},{4,0},{12,8},{1,5},{9,13},{5,1},{13,9},{2,6},{10,14},... | collective-permute-start | bytes 983048 | tf_op jit(solution)/shard_map/ppermute | solution.py:294
  40.4 9.5 %collective-permute-start.14 = (bf16[128,1280]{1,0:T(8,128)(2,1)S(1)}, bf16[128,1280]{1,0:T(8,128)(2,1)S(1)}, u32[]{:S(2)}, u32[]{:S(2)}) collective-permute-start(bf16[128,1280]{1,0:T(8,128)(2,1)S(1)} %get-tuple-element.141), channel_id=1, source_target_pairs={{4,8},{8,4},{5,9},{9,5},{6,10},{10,6},{7,11},{11,7},{20,24},{24,20... | collective-permute-start | bytes 983048 | tf_op jit(solution)/shard_map/ppermute | solution.py:294
  43.2 14.6 %collective-permute-start.11 = (bf16[128,1280]{1,0:T(8,128)(2,1)S(1)}, bf16[128,1280]{1,0:T(8,128)(2,1)S(1)}, u32[]{:S(2)}, u32[]{:S(2)}) collective-permute-start(bf16[128,1280]{1,0:T(8,128)(2,1)S(1)} %get-tuple-element.136), channel_id=1, source_target_pairs={{0,4},{8,12},{4,0},{12,8},{1,5},{9,13},{5,1},{13,9},{2,6},{10,14},... | collective-permute-start | bytes 983048 | tf_op jit(solution)/shard_map/ppermute | solution.py:294
  47.2 10.6 %collective-permute-start.12 = (bf16[128,1280]{1,0:T(8,128)(2,1)S(1)}, bf16[128,1280]{1,0:T(8,128)(2,1)S(1)}, u32[]{:S(2)}, u32[]{:S(2)}) collective-permute-start(bf16[128,1280]{1,0:T(8,128)(2,1)S(1)} %get-tuple-element.137), channel_id=1, source_target_pairs={{4,8},{8,4},{5,9},{9,5},{6,10},{10,6},{7,11},{11,7},{20,24},{24,20... | collective-permute-start | bytes 983048 | tf_op jit(solution)/shard_map/ppermute | solution.py:294
  49.9 5.0 %copy-start.5 = (bf16[4,1280,64]{1,2,0:T(8,128)(2,1)S(1)}, bf16[4,1280,64]{1,2,0:T(8,128)(2,1)}, u32[]{:S(2)}) copy-start(bf16[4,1280,64]{1,2,0:T(8,128)(2,1)} %param.9) | copy-start | bytes 1966084
  50.3 13.6 %collective-permute-start.15 = (bf16[128,1280]{1,0:T(8,128)(2,1)S(1)}, bf16[128,1280]{1,0:T(8,128)(2,1)S(1)}, u32[]{:S(2)}, u32[]{:S(2)}) collective-permute-start(bf16[128,1280]{1,0:T(8,128)(2,1)S(1)} %get-tuple-element.155), channel_id=1, source_target_pairs={{0,4},{8,12},{4,0},{12,8},{1,5},{9,13},{5,1},{13,9},{2,6},{10,14},... | collective-permute-start | bytes 983048 | tf_op jit(solution)/shard_map/ppermute | solution.py:294
  54.2 9.7 %collective-permute-start.16 = (bf16[128,1280]{1,0:T(8,128)(2,1)S(1)}, bf16[128,1280]{1,0:T(8,128)(2,1)S(1)}, u32[]{:S(2)}, u32[]{:S(2)}) collective-permute-start(bf16[128,1280]{1,0:T(8,128)(2,1)S(1)} %get-tuple-element.156), channel_id=1, source_target_pairs={{4,8},{8,4},{5,9},{9,5},{6,10},{10,6},{7,11},{11,7},{20,24},{24,20... | collective-permute-start | bytes 983048 | tf_op jit(solution)/shard_map/ppermute | solution.py:294
  58.2 12.7 %collective-permute-start.17 = (bf16[128,1280]{1,0:T(8,128)(2,1)S(1)}, bf16[128,1280]{1,0:T(8,128)(2,1)S(1)}, u32[]{:S(2)}, u32[]{:S(2)}) collective-permute-start(bf16[128,1280]{1,0:T(8,128)(2,1)S(1)} %get-tuple-element.171), channel_id=1, source_target_pairs={{0,4},{8,12},{4,0},{12,8},{1,5},{9,13},{5,1},{13,9},{2,6},{10,14},... | collective-permute-start | bytes 983048 | tf_op jit(solution)/shard_map/ppermute | solution.py:294
  61.3 9.6 %collective-permute-start.18 = (bf16[128,1280]{1,0:T(8,128)(2,1)S(1)}, bf16[128,1280]{1,0:T(8,128)(2,1)S(1)}, u32[]{:S(2)}, u32[]{:S(2)}) collective-permute-start(bf16[128,1280]{1,0:T(8,128)(2,1)S(1)} %get-tuple-element.172), channel_id=1, source_target_pairs={{4,8},{8,4},{5,9},{9,5},{6,10},{10,6},{7,11},{11,7},{20,24},{24,20... | collective-permute-start | bytes 983048 | tf_op jit(solution)/shard_map/ppermute | solution.py:294
  64.3 13.6 %collective-permute-start.23 = (bf16[128,1280]{1,0:T(8,128)(2,1)S(1)}, bf16[128,1280]{1,0:T(8,128)(2,1)S(1)}, u32[]{:S(2)}, u32[]{:S(2)}) collective-permute-start(bf16[128,1280]{1,0:T(8,128)(2,1)S(1)} %get-tuple-element.180), channel_id=1, source_target_pairs={{0,4},{8,12},{4,0},{12,8},{1,5},{9,13},{5,1},{13,9},{2,6},{10,14},... | collective-permute-start | bytes 983048 | tf_op jit(solution)/shard_map/ppermute | solution.py:294
  68.3 9.6 %collective-permute-start.24 = (bf16[128,1280]{1,0:T(8,128)(2,1)S(1)}, bf16[128,1280]{1,0:T(8,128)(2,1)S(1)}, u32[]{:S(2)}, u32[]{:S(2)}) collective-permute-start(bf16[128,1280]{1,0:T(8,128)(2,1)S(1)} %get-tuple-element.181), channel_id=1, source_target_pairs={{4,8},{8,4},{5,9},{9,5},{6,10},{10,6},{7,11},{11,7},{20,24},{24,20... | collective-permute-start | bytes 983048 | tf_op jit(solution)/shard_map/ppermute | solution.py:294
  70.9 1.3 %collective-permute-start.19 = (f32[32,1024]{1,0:T(8,128)S(1)}, f32[32,1024]{1,0:T(8,128)S(1)}, u32[]{:S(2)}, u32[]{:S(2)}) collective-permute-start(f32[32,1024]{1,0:T(8,128)S(1)} %get-tuple-element.175), channel_id=1, source_target_pairs={{0,1},{1,0},{2,3},{3,2},{4,5},{5,4},{6,7},{7,6},{8,9},{9,8},{10,11... | collective-permute-start | bytes 393224 | tf_op jit(solution)/shard_map/ppermute | solution.py:299
  72.3 5.6 %collective-permute-start.22 = (f32[32,1024]{1,0:T(8,128)S(1)}, f32[32,1024]{1,0:T(8,128)S(1)}, u32[]{:S(2)}, u32[]{:S(2)}) collective-permute-start(f32[32,1024]{1,0:T(8,128)S(1)} %add.43), channel_id=1, source_target_pairs={{0,2},{1,3},{2,0},{3,1},{4,6},{5,7},{6,4},{7,5},{8,10},{9,11},{10,... | collective-permute-start | bytes 393224 | tf_op jit(solution)/shard_map/ppermute | solution.py:299
  78.0 16.7 %collective-permute-start.26 = (bf16[1024,256]{1,0:T(8,128)(2,1)S(1)}, bf16[1024,256]{1,0:T(8,128)(2,1)S(1)}, u32[]{:S(2)}, u32[]{:S(2)}) collective-permute-start(bf16[1024,256]{1,0:T(8,128)(2,1)S(1)} %slice.21), channel_id=1, source_target_pairs={{0,2},{1,3},{2,0},{3,1},{4,6},{5,7},{6,4},{7,5},{8,10},{9,11},{10,... | collective-permute-start | bytes 1572872 | tf_op jit(solution)/shard_map/ppermute | solution.py:299
  79.5 1.3 %collective-permute-start.25 = (bf16[32,1024]{1,0:T(8,128)(2,1)S(1)}, bf16[32,1024]{1,0:T(8,128)(2,1)S(1)}, u32[]{:S(2)}, u32[]{:S(2)}) collective-permute-start(bf16[32,1024]{1,0:T(8,128)(2,1)S(1)} %add.44.refs_1_.refs_6_), channel_id=1, source_target_pairs={{0,1},{1,0},{2,3},{3,2},{4,5},{5,4},{6,7},{7,6},{8,9},{9,8},{10,11... | collective-permute-start | bytes 196616 | tf_op jit(solution)/shard_map/ppermute | solution.py:299
  81.6 15.4 %collective-permute-start.27 = (bf16[256,256]{1,0:T(8,128)(2,1)S(1)}, bf16[256,256]{1,0:T(8,128)(2,1)S(1)}, u32[]{:S(2)}, u32[]{:S(2)}) collective-permute-start(bf16[256,256]{1,0:T(8,128)(2,1)S(1)} %get-tuple-element.198), channel_id=1, source_target_pairs={{0,4},{4,8},{8,12},{12,0},{1,5},{5,9},{9,13},{13,1},{2,6},{6,10},{... | collective-permute-start | bytes 393224 | tf_op jit(solution)/shard_map/ppermute | solution.py:294
  85.6 11.4 %collective-permute-start.28 = (bf16[256,256]{1,0:T(8,128)(2,1)S(1)}, bf16[256,256]{1,0:T(8,128)(2,1)S(1)}, u32[]{:S(2)}, u32[]{:S(2)}) collective-permute-start(bf16[256,256]{1,0:T(8,128)(2,1)S(1)} %get-tuple-element.199), channel_id=1, source_target_pairs={{0,8},{4,12},{8,0},{12,4},{1,9},{5,13},{9,1},{13,5},{2,10},{6,14},... | collective-permute-start | bytes 393224 | tf_op jit(solution)/shard_map/ppermute | solution.py:294
  86.5 10.5 %collective-permute-start.29 = (bf16[256,256]{1,0:T(8,128)(2,1)S(1)}, bf16[256,256]{1,0:T(8,128)(2,1)S(1)}, u32[]{:S(2)}, u32[]{:S(2)}) collective-permute-start(bf16[256,256]{1,0:T(8,128)(2,1)S(1)} %get-tuple-element.200), channel_id=1, source_target_pairs={{0,12},{4,0},{8,4},{12,8},{1,13},{5,1},{9,5},{13,9},{2,14},{6,2},{... | collective-permute-start | bytes 393224 | tf_op jit(solution)/shard_map/ppermute | solution.py:294

commit v5 on v4

--- a/solution.py
+++ b/solution.py
@@ -400,9 +400,10 @@
         *back, ADAPTER_SCALE, core=(x,), during=base_products
     )
 
-    offsets = [fixed(0)] + [by_side(owners - s, s) for s in range(1, owners)]
-    terms = outer_terms("terms", back, places, x, offsets, [F32] * owners, per_owner, 1.0)
+    offsets = [by_side(owners - s, s) for s in range(1, owners)]
+    terms = outer_terms("terms", back, places, x, offsets, [F32] * last, per_owner, 1.0)
     *terms, got_a, got_b = tie(*terms, got_a, got_b)
+    terms = [None, *terms]
 
     half = rows // 2
     got_a, got_b, pieces = [got_a], [got_b], {}
@@ -420,7 +421,7 @@
             elif step > 2 and h == 1:
                 got_a[h], got_b[h], low = tie(got_a[h], got_b[h], low)
             if step == 2 and h == 0:
-                got_a[h], got_b[h], _ = tie(got_a[h], got_b[h], base_sum)
+                got_a[h], got_b[h], terms[0], base_sum = tie(got_a[h], got_b[h], terms[0], base_sum)
             if step == last and h == 0:
                 got_a[h], got_b[h], early = tie(got_a[h], got_b[h], early)
             outs = [((half, width_part), BF16)] * (2 * (2 // len(got_a)))
@@ -441,6 +442,9 @@
                     f"pick_{step - 1}", arrived, places, x_late, per_owner, low, flops=SLOT_FLOPS
                 )
             if step == 1:
+                (terms[0],) = outer_terms(
+                    "term_own", back, places_here, x, [fixed(0)], [F32], per_owner, 1.0
+                )
                 base_give, cot_here, _ = tie(base_give, cot, sends[0])
                 base_sum = base_keep + swap_narrow(base_give, near_bit)
                 cots = {0: cot_here, near_bit: cot_near}
@@ -515,7 +519,8 @@
         per_owner,
         ADAPTER_SCALE,
     )
-    places_late, *up_terms = tie(places, *up_terms)
+    *up_terms, places_late = tie(*up_terms[::-1], places)
+    up_terms = up_terms[::-1]
     got_up = [
         shift(term, [(d, (d + m) % owners) for d in range(owners)])
         for m, term in enumerate(up_terms, 1)

time: 98.2 us -> 98.1 us (level)
  waiting for transfers between devices: 14.8 us -> 13.5 us
    pallas_call x18 -> x19, Pallas kernels: 29.3 us -> 29.6 us  [local_kernel(): pl.pallas_call(fetching if late else kernel, name=name, out_shape=[jax.Sh...]
  transfers between devices with their start and end apart: 30 -> 30, of which waited for: 11 -> 10; matrix products, arithmetic and copies ran while one was open for 1% -> 1% of each run, Pallas kernels for 29% -> 30%
where the time goes in v5:
time: 98.1 us; the launch traced here: 97.7 us
  starting transfers between devices  48.6 us (50%)
  Pallas kernels  29.6 us (30%)
  waiting for transfers between devices  13.5 us (14%)
  local copies, waits for them, and re-layouts  3.04 us (3%)
  other arithmetic  1.89 us (2%)
  between operations  1.08 us (1%)
    ppermute x20, starting transfers between devices, shift(): return lax.ppermute(value, 'wide', pairs) if pairs else None  41.7 us
    pallas_call x19, Pallas kernels, local_kernel(): pl.pallas_call(fetching if late else kernel, name=name, out_shape=[jax.Sh...  29.6 us
    ppermute x10, waiting for transfers between devices, swap_narrow(): return lax.ppermute(value, 'narrow', [(d, d ^ bit) for d in range(size)])  7.1 us
    ppermute x10, starting transfers between devices, swap_narrow(): return lax.ppermute(value, 'narrow', [(d, d ^ bit) for d in range(size)])  6.95 us
    ppermute x20, waiting for transfers between devices, shift(): return lax.ppermute(value, 'wide', pairs) if pairs else None  6.42 us
    unnamed x14, local copies, waits for them, and re-layouts  2.85 us
  transfers between devices with their start and end apart: 30, of which 10 were waited for; matrix products, arithmetic and copies ran while one was open for 1% of the time, Pallas kernels for 30%

profile of v5, /device:TPU:0, one launch (start us, length us, event | category | flops | bytes accessed | tf_op | source)
XLA Modules:
  0.0 97.7 jit_solution(3142328193909981882)
XLA Ops:
  0.6 3.1 %collective-permute-start = (bf16[256,256]{1,0:T(8,128)(2,1)}, bf16[256,256]{1,0:T(8,128)(2,1)S(1)}, u32[]{:S(2)}, u32[]{:S(2)}) collective-permute-start(bf16[256,256]{1,0:T(8,128)(2,1)} %bitcast.14), channel_id=1, source_target_pairs={{4,0},{0,4},{12,8},{8,12},{5,1},{1,5},{13,9},{9,13},{6,2},{2,6},{1... | collective-permute-start | bytes 393224 | tf_op jit(solution)/shard_map/ppermute | solution.py:294
  3.7 2.6 %collective-permute-start.1 = (bf16[256,256]{1,0:T(8,128)(2,1)}, bf16[256,256]{1,0:T(8,128)(2,1)S(1)}, u32[]{:S(2)}, u32[]{:S(2)}) collective-permute-start(bf16[256,256]{1,0:T(8,128)(2,1)} %bitcast.15), channel_id=1, source_target_pairs={{8,0},{12,4},{0,8},{4,12},{9,1},{13,5},{1,9},{5,13},{10,2},{14,6},... | collective-permute-start | bytes 393224 | tf_op jit(solution)/shard_map/ppermute | solution.py:294
  6.3 0.9 collective-permute-start.6
  7.2 0.7 collective-permute-start.7
  7.9 0.7 compare_select_fusion.refs_1_.refs_4_.refs_2_.refs_5_.refs_9_.refs_8_
  8.6 1.7 %copy-done = bf16[1024,1280]{1,0:T(8,128)(2,1)S(1)} copy-done((bf16[1024,1280]{1,0:T(8,128)(2,1)S(1)}, bf16[1024,1280]{1,0:T(8,128)(2,1)}, u32[]{:S(2)}) %copy-start) | copy-done | bytes 2621464
  10.4 1.1 %copy-done.4 = bf16[4,1280,64]{1,2,0:T(8,128)(2,1)S(1)} copy-done((bf16[4,1280,64]{1,2,0:T(8,128)(2,1)S(1)}, bf16[4,1280,64]{1,2,0:T(8,128)(2,1)}, u32[]{:S(2)}) %copy-start.4) | copy-done | bytes 655384
  11.4 1.1 %pick_own.1.refs_4_ = f32[64,1024]{1,0:T(8,128)S(1)} custom-call(bf16[256,1280]{1,0:T(8,128)(2,1)S(1)} %bitcast.12, s32[1,1024]{1,0:T(1,128)S(1)} %compare_select_fusion.refs_1_.refs_4_.refs_2_.refs_5_.refs_9_.refs_8_, bf16[1024,1280]{1,0:T(8,128)(2,1)S(1)} %copy-done), custom_call_target="tpu_custom_call" | custom-call | flops 2000000000 | tf_op jit(solution)/shard_map/pick_own/pallas_call | solution.py:98
  12.5 4.3 %collective-permute-done.1.refs_2_ = bf16[256,256]{1,0:T(8,128)(2,1)S(1)} collective-permute-done((bf16[256,256]{1,0:T(8,128)(2,1)}, bf16[256,256]{1,0:T(8,128)(2,1)S(1)}, u32[]{:S(2)}, u32[]{:S(2)}) %collective-permute-start.1) | collective-permute-done | bytes 131104 | tf_op jit(solution)/shard_map/ppermute | solution.py:294
  16.9 1.5 %pick_back.1 = (f32[32,1024]{1,0:T(8,128)S(1)}, f32[32,1024]{1,0:T(8,128)S(1)}) custom-call(bf16[256,256]{1,0:T(8,128)(2,1)S(1)} %bitcast.17, bf16[256,256]{1,0:T(8,128)(2,1)S(1)} %collective-permute-done.refs_1_, bf16[256,256]{1,0:T(8,128)(2,1)S(1)} %collective-permute-done.1.refs_2_, bf16[256,256]{1,0:T(8,128)(2,1)S(1)} %collective-permute-done.2.refs_3_, ...), custom_call_target="tpu_custom_call" | custom-call | flops 4000000000 | tf_op jit(solution)/shard_map/pick_back/pallas_call | solution.py:98
  18.5 1.3 %collective-permute-done.3 = f32[32,1024]{1,0:T(8,128)S(1)} collective-permute-done((f32[32,1024]{1,0:T(8,128)S(1)}, f32[32,1024]{1,0:T(8,128)S(1)}, u32[]{:S(2)}, u32[]{:S(2)}) %collective-permute-start.3) | collective-permute-done | bytes 131104 | tf_op jit(solution)/shard_map/ppermute | solution.py:299
  19.8 1.6 %collective-permute-start.4 = (f32[32,1024]{1,0:T(8,128)S(1)}, f32[32,1024]{1,0:T(8,128)S(1)}, u32[]{:S(2)}, u32[]{:S(2)}) collective-permute-start(f32[32,1024]{1,0:T(8,128)S(1)} %add.40), channel_id=1, source_target_pairs={{0,2},{1,3},{2,0},{3,1},{4,6},{5,7},{6,4},{7,5},{8,10},{9,11},{10,... | collective-permute-start | bytes 393224 | tf_op jit(solution)/shard_map/ppermute | solution.py:299
  21.4 2.9 %base.1 = (f32[2048,256]{1,0:T(8,128)S(1)}, f32[2048,256]{1,0:T(8,128)S(1)}) custom-call(bf16[1024,1280]{1,0:T(8,128)(2,1)S(1)} %copy-done.1, bf16[1280,1024]{1,0:T(8,128)(2,1)S(1)} %copy-done.2), custom_call_target="tpu_custom_call" | custom-call | tf_op jit(solution)/shard_map/base/pallas_call | solution.py:98
  24.3 1.2 %collective-permute-done.4 = f32[32,1024]{1,0:T(8,128)S(1)} collective-permute-done((f32[32,1024]{1,0:T(8,128)S(1)}, f32[32,1024]{1,0:T(8,128)S(1)}, u32[]{:S(2)}, u32[]{:S(2)}) %collective-permute-start.4) | collective-permute-done | bytes 131104 | tf_op jit(solution)/shard_map/ppermute | solution.py:299
  25.6 1.2 %collective-permute-done.5.refs_0_.refs_4_.refs_8_ = bf16[32,1024]{1,0:T(8,128)(2,1)S(1)} collective-permute-done((bf16[32,1024]{1,0:T(8,128)(2,1)S(1)}, bf16[32,1024]{1,0:T(8,128)(2,1)S(1)}, u32[]{:S(2)}, u32[]{:S(2)}) %collective-permute-start.5) | collective-permute-done | bytes 65568 | tf_op jit(solution)/shard_map/ppermute | solution.py:299
  26.8 2.3 %terms.1 = (f32[256,1280]{1,0:T(8,128)S(1)}, f32[256,1280]{1,0:T(8,128)S(1)}, f32[256,1280]{1,0:T(8,128)S(1)}) custom-call(bf16[32,1024]{1,0:T(8,128)(2,1)S(1)} %collective-permute-done.5.refs_0_.refs_4_.refs_8_, bf16[32,1024]{1,0:T(8,128)(2,1)S(1)} %multiply_convert_fusion.refs_1_.refs_3_.refs_7_, ...), custom_call_target="tpu_custom_call" | custom-call | tf_op jit(solution)/shard_map/terms/pallas_call | solution.py:98
  30.3 3.8 %collective-permute-start.8 = (bf16[128,1280]{1,0:T(8,128)(2,1)S(1)}, bf16[128,1280]{1,0:T(8,128)(2,1)S(1)}, u32[]{:S(2)}, u32[]{:S(2)}) collective-permute-start(bf16[128,1280]{1,0:T(8,128)(2,1)S(1)} %get-tuple-element.126), channel_id=1, source_target_pairs={{0,4},{8,12},{4,0},{12,8},{1,5},{9,13},{5,1},{13,9},{2,6},{10,14},... | collective-permute-start | bytes 983048 | tf_op jit(solution)/shard_map/ppermute | solution.py:294
  34.1 0.7 collective-permute-start.9
  34.8 1.6 %collective-permute-start.21 = (bf16[2048,256]{1,0:T(8,128)(2,1)S(1)}, bf16[2048,256]{1,0:T(8,128)(2,1)S(1)}, u32[]{:S(2)}, u32[]{:S(2)}) collective-permute-start(bf16[2048,256]{1,0:T(8,128)(2,1)S(1)} %pad_maximum_fusion), channel_id=1, source_target_pairs={{0,2},{1,3},{2,0},{3,1},{4,6},{5,7},{6,4},{7,5},{8,10},{9,11},{10,... | collective-permute-start | bytes 3145736 | tf_op jit(solution)/shard_map/ppermute | solution.py:299
  36.4 3.7 %collective-permute-start.13 = (bf16[128,1280]{1,0:T(8,128)(2,1)S(1)}, bf16[128,1280]{1,0:T(8,128)(2,1)S(1)}, u32[]{:S(2)}, u32[]{:S(2)}) collective-permute-start(bf16[128,1280]{1,0:T(8,128)(2,1)S(1)} %get-tuple-element.141), channel_id=1, source_target_pairs={{0,4},{8,12},{4,0},{12,8},{1,5},{9,13},{5,1},{13,9},{2,6},{10,14},... | collective-permute-start | bytes 983048 | tf_op jit(solution)/shard_map/ppermute | solution.py:294
  40.1 0.7 collective-permute-start.14
  40.8 0.9 term_own.1.refs_4_
  42.9 4.0 %collective-permute-start.11 = (bf16[128,1280]{1,0:T(8,128)(2,1)S(1)}, bf16[128,1280]{1,0:T(8,128)(2,1)S(1)}, u32[]{:S(2)}, u32[]{:S(2)}) collective-permute-start(bf16[128,1280]{1,0:T(8,128)(2,1)S(1)} %get-tuple-element.137), channel_id=1, source_target_pairs={{0,4},{8,12},{4,0},{12,8},{1,5},{9,13},{5,1},{13,9},{2,6},{10,14},... | collective-permute-start | bytes 983048 | tf_op jit(solution)/shard_map/ppermute | solution.py:294
  47.0 0.7 collective-permute-start.12
  47.6 2.0 %pick_1.1.refs_6_ = f32[64,1024]{1,0:T(8,128)S(1)} custom-call(bf16[256,1280]{1,0:T(8,128)(2,1)S(1)} %collective-permute-done.6.refs_1_.refs_0_, bf16[256,1280]{1,0:T(8,128)(2,1)S(1)} %collective-permute-done.7.refs_0_.refs_1_.refs_2_, s32[1,1024]{1,0:T(1,128)S(1)} %compare_select_fusion.refs_1_.refs_4_.refs_2_.refs_5_.refs_9_.refs_8_, ...), custom_call_target="tpu_custom_call" | custom-call | flops 3000000000 | tf_op jit(solution)/shard_map/pick_1/pallas_call | solution.py:98
  50.0 3.9 %collective-permute-start.15 = (bf16[128,1280]{1,0:T(8,128)(2,1)S(1)}, bf16[128,1280]{1,0:T(8,128)(2,1)S(1)}, u32[]{:S(2)}, u32[]{:S(2)}) collective-permute-start(bf16[128,1280]{1,0:T(8,128)(2,1)S(1)} %get-tuple-element.156), channel_id=1, source_target_pairs={{0,4},{8,12},{4,0},{12,8},{1,5},{9,13},{5,1},{13,9},{2,6},{10,14},... | collective-permute-start | bytes 983048 | tf_op jit(solution)/shard_map/ppermute | solution.py:294
  54.0 0.7 collective-permute-start.16
  54.7 2.9 %input_early.1.refs_5_ = f32[1024,1280]{1,0:T(8,128)S(1)} custom-call(bf16[256,1280]{1,0:T(8,128)(2,1)S(1)} %bitcast.13, bf16[256,1280]{1,0:T(8,128)(2,1)S(1)} %collective-permute-done.6.refs_1_.refs_0_, bf16[256,1280]{1,0:T(8,128)(2,1)S(1)} %collective-permute-done.7.refs_0_.refs_1_.refs_2_, ...), custom_call_target="tpu_custom_call" | custom-call | tf_op jit(solution)/shard_map/input_early/pallas_call | solution.py:98
  58.0 3.0 %collective-permute-start.17 = (bf16[128,1280]{1,0:T(8,128)(2,1)S(1)}, bf16[128,1280]{1,0:T(8,128)(2,1)S(1)}, u32[]{:S(2)}, u32[]{:S(2)}) collective-permute-start(bf16[128,1280]{1,0:T(8,128)(2,1)S(1)} %get-tuple-element.172), channel_id=1, source_target_pairs={{0,4},{8,12},{4,0},{12,8},{1,5},{9,13},{5,1},{13,9},{2,6},{10,14},... | collective-permute-start | bytes 983048 | tf_op jit(solution)/shard_map/ppermute | solution.py:294
  61.7 1.3 %pick_2.1.refs_4_ = f32[64,1024]{1,0:T(8,128)S(1)} custom-call(bf16[128,1280]{1,0:T(8,128)(2,1)S(1)} %collective-permute-done.8.refs_1_.refs_0_.refs_2_, bf16[128,1280]{1,0:T(8,128)(2,1)S(1)} %collective-permute-done.13.refs_1_.refs_3_, bf16[128,1280]{1,0:T(8,128)(2,1)S(1)} %collective-permute-done.9.refs_0_.refs_2_.refs_4_, ...), custom_call_target="tpu_custom_call" | custom-call | flops 3000000000 | tf_op jit(solution)/shard_map/pick_2/pallas_call | solution.py:98
  64.0 4.0 %collective-permute-start.23 = (bf16[128,1280]{1,0:T(8,128)(2,1)S(1)}, bf16[128,1280]{1,0:T(8,128)(2,1)S(1)}, u32[]{:S(2)}, u32[]{:S(2)}) collective-permute-start(bf16[128,1280]{1,0:T(8,128)(2,1)S(1)} %get-tuple-element.181), channel_id=1, source_target_pairs={{0,4},{8,12},{4,0},{12,8},{1,5},{9,13},{5,1},{13,9},{2,6},{10,14},... | collective-permute-start | bytes 983048 | tf_op jit(solution)/shard_map/ppermute | solution.py:294
  68.0 0.7 collective-permute-start.24
  68.7 1.1 %pick_3.1 = (f32[32,1024]{1,0:T(8,128)S(1)}, f32[32,1024]{1,0:T(8,128)S(1)}) custom-call(bf16[128,1280]{1,0:T(8,128)(2,1)S(1)} %collective-permute-done.11.refs_1_.refs_0_, bf16[128,1280]{1,0:T(8,128)(2,1)S(1)} %collective-permute-done.15.refs_1_, s32[1,1024]{1,0:T(1,128)S(1)} %compare_select_fusion.refs_1_.refs_4_.refs_2_.refs_5_.refs_9_.refs_8_, ...), custom_call_target="tpu_custom_call" | custom-call | tf_op jit(solution)/shard_map/pick_3/pallas_call | solution.py:98
  69.8 0.8 collective-permute-done.17.refs_0_
  70.8 1.3 %collective-permute-done.19 = f32[32,1024]{1,0:T(8,128)S(1)} collective-permute-done((f32[32,1024]{1,0:T(8,128)S(1)}, f32[32,1024]{1,0:T(8,128)S(1)}, u32[]{:S(2)}, u32[]{:S(2)}) %collective-permute-start.19) | collective-permute-done | bytes 131104 | tf_op jit(solution)/shard_map/ppermute | solution.py:299
  72.0 1.6 %collective-permute-start.22 = (f32[32,1024]{1,0:T(8,128)S(1)}, f32[32,1024]{1,0:T(8,128)S(1)}, u32[]{:S(2)}, u32[]{:S(2)}) collective-permute-start(f32[32,1024]{1,0:T(8,128)S(1)} %add.43), channel_id=1, source_target_pairs={{0,2},{1,3},{2,0},{3,1},{4,6},{5,7},{6,4},{7,5},{8,10},{9,11},{10,... | collective-permute-start | bytes 393224 | tf_op jit(solution)/shard_map/ppermute | solution.py:299
  73.6 3.2 %base_back.1.refs_6_ = f32[1024,1280]{1,0:T(8,128)S(1)} custom-call(bf16[1024,256]{1,0:T(8,128)(2,1)S(1)} %copy-done.3, bf16[1024,256]{1,0:T(8,128)(2,1)S(1)} %collective-permute-done.20.refs_1_, bf16[1024,256]{1,0:T(8,128)(2,1)S(1)} %get-tuple-element.185.refs_2_, bf16[1024,256]{1,0:T(8,128)(2,1)S(1)} %get-tuple-element.186.refs_3_, ...), custom_call_target="tpu_custom_call" | custom-call | tf_op jit(solution)/shard_map/base_back/pallas_call | solution.py:98
  76.8 0.8 collective-permute-done.22
  77.8 1.6 %collective-permute-start.26 = (bf16[1024,256]{1,0:T(8,128)(2,1)S(1)}, bf16[1024,256]{1,0:T(8,128)(2,1)S(1)}, u32[]{:S(2)}, u32[]{:S(2)}) collective-permute-start(bf16[1024,256]{1,0:T(8,128)(2,1)S(1)} %slice.21), channel_id=1, source_target_pairs={{0,2},{1,3},{2,0},{3,1},{4,6},{5,7},{6,4},{7,5},{8,10},{9,11},{10,... | collective-permute-start | bytes 1572872 | tf_op jit(solution)/shard_map/ppermute | solution.py:299
  79.3 1.3 %collective-permute-done.25.refs_0_.refs_7_ = bf16[32,1024]{1,0:T(8,128)(2,1)S(1)} collective-permute-done((bf16[32,1024]{1,0:T(8,128)(2,1)S(1)}, bf16[32,1024]{1,0:T(8,128)(2,1)S(1)}, u32[]{:S(2)}, u32[]{:S(2)}) %collective-permute-start.25) | collective-permute-done | bytes 65568 | tf_op jit(solution)/shard_map/ppermute | solution.py:299
  80.6 0.8 up_terms.1
  81.4 4.0 %collective-permute-start.27 = (bf16[256,256]{1,0:T(8,128)(2,1)S(1)}, bf16[256,256]{1,0:T(8,128)(2,1)S(1)}, u32[]{:S(2)}, u32[]{:S(2)}) collective-permute-start(bf16[256,256]{1,0:T(8,128)(2,1)S(1)} %get-tuple-element.200), channel_id=1, source_target_pairs={{0,4},{4,8},{8,12},{12,0},{1,5},{5,9},{9,13},{13,1},{2,6},{6,10},{... | collective-permute-start | bytes 393224 | tf_op jit(solution)/shard_map/ppermute | solution.py:294
  85.3 1.1 %collective-permute-start.28 = (bf16[256,256]{1,0:T(8,128)(2,1)S(1)}, bf16[256,256]{1,0:T(8,128)(2,1)S(1)}, u32[]{:S(2)}, u32[]{:S(2)}) collective-permute-start(bf16[256,256]{1,0:T(8,128)(2,1)S(1)} %get-tuple-element.201), channel_id=1, source_target_pairs={{0,8},{4,12},{8,0},{12,4},{1,9},{5,13},{9,1},{13,5},{2,10},{6,14},... | collective-permute-start | bytes 393224 | tf_op jit(solution)/shard_map/ppermute | solution.py:294
  86.5 2.8 %collective-permute-start.29 = (bf16[256,256]{1,0:T(8,128)(2,1)S(1)}, bf16[256,256]{1,0:T(8,128)(2,1)S(1)}, u32[]{:S(2)}, u32[]{:S(2)}) collective-permute-start(bf16[256,256]{1,0:T(8,128)(2,1)S(1)} %get-tuple-element.202), channel_id=1, source_target_pairs={{0,12},{4,0},{8,4},{12,8},{1,13},{5,1},{9,5},{13,9},{2,14},{6,2},{... | collective-permute-start | bytes 393224 | tf_op jit(solution)/shard_map/ppermute | solution.py:294
  89.4 1.7 %grad_down.1 = f32[256,1280]{1,0:T(8,128)} custom-call(bf16[128,1280]{1,0:T(8,128)(2,1)S(1)} %collective-permute-done.17.refs_0_, bf16[128,1280]{1,0:T(8,128)(2,1)S(1)} %collective-permute-done.23.refs_1_, bf16[128,1280]{1,0:T(8,128)(2,1)S(1)} %collective-permute-done.18.refs_2_, bf16[128,1280]{1,0:T(8,128)(2,1)S(1)} %collective-permute-done.24.refs_3_, ...), custom_call_target="tpu_custom_call" | custom-call | tf_op jit(solution)/shard_map/grad_down/pallas_call | solution.py:98
  91.1 3.5 %input_grad.1 = bf16[1024,1280]{1,0:T(8,128)(2,1)} custom-call(bf16[128,1280]{1,0:T(8,128)(2,1)S(1)} %collective-permute-done.11.refs_1_.refs_0_, bf16[128,1280]{1,0:T(8,128)(2,1)S(1)} %collective-permute-done.15.refs_1_, bf16[128,1280]{1,0:T(8,128)(2,1)S(1)} %collective-permute-done.8.refs_1_.refs_0_.refs_2_, ...), custom_call_target="tpu_custom_call" | custom-call | tf_op jit(solution)/shard_map/input_grad/pallas_call | solution.py:98
  94.6 2.3 %projected.1 = bf16[1024,256]{1,0:T(8,128)(2,1)} custom-call(bf16[256,256]{1,0:T(8,128)(2,1)S(1)} %bitcast.18, bf16[256,256]{1,0:T(8,128)(2,1)S(1)} %collective-permute-done.refs_1_, bf16[256,256]{1,0:T(8,128)(2,1)S(1)} %collective-permute-done.1.refs_2_, bf16[256,256]{1,0:T(8,128)(2,1)S(1)} %collective-permute-done.2.refs_3_, ...), custom_call_target="tpu_custom_call" | custom-call | tf_op jit(solution)/shard_map/projected/pallas_call | solution.py:98
  97.0 0.8 convert_add_fusion
  (57 shorter events, 5.4 us)
Async XLA Ops:
  0.6 11.9 %collective-permute-start = (bf16[256,256]{1,0:T(8,128)(2,1)}, bf16[256,256]{1,0:T(8,128)(2,1)S(1)}, u32[]{:S(2)}, u32[]{:S(2)}) collective-permute-start(bf16[256,256]{1,0:T(8,128)(2,1)} %bitcast.14), channel_id=1, source_target_pairs={{4,0},{0,4},{12,8},{8,12},{5,1},{1,5},{13,9},{9,13},{6,2},{2,6},{1... | collective-permute-start | bytes 393224 | tf_op jit(solution)/shard_map/ppermute | solution.py:294
  3.7 13.2 %collective-permute-start.1 = (bf16[256,256]{1,0:T(8,128)(2,1)}, bf16[256,256]{1,0:T(8,128)(2,1)S(1)}, u32[]{:S(2)}, u32[]{:S(2)}) collective-permute-start(bf16[256,256]{1,0:T(8,128)(2,1)} %bitcast.15), channel_id=1, source_target_pairs={{8,0},{12,4},{0,8},{4,12},{9,1},{13,5},{1,9},{5,13},{10,2},{14,6},... | collective-permute-start | bytes 393224 | tf_op jit(solution)/shard_map/ppermute | solution.py:294
  6.3 10.6 %collective-permute-start.2 = (bf16[256,256]{1,0:T(8,128)(2,1)}, bf16[256,256]{1,0:T(8,128)(2,1)S(1)}, u32[]{:S(2)}, u32[]{:S(2)}) collective-permute-start(bf16[256,256]{1,0:T(8,128)(2,1)} %bitcast.16), channel_id=1, source_target_pairs={{12,0},{8,4},{4,8},{0,12},{13,1},{9,5},{5,9},{1,13},{14,2},{10,6},... | collective-permute-start | bytes 393224 | tf_op jit(solution)/shard_map/ppermute | solution.py:294
  6.3 22.8 %collective-permute-start.6 = (bf16[256,1280]{1,0:T(8,128)(2,1)}, bf16[256,1280]{1,0:T(8,128)(2,1)S(1)}, u32[]{:S(2)}, u32[]{:S(2)}) collective-permute-start(bf16[256,1280]{1,0:T(8,128)(2,1)} %bitcast.10), channel_id=1, source_target_pairs={{0,4},{8,12},{4,0},{12,8},{1,5},{9,13},{5,1},{13,9},{2,6},{10,14},... | collective-permute-start | bytes 1966088 | tf_op jit(solution)/shard_map/ppermute | solution.py:294
  7.2 21.9 %collective-permute-start.7 = (bf16[256,1280]{1,0:T(8,128)(2,1)}, bf16[256,1280]{1,0:T(8,128)(2,1)S(1)}, u32[]{:S(2)}, u32[]{:S(2)}) collective-permute-start(bf16[256,1280]{1,0:T(8,128)(2,1)} %bitcast.11), channel_id=1, source_target_pairs={{4,8},{8,4},{5,9},{9,5},{6,10},{10,6},{7,11},{11,7},{20,24},{24,20... | collective-permute-start | bytes 1966088 | tf_op jit(solution)/shard_map/ppermute | solution.py:294
  8.6 1.7 %copy-start = (bf16[1024,1280]{1,0:T(8,128)(2,1)S(1)}, bf16[1024,1280]{1,0:T(8,128)(2,1)}, u32[]{:S(2)}) copy-start(bf16[1024,1280]{1,0:T(8,128)(2,1)} %refs_3_.7) | copy-start | bytes 7864324
  10.3 1.1 %copy-start.4 = (bf16[4,1280,64]{1,2,0:T(8,128)(2,1)S(1)}, bf16[4,1280,64]{1,2,0:T(8,128)(2,1)}, u32[]{:S(2)}) copy-start(bf16[4,1280,64]{1,2,0:T(8,128)(2,1)} %param.9) | copy-start | bytes 1966084
  11.4 5.4 %copy-start.3 = (bf16[1024,256]{1,0:T(8,128)(2,1)S(1)}, bf16[1024,256]{1,0:T(8,128)(2,1)}, u32[]{:S(2)}) copy-start(bf16[1024,256]{1,0:T(8,128)(2,1)} %refs_3_.8) | copy-start | bytes 1572868
  11.4 5.4 %copy-start.6 = (bf16[4,64,256]{2,1,0:T(8,128)(2,1)S(1)}, bf16[4,64,256]{2,1,0:T(8,128)(2,1)}, u32[]{:S(2)}) copy-start(bf16[4,64,256]{2,1,0:T(8,128)(2,1)} %param.10) | copy-start | bytes 393220
  16.9 4.5 %copy-start.1 = (bf16[1024,1280]{1,0:T(8,128)(2,1)S(1)}, bf16[1024,1280]{1,0:T(8,128)(2,1)}, u32[]{:S(2)}) copy-start(bf16[1024,1280]{1,0:T(8,128)(2,1)} %refs_3_.7) | copy-start | bytes 7864324
  16.9 4.5 %copy-start.2 = (bf16[1280,1024]{1,0:T(8,128)(2,1)S(1)}, bf16[1280,1024]{1,0:T(8,128)(2,1)}, u32[]{:S(2)}) copy-start(bf16[1280,1024]{1,0:T(8,128)(2,1)} %refs_4_.1) | copy-start | bytes 7864324
  18.4 1.4 %collective-permute-start.3 = (f32[32,1024]{1,0:T(8,128)S(1)}, f32[32,1024]{1,0:T(8,128)S(1)}, u32[]{:S(2)}, u32[]{:S(2)}) collective-permute-start(f32[32,1024]{1,0:T(8,128)S(1)} %get-tuple-element.110), channel_id=1, source_target_pairs={{0,1},{1,0},{2,3},{3,2},{4,5},{5,4},{6,7},{7,6},{8,9},{9,8},{10,11... | collective-permute-start | bytes 393224 | tf_op jit(solution)/shard_map/ppermute | solution.py:299
  19.8 5.6 %collective-permute-start.4 = (f32[32,1024]{1,0:T(8,128)S(1)}, f32[32,1024]{1,0:T(8,128)S(1)}, u32[]{:S(2)}, u32[]{:S(2)}) collective-permute-start(f32[32,1024]{1,0:T(8,128)S(1)} %add.40), channel_id=1, source_target_pairs={{0,2},{1,3},{2,0},{3,1},{4,6},{5,7},{6,4},{7,5},{8,10},{9,11},{10,... | collective-permute-start | bytes 393224 | tf_op jit(solution)/shard_map/ppermute | solution.py:299
  25.5 1.3 %collective-permute-start.5 = (bf16[32,1024]{1,0:T(8,128)(2,1)S(1)}, bf16[32,1024]{1,0:T(8,128)(2,1)S(1)}, u32[]{:S(2)}, u32[]{:S(2)}) collective-permute-start(bf16[32,1024]{1,0:T(8,128)(2,1)S(1)} %multiply_convert_fusion.refs_1_.refs_3_.refs_7_), channel_id=1, source_target_pairs={{0,1},{1,0},{2,3},{3,2},{4,5},{5,4},{6,7},{7,6},{8,9},{9,8},{10,11... | collective-permute-start | bytes 196616 | tf_op jit(solution)/shard_map/ppermute | solution.py:299
  29.7 10.4 %collective-permute-start.10 = (f32[2048,256]{1,0:T(8,128)S(1)}, f32[2048,256]{1,0:T(8,128)S(1)}, u32[]{:S(2)}, u32[]{:S(2)}) collective-permute-start(f32[2048,256]{1,0:T(8,128)S(1)} %get-tuple-element.131), channel_id=1, source_target_pairs={{0,1},{1,0},{2,3},{3,2},{4,5},{5,4},{6,7},{7,6},{8,9},{9,8},{10,11... | collective-permute-start | bytes 6291464 | tf_op jit(solution)/shard_map/ppermute | solution.py:299
  29.9 4.8 %collective-permute-start.20 = (bf16[1024,256]{1,0:T(8,128)(2,1)S(1)}, bf16[1024,256]{1,0:T(8,128)(2,1)S(1)}, u32[]{:S(2)}, u32[]{:S(2)}) collective-permute-start(bf16[1024,256]{1,0:T(8,128)(2,1)S(1)} %copy-done.3), channel_id=1, source_target_pairs={{0,1},{1,0},{2,3},{3,2},{4,5},{5,4},{6,7},{7,6},{8,9},{9,8},{10,11... | collective-permute-start | bytes 1572872 | tf_op jit(solution)/shard_map/ppermute | solution.py:299
  30.3 12.3 %collective-permute-start.8 = (bf16[128,1280]{1,0:T(8,128)(2,1)S(1)}, bf16[128,1280]{1,0:T(8,128)(2,1)S(1)}, u32[]{:S(2)}, u32[]{:S(2)}) collective-permute-start(bf16[128,1280]{1,0:T(8,128)(2,1)S(1)} %get-tuple-element.126), channel_id=1, source_target_pairs={{0,4},{8,12},{4,0},{12,8},{1,5},{9,13},{5,1},{13,9},{2,6},{10,14},... | collective-permute-start | bytes 983048 | tf_op jit(solution)/shard_map/ppermute | solution.py:294
  34.1 8.5 %collective-permute-start.9 = (bf16[128,1280]{1,0:T(8,128)(2,1)S(1)}, bf16[128,1280]{1,0:T(8,128)(2,1)S(1)}, u32[]{:S(2)}, u32[]{:S(2)}) collective-permute-start(bf16[128,1280]{1,0:T(8,128)(2,1)S(1)} %get-tuple-element.127), channel_id=1, source_target_pairs={{4,8},{8,4},{5,9},{9,5},{6,10},{10,6},{7,11},{11,7},{20,24},{24,20... | collective-permute-start | bytes 983048 | tf_op jit(solution)/shard_map/ppermute | solution.py:294
  34.8 35.8 %collective-permute-start.21 = (bf16[2048,256]{1,0:T(8,128)(2,1)S(1)}, bf16[2048,256]{1,0:T(8,128)(2,1)S(1)}, u32[]{:S(2)}, u32[]{:S(2)}) collective-permute-start(bf16[2048,256]{1,0:T(8,128)(2,1)S(1)} %pad_maximum_fusion), channel_id=1, source_target_pairs={{0,2},{1,3},{2,0},{3,1},{4,6},{5,7},{6,4},{7,5},{8,10},{9,11},{10,... | collective-permute-start | bytes 3145736 | tf_op jit(solution)/shard_map/ppermute | solution.py:299
  36.4 13.3 %collective-permute-start.13 = (bf16[128,1280]{1,0:T(8,128)(2,1)S(1)}, bf16[128,1280]{1,0:T(8,128)(2,1)S(1)}, u32[]{:S(2)}, u32[]{:S(2)}) collective-permute-start(bf16[128,1280]{1,0:T(8,128)(2,1)S(1)} %get-tuple-element.141), channel_id=1, source_target_pairs={{0,4},{8,12},{4,0},{12,8},{1,5},{9,13},{5,1},{13,9},{2,6},{10,14},... | collective-permute-start | bytes 983048 | tf_op jit(solution)/shard_map/ppermute | solution.py:294
  40.1 9.6 %collective-permute-start.14 = (bf16[128,1280]{1,0:T(8,128)(2,1)S(1)}, bf16[128,1280]{1,0:T(8,128)(2,1)S(1)}, u32[]{:S(2)}, u32[]{:S(2)}) collective-permute-start(bf16[128,1280]{1,0:T(8,128)(2,1)S(1)} %get-tuple-element.142), channel_id=1, source_target_pairs={{4,8},{8,4},{5,9},{9,5},{6,10},{10,6},{7,11},{11,7},{20,24},{24,20... | collective-permute-start | bytes 983048 | tf_op jit(solution)/shard_map/ppermute | solution.py:294
  42.9 14.6 %collective-permute-start.11 = (bf16[128,1280]{1,0:T(8,128)(2,1)S(1)}, bf16[128,1280]{1,0:T(8,128)(2,1)S(1)}, u32[]{:S(2)}, u32[]{:S(2)}) collective-permute-start(bf16[128,1280]{1,0:T(8,128)(2,1)S(1)} %get-tuple-element.137), channel_id=1, source_target_pairs={{0,4},{8,12},{4,0},{12,8},{1,5},{9,13},{5,1},{13,9},{2,6},{10,14},... | collective-permute-start | bytes 983048 | tf_op jit(solution)/shard_map/ppermute | solution.py:294
  47.0 10.6 %collective-permute-start.12 = (bf16[128,1280]{1,0:T(8,128)(2,1)S(1)}, bf16[128,1280]{1,0:T(8,128)(2,1)S(1)}, u32[]{:S(2)}, u32[]{:S(2)}) collective-permute-start(bf16[128,1280]{1,0:T(8,128)(2,1)S(1)} %get-tuple-element.138), channel_id=1, source_target_pairs={{4,8},{8,4},{5,9},{9,5},{6,10},{10,6},{7,11},{11,7},{20,24},{24,20... | collective-permute-start | bytes 983048 | tf_op jit(solution)/shard_map/ppermute | solution.py:294
  49.6 5.0 %copy-start.5 = (bf16[4,1280,64]{1,2,0:T(8,128)(2,1)S(1)}, bf16[4,1280,64]{1,2,0:T(8,128)(2,1)}, u32[]{:S(2)}) copy-start(bf16[4,1280,64]{1,2,0:T(8,128)(2,1)} %param.9) | copy-start | bytes 1966084
  50.0 13.6 %collective-permute-start.15 = (bf16[128,1280]{1,0:T(8,128)(2,1)S(1)}, bf16[128,1280]{1,0:T(8,128)(2,1)S(1)}, u32[]{:S(2)}, u32[]{:S(2)}) collective-permute-start(bf16[128,1280]{1,0:T(8,128)(2,1)S(1)} %get-tuple-element.156), channel_id=1, source_target_pairs={{0,4},{8,12},{4,0},{12,8},{1,5},{9,13},{5,1},{13,9},{2,6},{10,14},... | collective-permute-start | bytes 983048 | tf_op jit(solution)/shard_map/ppermute | solution.py:294
  54.0 9.7 %collective-permute-start.16 = (bf16[128,1280]{1,0:T(8,128)(2,1)S(1)}, bf16[128,1280]{1,0:T(8,128)(2,1)S(1)}, u32[]{:S(2)}, u32[]{:S(2)}) collective-permute-start(bf16[128,1280]{1,0:T(8,128)(2,1)S(1)} %get-tuple-element.157), channel_id=1, source_target_pairs={{4,8},{8,4},{5,9},{9,5},{6,10},{10,6},{7,11},{11,7},{20,24},{24,20... | collective-permute-start | bytes 983048 | tf_op jit(solution)/shard_map/ppermute | solution.py:294
  58.0 12.7 %collective-permute-start.17 = (bf16[128,1280]{1,0:T(8,128)(2,1)S(1)}, bf16[128,1280]{1,0:T(8,128)(2,1)S(1)}, u32[]{:S(2)}, u32[]{:S(2)}) collective-permute-start(bf16[128,1280]{1,0:T(8,128)(2,1)S(1)} %get-tuple-element.172), channel_id=1, source_target_pairs={{0,4},{8,12},{4,0},{12,8},{1,5},{9,13},{5,1},{13,9},{2,6},{10,14},... | collective-permute-start | bytes 983048 | tf_op jit(solution)/shard_map/ppermute | solution.py:294
  61.0 9.7 %collective-permute-start.18 = (bf16[128,1280]{1,0:T(8,128)(2,1)S(1)}, bf16[128,1280]{1,0:T(8,128)(2,1)S(1)}, u32[]{:S(2)}, u32[]{:S(2)}) collective-permute-start(bf16[128,1280]{1,0:T(8,128)(2,1)S(1)} %get-tuple-element.173), channel_id=1, source_target_pairs={{4,8},{8,4},{5,9},{9,5},{6,10},{10,6},{7,11},{11,7},{20,24},{24,20... | collective-permute-start | bytes 983048 | tf_op jit(solution)/shard_map/ppermute | solution.py:294
  64.0 13.7 %collective-permute-start.23 = (bf16[128,1280]{1,0:T(8,128)(2,1)S(1)}, bf16[128,1280]{1,0:T(8,128)(2,1)S(1)}, u32[]{:S(2)}, u32[]{:S(2)}) collective-permute-start(bf16[128,1280]{1,0:T(8,128)(2,1)S(1)} %get-tuple-element.181), channel_id=1, source_target_pairs={{0,4},{8,12},{4,0},{12,8},{1,5},{9,13},{5,1},{13,9},{2,6},{10,14},... | collective-permute-start | bytes 983048 | tf_op jit(solution)/shard_map/ppermute | solution.py:294
  68.0 9.7 %collective-permute-start.24 = (bf16[128,1280]{1,0:T(8,128)(2,1)S(1)}, bf16[128,1280]{1,0:T(8,128)(2,1)S(1)}, u32[]{:S(2)}, u32[]{:S(2)}) collective-permute-start(bf16[128,1280]{1,0:T(8,128)(2,1)S(1)} %get-tuple-element.182), channel_id=1, source_target_pairs={{4,8},{8,4},{5,9},{9,5},{6,10},{10,6},{7,11},{11,7},{20,24},{24,20... | collective-permute-start | bytes 983048 | tf_op jit(solution)/shard_map/ppermute | solution.py:294
  70.7 1.3 %collective-permute-start.19 = (f32[32,1024]{1,0:T(8,128)S(1)}, f32[32,1024]{1,0:T(8,128)S(1)}, u32[]{:S(2)}, u32[]{:S(2)}) collective-permute-start(f32[32,1024]{1,0:T(8,128)S(1)} %get-tuple-element.176), channel_id=1, source_target_pairs={{0,1},{1,0},{2,3},{3,2},{4,5},{5,4},{6,7},{7,6},{8,9},{9,8},{10,11... | collective-permute-start | bytes 393224 | tf_op jit(solution)/shard_map/ppermute | solution.py:299
  72.0 5.6 %collective-permute-start.22 = (f32[32,1024]{1,0:T(8,128)S(1)}, f32[32,1024]{1,0:T(8,128)S(1)}, u32[]{:S(2)}, u32[]{:S(2)}) collective-permute-start(f32[32,1024]{1,0:T(8,128)S(1)} %add.43), channel_id=1, source_target_pairs={{0,2},{1,3},{2,0},{3,1},{4,6},{5,7},{6,4},{7,5},{8,10},{9,11},{10,... | collective-permute-start | bytes 393224 | tf_op jit(solution)/shard_map/ppermute | solution.py:299
  77.8 16.8 %collective-permute-start.26 = (bf16[1024,256]{1,0:T(8,128)(2,1)S(1)}, bf16[1024,256]{1,0:T(8,128)(2,1)S(1)}, u32[]{:S(2)}, u32[]{:S(2)}) collective-permute-start(bf16[1024,256]{1,0:T(8,128)(2,1)S(1)} %slice.21), channel_id=1, source_target_pairs={{0,2},{1,3},{2,0},{3,1},{4,6},{5,7},{6,4},{7,5},{8,10},{9,11},{10,... | collective-permute-start | bytes 1572872 | tf_op jit(solution)/shard_map/ppermute | solution.py:299
  79.3 1.3 %collective-permute-start.25 = (bf16[32,1024]{1,0:T(8,128)(2,1)S(1)}, bf16[32,1024]{1,0:T(8,128)(2,1)S(1)}, u32[]{:S(2)}, u32[]{:S(2)}) collective-permute-start(bf16[32,1024]{1,0:T(8,128)(2,1)S(1)} %add.44.refs_1_.refs_6_), channel_id=1, source_target_pairs={{0,1},{1,0},{2,3},{3,2},{4,5},{5,4},{6,7},{7,6},{8,9},{9,8},{10,11... | collective-permute-start | bytes 196616 | tf_op jit(solution)/shard_map/ppermute | solution.py:299
  81.4 15.6 %collective-permute-start.27 = (bf16[256,256]{1,0:T(8,128)(2,1)S(1)}, bf16[256,256]{1,0:T(8,128)(2,1)S(1)}, u32[]{:S(2)}, u32[]{:S(2)}) collective-permute-start(bf16[256,256]{1,0:T(8,128)(2,1)S(1)} %get-tuple-element.200), channel_id=1, source_target_pairs={{0,4},{4,8},{8,12},{12,0},{1,5},{5,9},{9,13},{13,1},{2,6},{6,10},{... | collective-permute-start | bytes 393224 | tf_op jit(solution)/shard_map/ppermute | solution.py:294
  85.3 11.6 %collective-permute-start.28 = (bf16[256,256]{1,0:T(8,128)(2,1)S(1)}, bf16[256,256]{1,0:T(8,128)(2,1)S(1)}, u32[]{:S(2)}, u32[]{:S(2)}) collective-permute-start(bf16[256,256]{1,0:T(8,128)(2,1)S(1)} %get-tuple-element.201), channel_id=1, source_target_pairs={{0,8},{4,12},{8,0},{12,4},{1,9},{5,13},{9,1},{13,5},{2,10},{6,14},... | collective-permute-start | bytes 393224 | tf_op jit(solution)/shard_map/ppermute | solution.py:294
  86.5 10.5 %collective-permute-start.29 = (bf16[256,256]{1,0:T(8,128)(2,1)S(1)}, bf16[256,256]{1,0:T(8,128)(2,1)S(1)}, u32[]{:S(2)}, u32[]{:S(2)}) collective-permute-start(bf16[256,256]{1,0:T(8,128)(2,1)S(1)} %get-tuple-element.202), channel_id=1, source_target_pairs={{0,12},{4,0},{8,4},{12,8},{1,13},{5,1},{9,5},{13,9},{2,14},{6,2},{... | collective-permute-start | bytes 393224 | tf_op jit(solution)/shard_map/ppermute | solution.py:294
